TPU v7x, 512 devices: a whole 4x8x8 slice. The times are simulated.
512 devices in a mesh: seg: 64 (over y, z), kvh: 8 (over x, core).
Axes of the slice: x: 4, y: 8, z: 8, core: 2. Of those that a mesh axis runs over, the one named last changes fastest.
Arguments:
- queries: bfloat16 [16384, 5120], P('seg', 'kvh'), may hold values from -12 to 12
- key_rows: bfloat16 [16384, 1024], P('seg', 'kvh'), may hold values from -4 to 4
- value_rows: bfloat16 [16384, 1024], P('seg', 'kvh'), may hold values from -6 to 6
- grad_out: bfloat16 [16384, 5120], P('seg', 'kvh'), may hold values from -48 to 48
- w_key: bfloat16 [5120, 1024], P(None, 'kvh'), may hold values from -0.125 to 0.125
- w_value: bfloat16 [5120, 1024], P(None, 'kvh'), may hold values from -0.125 to 0.125
- trunk_len: int32 [64], replicated, may hold values from 64 to 128
- leaf_len: int32 [64, 64], replicated, may hold values from 1 to 2, as said below
- leaf_tree: int32 [64, 64], replicated, may hold values from 0 to 63, as said below
Outputs:
- grad_query: bfloat16 [16384, 5120], P('seg', 'kvh')
- grad_hidden: bfloat16 [16384, 5120], P('seg', 'kvh')
Inputs may be any that keep to these rules, and one draw needn't show every extreme that they name: `leaf_tree`: each row lists every device once. `leaf_len`: the leaves whose parent is one device, drawn anew, have 2 live positions.
All inputs are finite; a program needn't handle non-finite values.
Results may differ from a plain program's by a relative error of at most 0.018.
Values may be sent and summed in bfloat16 or wider, within the bound.
No kernel may reach another device: no remote copies, remote signals or barrier semaphores. Data moves between devices by JAX's collectives and lax.ppermute only.
A program may use at most 128 MiB of HBM per device.

v0:
```python
import math

import jax
import jax.numpy as jnp
from jax import lax
from jax.sharding import PartitionSpec as P

GROUP = 5
TRUNK = 128
LEAF = 2


very_negative = -1e30


def pair_products(query_rows, key_cols):
    batch_size, row_count, row_width = query_rows.shape
    head_rows = query_rows.reshape(batch_size, row_count, GROUP, row_width // GROUP)
    return jnp.einsum("brgd,bcd->bgrc", head_rows, key_cols, preferred_element_type=jnp.float32)


def partial_stats(scores, prob_grad, visible):
    masked = visible[:, None]
    row_max = jnp.max(jnp.where(masked, scores, very_negative), axis=-1)
    weights = jnp.where(masked, jnp.exp(scores - row_max[..., None]), 0.0)
    return (row_max, jnp.sum(weights, axis=-1), jnp.sum(weights * prob_grad, axis=-1))


def merge_stats(first_part, second_part):
    row_max = jnp.maximum(first_part[0], second_part[0])
    first_scale = jnp.exp(first_part[0] - row_max)
    second_scale = jnp.exp(second_part[0] - row_max)
    return (
        row_max,
        first_part[1] * first_scale + second_part[1] * second_scale,
        first_part[2] * first_scale + second_part[2] * second_scale,
    )


def finish_stats(stats):
    row_total = jnp.maximum(stats[1], 1.0)
    return (stats[0] + jnp.log(row_total), stats[2] / row_total)


def row_grads(query_rows, grad_rows, key_cols, visible, scores, prob_grad, log_total, row_delta):
    batch_size, row_count, row_width = query_rows.shape
    head_size = row_width // GROUP
    score_scale = 1.0 / math.sqrt(head_size)
    probability = jnp.where(visible[:, None], jnp.exp(scores - log_total[..., None]), 0.0)
    score_grad = (probability * (prob_grad - row_delta[..., None])).astype(jnp.bfloat16)
    probability_low = probability.astype(jnp.bfloat16)
    head_rows = query_rows.reshape(batch_size, row_count, GROUP, head_size)
    head_grads = grad_rows.reshape(batch_size, row_count, GROUP, head_size)
    query_grad = (
        jnp.einsum("bgrc,bcd->brgd", score_grad, key_cols, preferred_element_type=jnp.float32)
        * score_scale
    )
    key_grad = (
        jnp.einsum("bgrc,brgd->bcd", score_grad, head_rows, preferred_element_type=jnp.float32)
        * score_scale
    )
    value_grad = jnp.einsum(
        "bgrc,brgd->bcd", probability_low, head_grads, preferred_element_type=jnp.float32
    )
    return (query_grad.reshape(batch_size, row_count, row_width), key_grad, value_grad)


def shards(queries, key_rows, value_rows, grad_out, w_key, w_value, trunk_len, leaf_len, leaf_tree):
    seg_count = lax.axis_size("seg")
    device_index = lax.axis_index("seg")
    leaf_count = leaf_tree.shape[1]
    row_width = queries.shape[1]
    head_size = key_rows.shape[1]
    score_scale = 1.0 / math.sqrt(head_size)
    my_tree = lax.dynamic_index_in_dim(leaf_tree, device_index, 0, keepdims=False)
    my_lengths = lax.dynamic_index_in_dim(leaf_len, device_index, 0, keepdims=False)
    my_trunk = lax.dynamic_index_in_dim(trunk_len, device_index, 0, keepdims=False)
    positions = jnp.arange(TRUNK)
    leaf_pos = jnp.arange(LEAF)
    trunk_k = key_rows[:TRUNK][None]
    trunk_v = value_rows[:TRUNK][None]
    leaf_q = queries[TRUNK:].reshape(leaf_count, LEAF, row_width)
    leaf_g = grad_out[TRUNK:].reshape(leaf_count, LEAF, row_width)
    leaf_k = key_rows[TRUNK:].reshape(leaf_count, LEAF, head_size)
    leaf_v = value_rows[TRUNK:].reshape(leaf_count, LEAF, head_size)
    own_visible = (leaf_pos[None, :] <= leaf_pos[:, None])[None] & (
        leaf_pos[None, :, None] < my_lengths[:, None, None]
    )
    selector = my_tree[None, :] == jnp.arange(seg_count)[:, None]
    hot_float = selector.astype(jnp.float32)
    highest = lax.Precision.HIGHEST
    own_scores = pair_products(leaf_q, leaf_k) * score_scale
    own_prob_grad = pair_products(leaf_g, leaf_v)
    own_stats = partial_stats(own_scores, own_prob_grad, own_visible)
    one_hot = selector.astype(jnp.bfloat16)
    send_q = jnp.einsum("tj,jrc->trc", one_hot, leaf_q, preferred_element_type=jnp.float32).astype(
        jnp.bfloat16
    )
    send_g = jnp.einsum("tj,jrc->trc", one_hot, leaf_g, preferred_element_type=jnp.float32).astype(
        jnp.bfloat16
    )
    in_q, in_g = (
        lax.all_to_all(send_q, "seg", split_axis=0, concat_axis=0, tiled=True),
        lax.all_to_all(send_g, "seg", split_axis=0, concat_axis=0, tiled=True),
    )
    in_len = jnp.sum(jnp.where(leaf_tree == device_index, leaf_len, 0), axis=1)
    all_q = jnp.concatenate([queries[:TRUNK], in_q.reshape(seg_count * LEAF, row_width)], axis=0)[
        None
    ]
    all_g = jnp.concatenate([grad_out[:TRUNK], in_g.reshape(seg_count * LEAF, row_width)], axis=0)[
        None
    ]
    row_limit = jnp.concatenate([positions, jnp.full((seg_count * LEAF,), TRUNK)])
    row_pos = jnp.concatenate([positions, jnp.tile(leaf_pos, seg_count)])
    row_len = jnp.concatenate([jnp.full((TRUNK,), my_trunk), jnp.repeat(in_len, LEAF)])
    all_visible = (
        (positions[None, :] <= row_limit[:, None])
        & (positions[None, :] < my_trunk)
        & (row_pos < row_len)[:, None]
    )[None]
    all_scores = pair_products(all_q, trunk_k) * score_scale
    all_prob_grad = pair_products(all_g, trunk_v)
    all_max, all_total, all_weighted = partial_stats(all_scores, all_prob_grad, all_visible)
    out_max = all_max[0, :, TRUNK:].reshape(GROUP, seg_count, LEAF)
    out_total = all_total[0, :, TRUNK:].reshape(GROUP, seg_count, LEAF)
    out_weighted = all_weighted[0, :, TRUNK:].reshape(GROUP, seg_count, LEAF)
    back_max, back_total, back_weighted = (
        lax.all_to_all(out_max, "seg", split_axis=1, concat_axis=1, tiled=True),
        lax.all_to_all(out_total, "seg", split_axis=1, concat_axis=1, tiled=True),
        lax.all_to_all(out_weighted, "seg", split_axis=1, concat_axis=1, tiled=True),
    )
    remote = tuple(
        (
            jnp.swapaxes(jnp.take(member, my_tree, axis=1), 0, 1)
            for member in (back_max, back_total, back_weighted)
        )
    )
    leaf_log, leaf_delta = finish_stats(merge_stats(own_stats, remote))
    send_log = jnp.einsum("tj,jgr->gtr", hot_float, leaf_log, precision=highest)
    send_delta = jnp.einsum("tj,jgr->gtr", hot_float, leaf_delta, precision=highest)
    in_log, in_delta = (
        lax.all_to_all(send_log, "seg", split_axis=1, concat_axis=1, tiled=True),
        lax.all_to_all(send_delta, "seg", split_axis=1, concat_axis=1, tiled=True),
    )
    trunk_log, trunk_delta = finish_stats(
        (all_max[:, :, :TRUNK], all_total[:, :, :TRUNK], all_weighted[:, :, :TRUNK])
    )
    all_log = jnp.concatenate([trunk_log, in_log.reshape(1, GROUP, seg_count * LEAF)], axis=2)
    all_delta = jnp.concatenate([trunk_delta, in_delta.reshape(1, GROUP, seg_count * LEAF)], axis=2)
    all_dq, owner_dk, owner_dv = row_grads(
        all_q, all_g, trunk_k, all_visible, all_scores, all_prob_grad, all_log, all_delta
    )
    back_dq = lax.all_to_all(
        all_dq[0, TRUNK:].reshape(seg_count, LEAF, row_width).astype(jnp.bfloat16),
        "seg",
        split_axis=0,
        concat_axis=0,
        tiled=True,
    ).astype(jnp.float32)
    leaf_dq, leaf_dk, leaf_dv = row_grads(
        leaf_q, leaf_g, leaf_k, own_visible, own_scores, own_prob_grad, leaf_log, leaf_delta
    )
    leaf_dq = leaf_dq + jnp.take(back_dq, my_tree, axis=0)
    trunk_dq = all_dq[0, :TRUNK]
    trunk_dk = owner_dk[0]
    trunk_dv = owner_dv[0]
    grad_query = jnp.concatenate(
        [trunk_dq, leaf_dq.reshape(leaf_count * LEAF, row_width)], axis=0
    ).astype(jnp.bfloat16)
    key_grad = jnp.concatenate(
        [trunk_dk, leaf_dk.reshape(leaf_count * LEAF, head_size)], axis=0
    ).astype(jnp.bfloat16)
    value_grad = jnp.concatenate(
        [trunk_dv, leaf_dv.reshape(leaf_count * LEAF, head_size)], axis=0
    ).astype(jnp.bfloat16)
    head_part = jnp.einsum("rd,cd->rc", key_grad, w_key, preferred_element_type=jnp.float32)
    head_part = head_part + jnp.einsum(
        "rd,cd->rc", value_grad, w_value, preferred_element_type=jnp.float32
    )
    grad_hidden = lax.psum_scatter(
        head_part.astype(jnp.bfloat16), "kvh", scatter_dimension=1, tiled=True
    )
    return (grad_query, grad_hidden)


def solution(mesh):
    in_specs = (
        P("seg", "kvh"),
        P("seg", "kvh"),
        P("seg", "kvh"),
        P("seg", "kvh"),
        P(None, "kvh"),
        P(None, "kvh"),
        P(),
        P(),
        P(),
    )
    out_specs = (P("seg", "kvh"), P("seg", "kvh"))
    return jax.shard_map(shards, mesh=mesh, in_specs=in_specs, out_specs=out_specs, check_vma=False)
```

profile of v0, /device:TPU:1, one launch (start us, length us, event | category | flops | bytes accessed | tf_op | source)
XLA Modules:
  0.0 202.9 jit_solution(721649958143276263)
XLA Ops:
  7.2 1.1 fusion.66
  8.4 1.3 compare_and_fusion
  9.9 0.8 copy.96
  10.7 17.1 %all-to-all-start = ((bf16[64,2,640]{2,1,0:T(2,128)(2,1)}), bf16[64,2,640]{2,1,0:T(2,128)(2,1)S(1)}, u32[]{:S(2)}, u32[]{:S(2)}) async-start(bf16[64,2,640]{2,1,0:T(2,128)(2,1)} %copy.96), calls=%async_computation | async-start | bytes 327680 | tf_op jit(solution)/shard_map/all_to_all | solution.py:103
  27.9 0.9 select_reduce_fusion.2
  29.5 1.3 dynamic_slice.11
  31.9 1.0 fusion.65
  33.2 0.8 copy.112
  34.9 4.7 %all-to-all-done = bf16[64,2,640]{2,1,0:T(2,128)(2,1)S(1)} async-done(((bf16[64,2,640]{2,1,0:T(2,128)(2,1)}), bf16[64,2,640]{2,1,0:T(2,128)(2,1)S(1)}, u32[]{:S(2)}, u32[]{:S(2)}) %all-to-all-start) | async-done | bytes 163872 | tf_op jit(solution)/shard_map/all_to_all | solution.py:103
  39.6 7.5 %all-to-all-start.4 = ((bf16[64,2,640]{2,1,0:T(2,128)(2,1)}), bf16[64,2,640]{2,1,0:T(2,128)(2,1)S(1)}, u32[]{:S(2)}, u32[]{:S(2)}) async-start(bf16[64,2,640]{2,1,0:T(2,128)(2,1)} %copy.112), calls=%async_computation.4 | async-start | bytes 327680 | tf_op jit(solution)/shard_map/all_to_all | solution.py:104
  47.4 0.9 reshape_reshape.9
  49.0 1.9 select_reduce_fusion.1
  51.1 7.7 %all-to-all-done.4 = bf16[64,2,640]{2,1,0:T(2,128)(2,1)S(1)} async-done(((bf16[64,2,640]{2,1,0:T(2,128)(2,1)}), bf16[64,2,640]{2,1,0:T(2,128)(2,1)S(1)}, u32[]{:S(2)}, u32[]{:S(2)}) %all-to-all-start.4) | async-done | bytes 163872 | tf_op jit(solution)/shard_map/all_to_all | solution.py:104
  60.1 0.7 copy.116
  60.9 4.6 %all-to-all-start.5 = ((f32[5,64,2]{0,2,1:T(2,128)}), f32[5,64,2]{0,2,1:T(2,128)S(1)}, u32[]{:S(2)}, u32[]{:S(2)}) async-start(f32[5,64,2]{0,2,1:T(2,128)} %bitcast.40), calls=%async_computation.5 | async-start | bytes 131072 | tf_op jit(solution)/shard_map/all_to_all | solution.py:130
  65.6 3.6 %fusion.62 = (f32[64,5,2]{1,2,0:T(2,128)}, f32[64,5,2]{1,2,0:T(2,128)}, f32[64,5,2,2]{1,3,2,0:T(2,128)}) fusion(f32[64,5,2,2]{1,3,2,0:T(2,128)S(1)} %get-tuple-element.23, f32[64,5,2]{1,2,0:T(2,128)} %get-tuple-element.22, pred[64,2,2]{2,1,0:T(4,128)(4,1)S(1)} %broadcast_and_fusion, bf16[64,2,128,1]{2,1,3,0:T(2,128)(2,1)S(1)} %bitcast.164, ...), kind=kOutput, calls=%fused_computation.118 | convolution fusion | flops 332800 | bytes 214784 | tf_op jit(solution)/shard_map/brgd,bcd->bgrc/dot_general | solution.py:19
  69.1 0.7 copy.104
  69.9 6.7 %all-to-all-done.5 = f32[5,64,2]{0,2,1:T(2,128)S(1)} async-done(((f32[5,64,2]{0,2,1:T(2,128)}), f32[5,64,2]{0,2,1:T(2,128)S(1)}, u32[]{:S(2)}, u32[]{:S(2)}) %all-to-all-start.5) | async-done | bytes 2592 | tf_op jit(solution)/shard_map/all_to_all | solution.py:130
  76.6 5.5 %all-to-all-start.2 = ((f32[5,64,2]{0,2,1:T(2,128)}), f32[5,64,2]{0,2,1:T(2,128)S(1)}, u32[]{:S(2)}, u32[]{:S(2)}) async-start(f32[5,64,2]{0,2,1:T(2,128)} %bitcast.21), calls=%async_computation.2 | async-start | bytes 131072 | tf_op jit(solution)/shard_map/all_to_all | solution.py:129
  82.1 0.7 copy.99
  82.8 10.4 %all-to-all-done.2 = f32[5,64,2]{0,2,1:T(2,128)S(1)} async-done(((f32[5,64,2]{0,2,1:T(2,128)}), f32[5,64,2]{0,2,1:T(2,128)S(1)}, u32[]{:S(2)}, u32[]{:S(2)}) %all-to-all-start.2) | async-done | bytes 2592 | tf_op jit(solution)/shard_map/all_to_all | solution.py:129
  93.2 4.6 %all-to-all-start.1 = ((f32[5,64,2]{0,2,1:T(2,128)}), f32[5,64,2]{0,2,1:T(2,128)S(1)}, u32[]{:S(2)}, u32[]{:S(2)}) async-start(f32[5,64,2]{0,2,1:T(2,128)} %bitcast.18), calls=%async_computation.1 | async-start | bytes 131072 | tf_op jit(solution)/shard_map/all_to_all | solution.py:128
  97.8 0.9 copy.101
  98.7 1.5 copy.103
  100.2 1.5 copy.115
  101.7 1.3 copy.108
  103.0 1.3 copy.120
  106.3 2.5 %all-to-all-done.1 = f32[5,64,2]{0,2,1:T(2,128)S(1)} async-done(((f32[5,64,2]{0,2,1:T(2,128)}), f32[5,64,2]{0,2,1:T(2,128)S(1)}, u32[]{:S(2)}, u32[]{:S(2)}) %all-to-all-start.1) | async-done | bytes 2592 | tf_op jit(solution)/shard_map/all_to_all | solution.py:128
  109.6 0.8 log_add_fusion
  110.4 0.8 convolution_bitcast_fusion.6
  111.2 0.7 copy.119
  112.0 9.8 %all-to-all-start.6 = ((f32[5,64,2]{0,2,1:T(2,128)}), f32[5,64,2]{0,2,1:T(2,128)S(1)}, u32[]{:S(2)}, u32[]{:S(2)}) async-start(f32[5,64,2]{0,2,1:T(2,128)} %copy.119), calls=%async_computation.6 | async-start | bytes 131072 | tf_op jit(solution)/shard_map/all_to_all | solution.py:143
  122.0 2.2 %fusion.7 = bf16[64,2,128]{2,1,0:T(2,128)(2,1)} fusion(bf16[64,2,5,128]{3,2,1,0:T(8,128)(2,1)} %reshape_reshape.9, f32[64,5,2,2]{1,3,2,0:T(2,128)} %copy-done.6, pred[64,2,2]{2,1,0:T(4,128)(4,1)} %copy-done.9, f32[64,5,2]{1,2,0:T(2,128)S(1)} %copy.125), kind=kOutput, calls=%fused_computation.24 | convolution fusion | flops 347904 | bytes 204544 | tf_op jit(solution)/shard_map/bgrc,brgd->bcd/dot_general | solution.py:62
  124.5 0.8 convolution_bitcast_fusion.7
  125.2 0.8 copy.107
  126.0 6.8 %all-to-all-done.6 = f32[5,64,2]{0,2,1:T(2,128)S(1)} async-done(((f32[5,64,2]{0,2,1:T(2,128)}), f32[5,64,2]{0,2,1:T(2,128)S(1)}, u32[]{:S(2)}, u32[]{:S(2)}) %all-to-all-start.6) | async-done | bytes 2592 | tf_op jit(solution)/shard_map/all_to_all | solution.py:143
  132.7 5.2 %all-to-all-start.3 = ((f32[5,64,2]{0,2,1:T(2,128)}), f32[5,64,2]{0,2,1:T(2,128)S(1)}, u32[]{:S(2)}, u32[]{:S(2)}) async-start(f32[5,64,2]{0,2,1:T(2,128)} %copy.107), calls=%async_computation.3 | async-start | bytes 131072 | tf_op jit(solution)/shard_map/all_to_all | solution.py:142
  138.4 10.7 %all-to-all-done.3 = f32[5,64,2]{0,2,1:T(2,128)S(1)} async-done(((f32[5,64,2]{0,2,1:T(2,128)}), f32[5,64,2]{0,2,1:T(2,128)S(1)}, u32[]{:S(2)}, u32[]{:S(2)}) %all-to-all-start.3) | async-done | bytes 2592 | tf_op jit(solution)/shard_map/all_to_all | solution.py:142
  150.4 0.8 fusion.23
  151.7 2.4 %fusion = bf16[256,5120]{1,0:T(8,128)(2,1)} fusion(f32[256,5120]{1,0:T(8,128)S(1)} %fusion.23, bf16[5120,128]{1,0:T(8,128)(2,1)S(1)} %copy-done.1, bf16[128,128]{1,0:T(8,128)(2,1)S(1)} %bitcast.165, bf16[128,128]{1,0:T(8,128)(2,1)S(1)} %fusion.6), kind=kOutput, calls=%fused_computation.5 | convolution fusion | flops 338296832 | bytes 9240576 | tf_op jit(solution)/shard_map/rd,cd->rc/dot_general | solution.py:177
  154.1 4.4 %copy.135 = bf16[256,5120]{0,1:T(8,128)(2,1)} copy(bf16[256,5120]{1,0:T(8,128)(2,1)} %fusion) | data formatting | bytes 5242880
  160.6 0.7 convert_element_type.37
  161.4 4.6 %all-to-all-start.7 = ((bf16[64,2,640]{2,1,0:T(2,128)(2,1)}), bf16[64,2,640]{2,1,0:T(2,128)(2,1)S(1)}, u32[]{:S(2)}, u32[]{:S(2)}) async-start(bf16[64,2,640]{2,1,0:T(2,128)(2,1)} %convert_element_type.37), calls=%async_computation.7 | async-start | bytes 327680 | tf_op jit(solution)/shard_map/all_to_all | solution.py:153
  166.4 11.3 %all-to-all-done.7 = bf16[64,2,640]{2,1,0:T(2,128)(2,1)S(1)} async-done(((bf16[64,2,640]{2,1,0:T(2,128)(2,1)}), bf16[64,2,640]{2,1,0:T(2,128)(2,1)S(1)}, u32[]{:S(2)}, u32[]{:S(2)}) %all-to-all-start.7) | async-done | bytes 163872 | tf_op jit(solution)/shard_map/all_to_all | solution.py:153
  177.9 0.9 gather_fusion
  179.2 0.8 pad_maximum_fusion
  179.9 14.2 %reduce-scatter.4.cloned.1.call-done = bf16[640,256]{1,0:T(8,128)(2,1)} async-done(((bf16[5120,256]{1,0:T(8,128)(2,1)}), bf16[640,256]{1,0:T(8,128)(2,1)}) %reduce-scatter.4.cloned.1.call-update) | async-done | bytes 327696
  194.2 1.9 copy.136
  (105 shorter events, 14.1 us)
Async XLA Ops:
  7.2 143.2 %copy-start = (bf16[5120,128]{1,0:T(8,128)(2,1)S(1)}, bf16[5120,128]{1,0:T(8,128)(2,1)}, u32[]{:S(2)}) copy-start(bf16[5120,128]{1,0:T(8,128)(2,1)} %param.15) | copy-start | bytes 3932164
  7.2 39.9 %copy-start.19 = (s32[256]{0:T(256)S(1)}, s32[256]{0:T(256)}, u32[]{:S(2)}) copy-start(s32[256]{0:T(256)} %constant.23.clone.1) | copy-start | bytes 3076
  7.2 41.1 %copy-start.11 = (bf16[256,128]{1,0:T(8,128)(2,1)S(1)}, bf16[256,128]{1,0:T(8,128)(2,1)}, u32[]{:S(2)}) copy-start(bf16[256,128]{1,0:T(8,128)(2,1)} %param.12) | copy-start | bytes 196612
  9.7 72.3 %copy-start.15 = (s32[64]{0:T(128)}, s32[64]{0:T(128)S(1)}, u32[]{:S(2)}) copy-start(s32[64]{0:T(128)S(1)} %get-tuple-element.8) | copy-start | bytes 772
  10.7 28.8 %all-to-all-start = ((bf16[64,2,640]{2,1,0:T(2,128)(2,1)}), bf16[64,2,640]{2,1,0:T(2,128)(2,1)S(1)}, u32[]{:S(2)}, u32[]{:S(2)}) async-start(bf16[64,2,640]{2,1,0:T(2,128)(2,1)} %copy.96), calls=%async_computation | async-start | bytes 327680 | tf_op jit(solution)/shard_map/all_to_all | solution.py:103
  34.9 30.7 %copy-start.9 = (pred[64,2,2]{2,1,0:T(4,128)(4,1)}, pred[64,2,2]{2,1,0:T(4,128)(4,1)S(1)}, u32[]{:S(2)}) copy-start(pred[64,2,2]{2,1,0:T(4,128)(4,1)S(1)} %broadcast_and_fusion) | copy-start | bytes 772
  39.6 19.2 %all-to-all-start.4 = ((bf16[64,2,640]{2,1,0:T(2,128)(2,1)}), bf16[64,2,640]{2,1,0:T(2,128)(2,1)S(1)}, u32[]{:S(2)}, u32[]{:S(2)}) async-start(bf16[64,2,640]{2,1,0:T(2,128)(2,1)} %copy.112), calls=%async_computation.4 | async-start | bytes 327680 | tf_op jit(solution)/shard_map/all_to_all | solution.py:104
  48.6 10.3 %copy-start.2 = (bf16[1,128,5,128]{3,1,2,0:T(8,128)(2,1)}, bf16[1,128,5,128]{3,1,2,0:T(8,128)(2,1)S(1)}, u32[]{:S(2)}) copy-start(bf16[1,128,5,128]{3,1,2,0:T(8,128)(2,1)S(1)} %copy.97) | copy-start | bytes 491524
  49.0 10.2 %copy-start.13 = (bf16[256,128]{1,0:T(8,128)(2,1)S(1)}, bf16[256,128]{1,0:T(8,128)(2,1)}, u32[]{:S(2)}) copy-start(bf16[256,128]{1,0:T(8,128)(2,1)} %param.13) | copy-start | bytes 196612
  50.9 18.2 %copy-start.6 = (f32[64,5,2,2]{1,3,2,0:T(2,128)}, f32[64,5,2,2]{1,3,2,0:T(2,128)S(1)}, u32[]{:S(2)}) copy-start(f32[64,5,2,2]{1,3,2,0:T(2,128)S(1)} %get-tuple-element.23) | copy-start | bytes 15364
  50.9 14.6 %slice-start = ((bf16[256,128]{1,0:T(8,128)(2,1)}), bf16[128,128]{1,0:T(8,128)(2,1)S(1)}, s32[]{:S(2)}) async-start(bf16[256,128]{1,0:T(8,128)(2,1)} %param.13), calls=%async_computation.10 | async-start | bytes 65536 | tf_op jit(solution)/shard_map/slice | solution.py:85
  51.1 8.1 %copy-start.4 = (bf16[1,128,5,128]{3,1,2,0:T(8,128)(2,1)}, bf16[1,128,5,128]{3,1,2,0:T(8,128)(2,1)S(1)}, u32[]{:S(2)}) copy-start(bf16[1,128,5,128]{3,1,2,0:T(8,128)(2,1)S(1)} %copy.98) | copy-start | bytes 491524
  60.9 15.7 %all-to-all-start.5 = ((f32[5,64,2]{0,2,1:T(2,128)}), f32[5,64,2]{0,2,1:T(2,128)S(1)}, u32[]{:S(2)}, u32[]{:S(2)}) async-start(f32[5,64,2]{0,2,1:T(2,128)} %bitcast.40), calls=%async_computation.5 | async-start | bytes 131072 | tf_op jit(solution)/shard_map/all_to_all | solution.py:130
  76.6 16.6 %all-to-all-start.2 = ((f32[5,64,2]{0,2,1:T(2,128)}), f32[5,64,2]{0,2,1:T(2,128)S(1)}, u32[]{:S(2)}, u32[]{:S(2)}) async-start(f32[5,64,2]{0,2,1:T(2,128)} %bitcast.21), calls=%async_computation.2 | async-start | bytes 131072 | tf_op jit(solution)/shard_map/all_to_all | solution.py:129
  93.2 15.7 %all-to-all-start.1 = ((f32[5,64,2]{0,2,1:T(2,128)}), f32[5,64,2]{0,2,1:T(2,128)S(1)}, u32[]{:S(2)}, u32[]{:S(2)}) async-start(f32[5,64,2]{0,2,1:T(2,128)} %bitcast.18), calls=%async_computation.1 | async-start | bytes 131072 | tf_op jit(solution)/shard_map/all_to_all | solution.py:128
  112.0 20.7 %all-to-all-start.6 = ((f32[5,64,2]{0,2,1:T(2,128)}), f32[5,64,2]{0,2,1:T(2,128)S(1)}, u32[]{:S(2)}, u32[]{:S(2)}) async-start(f32[5,64,2]{0,2,1:T(2,128)} %copy.119), calls=%async_computation.6 | async-start | bytes 131072 | tf_op jit(solution)/shard_map/all_to_all | solution.py:143
  121.9 2.2 %copy-start.7 = (f32[64,5,2,2]{1,3,2,0:T(2,128)S(1)}, f32[64,5,2,2]{1,3,2,0:T(2,128)}, u32[]{:S(2)}) copy-start(f32[64,5,2,2]{1,3,2,0:T(2,128)} %copy-done.6) | copy-start | bytes 15364
  121.9 2.2 %copy-start.8 = (f32[64,5,2,2]{1,3,2,0:T(2,128)S(1)}, f32[64,5,2,2]{1,3,2,0:T(2,128)}, u32[]{:S(2)}) copy-start(f32[64,5,2,2]{1,3,2,0:T(2,128)} %get-tuple-element.27) | copy-start | bytes 15364
  121.9 2.2 %copy-start.10 = (pred[64,2,2]{2,1,0:T(4,128)(4,1)S(1)}, pred[64,2,2]{2,1,0:T(4,128)(4,1)}, u32[]{:S(2)}) copy-start(pred[64,2,2]{2,1,0:T(4,128)(4,1)} %copy-done.9) | copy-start | bytes 772
  122.0 27.2 %copy-start.17 = (f32[1,5,128]{2,0,1:T(1,128)S(1)}, f32[1,5,128]{2,0,1:T(1,128)}, u32[]{:S(2)}) copy-start(f32[1,5,128]{2,0,1:T(1,128)} %copy.120) | copy-start | bytes 7684
  122.0 27.2 %copy-start.16 = (f32[1,5,128]{2,0,1:T(1,128)S(1)}, f32[1,5,128]{2,0,1:T(1,128)}, u32[]{:S(2)}) copy-start(f32[1,5,128]{2,0,1:T(1,128)} %copy.108) | copy-start | bytes 7684
  132.7 16.3 %all-to-all-start.3 = ((f32[5,64,2]{0,2,1:T(2,128)}), f32[5,64,2]{0,2,1:T(2,128)S(1)}, u32[]{:S(2)}, u32[]{:S(2)}) async-start(f32[5,64,2]{0,2,1:T(2,128)} %copy.107), calls=%async_computation.3 | async-start | bytes 131072 | tf_op jit(solution)/shard_map/all_to_all | solution.py:142
  137.9 56.2 %reduce-scatter.4.cloned.1.call-start = ((), (), s32[]{:S(2)}) async-start(), calls=%async_computation.9 | async-start | bytes 2949120
  149.1 0.9 copy-start.3
  149.1 1.0 copy-start.5
  150.4 1.3 copy-start.1
  150.4 1.3 copy-start.14
  158.5 0.7 copy-start.18
  158.5 1.6 copy-start.12
  161.4 16.4 %all-to-all-start.7 = ((bf16[64,2,640]{2,1,0:T(2,128)(2,1)}), bf16[64,2,640]{2,1,0:T(2,128)(2,1)S(1)}, u32[]{:S(2)}, u32[]{:S(2)}) async-start(bf16[64,2,640]{2,1,0:T(2,128)(2,1)} %convert_element_type.37), calls=%async_computation.7 | async-start | bytes 327680 | tf_op jit(solution)/shard_map/all_to_all | solution.py:153
Sparse Core Ops, SparseCore 0:
  158.7 35.4 reduce-scatter.3
where the time goes:
time: 205 us; the launch traced here: 203 us
  waiting for transfers between devices  75 us (37%)
  starting transfers between devices  59 us (29%)
  local copies, waits for them, and re-layouts  32.2 us (16%)
  matrix products  14.7 us (7%)
  between operations  14.6 us (7%)
  other arithmetic  7.41 us (4%)
    all_to_all x1, starting transfers between devices, shards(): lax.all_to_all(send_q, 'seg', split_axis=0, concat_axis=0, tiled=True)  17.1 us
    unnamed x2, waiting for transfers between devices  14.3 us
    all_to_all x1, waiting for transfers between devices, shards(): lax.all_to_all(all_dq[0, TRUNK:].reshape(seg_count, LEAF, row_width).asty...  11.3 us
    all_to_all x1, waiting for transfers between devices, shards(): lax.all_to_all(send_log, 'seg', split_axis=1, concat_axis=1, tiled=True)  10.7 us
    all_to_all x1, waiting for transfers between devices, shards(): lax.all_to_all(out_total, 'seg', split_axis=1, concat_axis=1, tiled=True)  10.4 us
    all_to_all x1, starting transfers between devices, shards(): lax.all_to_all(send_delta, 'seg', split_axis=1, concat_axis=1, tiled=True)  9.8 us
    unnamed x47, local copies, waits for them, and re-layouts  8.64 us
    all_to_all x1, waiting for transfers between devices, shards(): lax.all_to_all(send_g, 'seg', split_axis=0, concat_axis=0, tiled=True)  7.68 us
  transfers between devices with their start and end apart: 9, of which 9 were waited for; matrix products, arithmetic and copies ran while one was open for 17% of the time, Pallas kernels for 0%

commit v1 on v0

v1 whole, which is shorter than its diff:
```python
import functools
import math

import jax
import jax.numpy as jnp
from jax import lax
from jax.experimental import pallas as pl
from jax.experimental.pallas import tpu as pltpu
from jax.sharding import PartitionSpec as P

GROUP = 5
TRUNK = 128
LEAF = 2
HEAD = 128
OUT_TILES = 2 * GROUP + 2
OUT_ROWS = OUT_TILES * LEAF
BACK_TILES = GROUP + 2
BACK_ROWS = 16
VERY_NEGATIVE = -1e30
SCALE = 1.0 / math.sqrt(HEAD)

f32 = jnp.float32
bf16 = jnp.bfloat16
vmem = pl.BlockSpec(memory_space=pltpu.VMEM)
smem = pl.BlockSpec(memory_space=pltpu.SMEM)


def dot(a, b, contract):
    return lax.dot_general(a, b, ((contract[0:1], contract[1:2]), ((), ())), preferred_element_type=f32)


def leaf_selector(leaf_tree_ref, seg):
    count = leaf_tree_ref.shape[0]
    tree_row = leaf_tree_ref[pl.ds(seg, 1), :].astype(f32).astype(bf16)
    tree_rows = jnp.broadcast_to(tree_row, (16, count))
    leaf = lax.broadcasted_iota(jnp.int32, (count, LEAF * count), 0)
    col = lax.broadcasted_iota(jnp.int32, (count, LEAF * count), 1)
    repeat = (leaf == (col >> 1)).astype(f32).astype(bf16)
    tree_of_col = dot(tree_rows, repeat, (1, 0))[0:1, :].astype(jnp.int32)
    row = lax.broadcasted_iota(jnp.int32, (LEAF * count, LEAF * count), 0)
    col = lax.broadcasted_iota(jnp.int32, (LEAF * count, LEAF * count), 1)
    row_pos = (row >= count).astype(jnp.int32)
    hit = (tree_of_col == row - row_pos * count) & (row_pos == (col & 1))
    return hit.astype(f32).astype(bf16)


def send_kernel(q_ref, g_ref, k_ref, v_ref, leaf_tree_ref, out_ref, rows_ref):
    count = leaf_tree_ref.shape[0]
    seg = lax.axis_index("seg")
    selector = leaf_selector(leaf_tree_ref, seg)
    leaf_rows = LEAF * count
    tile = 0
    for ref in (q_ref, g_ref, k_ref, v_ref):
        moved = dot(selector, ref[TRUNK : TRUNK + leaf_rows, :], (1, 0))
        for part in range(ref.shape[1] // HEAD):
            for a in range(LEAF):
                rows_ref[pl.ds(tile * LEAF + a, count, OUT_ROWS), :] = moved[
                    a * count : (a + 1) * count, part * HEAD : (part + 1) * HEAD
                ]
            tile += 1
    out_ref[...] = rows_ref[...].astype(bf16)


def softmax_grads(scores, prob_grad, visible):
    masked = jnp.where(visible, scores, VERY_NEGATIVE)
    row_max = jnp.max(masked, axis=-1, keepdims=True)
    weights = jnp.where(visible, jnp.exp(masked - row_max), 0.0)
    row_total = jnp.maximum(jnp.sum(weights, axis=-1, keepdims=True), 1.0)
    probability = weights * (1.0 / row_total)
    row_delta = jnp.sum(probability * prob_grad, axis=-1, keepdims=True)
    score_grad = (probability * (prob_grad - row_delta)).astype(bf16)
    return probability.astype(bf16), score_grad


def trunk_kernel(q_ref, g_ref, k_ref, v_ref, trunk_len_ref, dq_ref, dk_ref, dv_ref):
    seg = lax.axis_index("seg")
    trunk_len = trunk_len_ref[seg]
    keys = k_ref[0:TRUNK, :]
    values = v_ref[0:TRUNK, :]
    row = lax.broadcasted_iota(jnp.int32, (TRUNK, TRUNK), 0)
    col = lax.broadcasted_iota(jnp.int32, (TRUNK, TRUNK), 1)
    visible = (col <= row) & (row < trunk_len)
    for g in range(GROUP):
        head_q = q_ref[0:TRUNK, g * HEAD : (g + 1) * HEAD]
        head_g = g_ref[0:TRUNK, g * HEAD : (g + 1) * HEAD]
        scores = dot(head_q, keys, (1, 1)) * SCALE
        prob_grad = dot(head_g, values, (1, 1))
        probability, score_grad = softmax_grads(scores, prob_grad, visible)
        dq_ref[:, g * HEAD : (g + 1) * HEAD] = (dot(score_grad, keys, (1, 0)) * SCALE).astype(bf16)
        head_dk = dot(score_grad, head_q, (0, 0))
        head_dv = dot(probability, head_g, (0, 0))
        if g == 0:
            dk_ref[...] = head_dk
            dv_ref[...] = head_dv
        else:
            dk_ref[...] += head_dk
            dv_ref[...] += head_dv


def leaf_kernel(
    in_ref, k_ref, v_ref, trunk_dk_ref, trunk_dv_ref, leaf_tree_ref, leaf_len_ref, trunk_len_ref,
    out_ref, trunk_kv_ref, rows_ref, back_ref, dk_ref, dv_ref,
):
    count = leaf_tree_ref.shape[0]
    seg = lax.axis_index("seg")
    trunk_len = trunk_len_ref[seg]
    rows_ref[...] = in_ref[...].astype(f32)

    def gather(tile):
        parts = [rows_ref[pl.ds(tile * LEAF + a, count, OUT_ROWS), :] for a in range(LEAF)]
        return jnp.concatenate(parts, axis=0).astype(bf16)

    keys = jnp.concatenate([k_ref[0:TRUNK, :], gather(2 * GROUP)], axis=0)
    values = jnp.concatenate([v_ref[0:TRUNK, :], gather(2 * GROUP + 1)], axis=0)
    in_len = jnp.sum(jnp.where(leaf_tree_ref[...] == seg, leaf_len_ref[...], 0), axis=1, keepdims=True)
    row_len = jnp.concatenate([in_len] * LEAF, axis=0)
    leaf_rows = LEAF * count
    shape = (leaf_rows, TRUNK + leaf_rows)
    row = lax.broadcasted_iota(jnp.int32, shape, 0)
    col = lax.broadcasted_iota(jnp.int32, shape, 1)
    row_pos = (row >= count).astype(jnp.int32)
    leaf_col = col - TRUNK
    col_pos = (leaf_col >= count).astype(jnp.int32)
    own = (row - row_pos * count == leaf_col - col_pos * count) & (col_pos <= row_pos)
    visible = ((col < trunk_len) & (col < TRUNK)) | ((col >= TRUNK) & own)
    visible = visible & (row_pos < row_len)
    for g in range(GROUP):
        head_q = gather(g)
        head_g = gather(GROUP + g)
        scores = dot(head_q, keys, (1, 1)) * SCALE
        prob_grad = dot(head_g, values, (1, 1))
        probability, score_grad = softmax_grads(scores, prob_grad, visible)
        head_dq = dot(score_grad, keys, (1, 0)) * SCALE
        for a in range(LEAF):
            back_ref[pl.ds(g * LEAF + a, count, BACK_ROWS), :] = head_dq[a * count : (a + 1) * count, :]
        head_dk = dot(score_grad, head_q, (0, 0))
        head_dv = dot(probability, head_g, (0, 0))
        if g == 0:
            dk_ref[...] = head_dk
            dv_ref[...] = head_dv
        else:
            dk_ref[...] += head_dk
            dv_ref[...] += head_dv
    for a in range(LEAF):
        at = TRUNK + a * count
        back_ref[pl.ds(GROUP * LEAF + a, count, BACK_ROWS), :] = dk_ref[at : at + count, :] * SCALE
        back_ref[pl.ds((GROUP + 1) * LEAF + a, count, BACK_ROWS), :] = dv_ref[at : at + count, :]
    for spare in range(BACK_TILES * LEAF, BACK_ROWS):
        back_ref[pl.ds(spare, count, BACK_ROWS), :] = jnp.zeros((count, HEAD), f32)
    out_ref[...] = back_ref[...].astype(bf16)
    trunk_kv_ref[:, 0:HEAD] = (trunk_dk_ref[...] + dk_ref[0:TRUNK, :]) * SCALE
    trunk_kv_ref[:, HEAD : 2 * HEAD] = trunk_dv_ref[...] + dv_ref[0:TRUNK, :]


def back_kernel(in_ref, trunk_dq_ref, leaf_tree_ref, dq_ref, leaf_kv_ref, rows_ref):
    count = leaf_tree_ref.shape[0]
    seg = lax.axis_index("seg")
    selector = leaf_selector(leaf_tree_ref, seg)
    rows_ref[...] = in_ref[...].astype(f32)
    leaf_rows = LEAF * count
    for tile in range(BACK_TILES):
        parts = [rows_ref[pl.ds(tile * LEAF + a, count, BACK_ROWS), :] for a in range(LEAF)]
        moved = dot(selector, jnp.concatenate(parts, axis=0).astype(bf16), (0, 0)).astype(bf16)
        if tile < GROUP:
            dq_ref[TRUNK : TRUNK + leaf_rows, tile * HEAD : (tile + 1) * HEAD] = moved
        else:
            at = (tile - GROUP) * HEAD
            leaf_kv_ref[:, at : at + HEAD] = moved
    dq_ref[0:TRUNK, :] = trunk_dq_ref[...]


def hidden_sum(kv_ref, kept_refs, swapped_ref):
    rows = kv_ref.shape[0] // (2 * len(kept_refs))
    kvh = lax.axis_index("kvh")
    chip, core = kvh >> 1, kvh & 1
    chips = len(kept_refs)
    total = None
    for step in range(chips):
        from_chip = lax.rem(chip + chips - step, chips)
        for other in range(2):
            head = 2 * from_chip + (core if other == 0 else 1 - core)
            kv = kv_ref[pl.ds(pl.multiple_of(head * rows, rows), rows), :].astype(bf16)
            for part in range(2):
                if other == 0:
                    weight = kept_refs[step][part, core]
                else:
                    weight = swapped_ref[step, part]
                term = dot(kv[:, part * HEAD : (part + 1) * HEAD], weight, (1, 1))
                total = term if total is None else total + term
    return total.astype(bf16)


def hidden_trunk_kernel(kv_ref, swapped_ref, *refs):
    refs[-1][...] = hidden_sum(kv_ref, refs[:-1], swapped_ref)


def hidden_leaf_kernel(kv_ref, trunk_ref, swapped_ref, *refs):
    out_ref = refs[-1]
    out_ref[0:TRUNK, :] = trunk_ref[...]
    out_ref[TRUNK:, :] = hidden_sum(kv_ref, refs[:-1], swapped_ref)


def call(kernel, outs, in_specs, scratch=(), flops=0, moved=0):
    many = isinstance(outs, list)
    return pl.pallas_call(
        kernel,
        out_shape=outs,
        in_specs=in_specs,
        out_specs=[vmem] * len(outs) if many else vmem,
        scratch_shapes=list(scratch),
        compiler_params=pltpu.CompilerParams(vmem_limit_bytes=48 * 1024 * 1024),
        cost_estimate=pl.CostEstimate(flops=flops, bytes_accessed=moved, transcendentals=0),
    )


def shards(queries, key_rows, value_rows, grad_out, w_key, w_value, trunk_len, leaf_len, leaf_tree):
    count = lax.axis_size("seg")
    heads = lax.axis_size("kvh")
    chips = heads // 2
    leaf_rows = LEAF * count
    row_width = queries.shape[1]
    hidden = w_key.shape[0]
    kvh = lax.axis_index("kvh")
    chip, core = kvh // 2, kvh % 2
    out = jax.ShapeDtypeStruct

    send = call(
        send_kernel,
        out((count * OUT_ROWS, HEAD), bf16),
        [vmem] * 5,
        [pltpu.VMEM((count * OUT_ROWS, HEAD), f32)],
        flops=10**8,
        moved=10**6,
    )(queries, grad_out, key_rows, value_rows, leaf_tree)
    got = lax.all_to_all(
        send.reshape(count, OUT_ROWS, HEAD), "seg", split_axis=0, concat_axis=0, tiled=True
    ).reshape(count * OUT_ROWS, HEAD)

    per_chip = hidden // chips

    def piece(step):
        at = lax.rem(chip + step, chips) * per_chip
        parts = [lax.dynamic_slice_in_dim(w, at, per_chip, axis=0) for w in (w_key, w_value)]
        return jnp.stack(parts).reshape(2, 2, per_chip // 2, HEAD)

    kept = [piece(0)]
    for step in range(1, chips):
        route = [(2 * x + c, 2 * ((x + step) % chips) + c) for x in range(chips) for c in range(2)]
        kept.append(lax.ppermute(piece(step), "kvh", route))
    for_other = jnp.stack([lax.dynamic_index_in_dim(w, 1 - core, 1, keepdims=False) for w in kept])
    swapped = lax.ppermute(for_other, "kvh", [(i, i ^ 1) for i in range(heads)])

    trunk_dq, trunk_dk, trunk_dv = call(
        trunk_kernel,
        [out((TRUNK, row_width), bf16), out((TRUNK, HEAD), f32), out((TRUNK, HEAD), f32)],
        [vmem] * 4 + [smem],
        flops=5 * 2 * GROUP * TRUNK * TRUNK * HEAD,
        moved=10**6,
    )(queries, grad_out, key_rows, value_rows, trunk_len)

    keys_all = TRUNK + leaf_rows
    back, trunk_kv = call(
        leaf_kernel,
        [out((count * BACK_ROWS, HEAD), bf16), out((TRUNK, 2 * HEAD), f32)],
        [vmem] * 7 + [smem],
        [
            pltpu.VMEM((count * OUT_ROWS, HEAD), f32),
            pltpu.VMEM((count * BACK_ROWS, HEAD), f32),
            pltpu.VMEM((keys_all, HEAD), f32),
            pltpu.VMEM((keys_all, HEAD), f32),
        ],
        flops=5 * 2 * GROUP * leaf_rows * keys_all * HEAD,
        moved=10**6,
    )(got, key_rows, value_rows, trunk_dk, trunk_dv, leaf_tree, leaf_len, trunk_len)

    trunk_all = lax.all_gather(trunk_kv, "kvh", axis=0, tiled=True)
    back = lax.all_to_all(
        back.reshape(count, BACK_ROWS, HEAD), "seg", split_axis=0, concat_axis=0, tiled=True
    ).reshape(count * BACK_ROWS, HEAD)
    grad_query, leaf_kv = call(
        back_kernel,
        [out(queries.shape, bf16), out((leaf_rows, 2 * HEAD), bf16)],
        [vmem] * 3,
        [pltpu.VMEM((count * BACK_ROWS, HEAD), f32)],
        flops=10**8,
        moved=10**6,
    )(back, trunk_dq, leaf_tree)
    leaf_all = lax.all_gather(leaf_kv, "kvh", axis=0, tiled=True)
    columns = hidden // heads
    flops = 2 * TRUNK * 2 * HEAD * heads * columns
    hidden_trunk = call(
        hidden_trunk_kernel, out((TRUNK, columns), bf16), [vmem] * (2 + chips), flops=flops, moved=4 * 10**6
    )(trunk_all, swapped, *kept)
    grad_hidden = call(
        hidden_leaf_kernel, out((TRUNK + leaf_rows, columns), bf16), [vmem] * (3 + chips), flops=flops, moved=4 * 10**6
    )(leaf_all, hidden_trunk, swapped, *kept)
    return (grad_query, grad_hidden)


def solution(mesh):
    in_specs = (
        P("seg", "kvh"),
        P("seg", "kvh"),
        P("seg", "kvh"),
        P("seg", "kvh"),
        P(None, "kvh"),
        P(None, "kvh"),
        P(),
        P(),
        P(),
    )
    out_specs = (P("seg", "kvh"), P("seg", "kvh"))
    return jax.shard_map(shards, mesh=mesh, in_specs=in_specs, out_specs=out_specs, check_vma=False)
```

time: 205 us -> 132 us (0.64)
  waiting for transfers between devices: 75 us -> 27.9 us
  local copies, waits for them, and re-layouts: 32.2 us -> 12.1 us
  blocking collectives: 0 us -> 16.4 us
  starting transfers between devices: 59 us -> 42.9 us
  matrix products: 14.7 us -> 0 us
  Pallas kernels: 0 us -> 11.5 us
    all_to_all x8 -> x2, waiting for transfers between devices: 60.7 us -> 12.4 us  [the longest x1 12.4 us: shards(): lax.all_to_all(back.reshape(count, BACK_ROWS, HEAD), 'seg', split_axis=0,...]
    all_to_all x8 -> x2, starting transfers between devices: 58.9 us -> 29.3 us  [the longest x1 17.1 us: shards(): lax.all_to_all(send.reshape(count, OUT_ROWS, HEAD), 'seg', split_axis=0,...]
    all_gather x0 -> x1, blocking collectives: none -> 16.4 us  [shards(): leaf_all = lax.all_gather(leaf_kv, 'kvh', axis=0, tiled=True)]
    ppermute x0 -> x4, waiting for transfers between devices: none -> 15.5 us  [the longest x3 15.5 us: shards(): kept.append(lax.ppermute(piece(step), 'kvh', route))]
    dot_general x16 -> x0, matrix products: 14.7 us -> none  [the longest x4 6.08 us: pair_products(): jnp.einsum('brgd,bcd->bgrc', head_rows, key_cols, preferred_element_type=...]
    unnamed x2 -> x1, waiting for transfers between devices: 14.3 us -> 0.02 us
    ppermute x0 -> x4, starting transfers between devices: none -> 13.6 us  [the longest x3 10.6 us: shards(): kept.append(lax.ppermute(piece(step), 'kvh', route))]
    pallas_call x0 -> x6, Pallas kernels: none -> 11.5 us  [the longest x1 3.62 us: shards(): call(leaf_kernel, [out((count * BACK_ROWS, HEAD), bf16), out((TRUNK, 2 *...]
  transfers between devices with their start and end apart: 9 -> 7, of which waited for: 9 -> 3; matrix products, arithmetic and copies ran while one was open for 17% -> 6% of each run, Pallas kernels for 0% -> 6%
where the time goes in v1:
time: 132 us; the launch traced here: 131 us
  starting transfers between devices  42.9 us (32%)
  waiting for transfers between devices  27.9 us (21%)
  blocking collectives  16.4 us (12%)
  between operations  14.3 us (11%)
  local copies, waits for them, and re-layouts  12.1 us (9%)
  Pallas kernels  11.5 us (9%)
  other arithmetic  6.17 us (5%)
    all_to_all x1, starting transfers between devices, shards(): lax.all_to_all(send.reshape(count, OUT_ROWS, HEAD), 'seg', split_axis=0,...  17.1 us
    all_gather x1, blocking collectives, shards(): leaf_all = lax.all_gather(leaf_kv, 'kvh', axis=0, tiled=True)  16.4 us
    ppermute x3, waiting for transfers between devices, shards(): kept.append(lax.ppermute(piece(step), 'kvh', route))  15.5 us
    all_to_all x1, waiting for transfers between devices, shards(): lax.all_to_all(back.reshape(count, BACK_ROWS, HEAD), 'seg', split_axis=0,...  12.4 us
    all_to_all x1, starting transfers between devices, shards(): lax.all_to_all(back.reshape(count, BACK_ROWS, HEAD), 'seg', split_axis=0,...  12.2 us
    ppermute x3, starting transfers between devices, shards(): kept.append(lax.ppermute(piece(step), 'kvh', route))  10.6 us
    unnamed x42, local copies, waits for them, and re-layouts  9.78 us
    another operation x4, other arithmetic, piece(): return jnp.stack(parts).reshape(2, 2, per_chip // 2, HEAD)  3.85 us
  transfers between devices with their start and end apart: 7, of which 3 were waited for; matrix products, arithmetic and copies ran while one was open for 6% of the time, Pallas kernels for 6%

profile of v1, /device:TPU:1, one launch (start us, length us, event | category | flops | bytes accessed | tf_op | source)
XLA Modules:
  0.0 131.4 jit_solution(13686611766314152178)
XLA Ops:
  7.2 0.0 copy-start.3
  7.2 1.0 copy-done.3
  8.1 1.0 copy-done.5
  9.1 0.8 copy-done.9
  10.0 0.8 copy-done.11
  10.8 0.8 copy-done.15
  11.6 1.2 shard_map.104
  12.7 17.1 %all-to-all-start = ((bf16[64,24,128]{2,1,0:T(8,128)(2,1)}), bf16[64,24,128]{2,1,0:T(8,128)(2,1)S(1)}, u32[]{:S(2)}, u32[]{:S(2)}) async-start(bf16[64,24,128]{2,1,0:T(8,128)(2,1)} %bitcast), calls=%async_computation | async-start | bytes 786432 | tf_op jit(solution)/shard_map/all_to_all | solution.py:235
  29.9 0.0 all-gather.2.cloned.1.call-start
  30.0 0.0 copy-done.20
  30.0 2.3 %constant_dynamic-slice_fusion.6 = (bf16[1280,128]{1,0:T(8,128)(2,1)}, bf16[1280,128]{1,0:T(8,128)(2,1)S(1)}, bf16[1280,128]{1,0:T(8,128)(2,1)S(1)}, bf16[1280,1...) fusion(bf16[5120,128]{1,0:T(8,128)(2,1)S(1)} %copy-done.20, ...), kind=kLoop, calls=%fused_computation.18 | loop fusion | bytes 5242896 | tf_op jit(solution)/shard_map/dynamic_slice | solution.py:243
  32.3 0.9 pad_maximum_fusion.2
  33.2 3.1 %collective-permute-start = (bf16[2,2,640,128]{3,2,1,0:T(8,128)(2,1)}, bf16[2,2,640,128]{3,2,1,0:T(8,128)(2,1)S(1)}, u32[]{:S(2)}, u32[]{:S(2)}) collective-permute-start(bf16[2,2,640,128]{3,2,1,0:T(8,128)(2,1)} %pad_maximum_fusion.2), channel_id=1, source_target_pairs={{0,2},{1,3},{2,4},{3,5},{4,6},{5,7},{6,0},{7,1},{8,10},{9,11},{10,... | collective-permute-start | bytes 1966088 | tf_op jit(solution)/shard_map/ppermute | solution.py:249
  36.3 0.0 copy-start.4
  36.3 0.0 copy-start.6
  36.3 0.0 copy-start.10
  36.3 0.0 copy-start.12
  36.4 0.0 copy-start.18
  36.4 0.9 pad_maximum_fusion.3
  37.3 4.5 %collective-permute-start.1 = (bf16[2,2,640,128]{3,2,1,0:T(8,128)(2,1)}, bf16[2,2,640,128]{3,2,1,0:T(8,128)(2,1)S(1)}, u32[]{:S(2)}, u32[]{:S(2)}) collective-permute-start(bf16[2,2,640,128]{3,2,1,0:T(8,128)(2,1)} %pad_maximum_fusion.3), channel_id=1, source_target_pairs={{0,4},{1,5},{2,6},{3,7},{4,0},{5,1},{6,2},{7,3},{8,12},{9,13},{10,... | collective-permute-start | bytes 1966088 | tf_op jit(solution)/shard_map/ppermute | solution.py:249
  41.8 0.9 pad_maximum_fusion.4
  42.7 3.1 %collective-permute-start.2 = (bf16[2,2,640,128]{3,2,1,0:T(8,128)(2,1)}, bf16[2,2,640,128]{3,2,1,0:T(8,128)(2,1)S(1)}, u32[]{:S(2)}, u32[]{:S(2)}) collective-permute-start(bf16[2,2,640,128]{3,2,1,0:T(8,128)(2,1)} %pad_maximum_fusion.4), channel_id=1, source_target_pairs={{0,6},{1,7},{2,0},{3,1},{4,2},{5,3},{6,4},{7,5},{8,14},{9,15},{10,... | collective-permute-start | bytes 1966088 | tf_op jit(solution)/shard_map/ppermute | solution.py:249
  45.8 0.0 copy-done.4
  45.8 2.8 %shard_map.105 = (bf16[128,640]{1,0:T(8,128)(2,1)S(1)}, f32[128,128]{1,0:T(8,128)S(1)}, f32[128,128]{1,0:T(8,128)S(1)}) custom-call(bf16[256,640]{1,0:T(8,128)(2,1)S(1)} %copy-done.4, bf16[256,640]{1,0:T(8,128)(2,1)S(1)} %copy-done.6, bf16[256,128]{1,0:T(8,128)(2,1)S(1)} %copy-done.10, bf16[256,128]{1,0:T(8,128)(2,1)S(1)} %copy-done.12, s32[64]{0:T(128)S(1)} %copy-done.18), custom_call_target="tpu_custom_call" | custom-call | flops 104857600 | bytes 1000000 | tf_op jit(solution)/shard_map/pallas_call | solution.py:253
  48.7 0.6 copy-done.13
  49.3 0.0 all-to-all-done
  49.3 3.6 %shard_map.106 = (bf16[1024,128]{1,0:T(8,128)(2,1)S(1)}, f32[128,256]{1,0:T(8,128)}) custom-call(bf16[1536,128]{1,0:T(8,128)(2,1)S(1)} %bitcast.21, bf16[256,128]{1,0:T(8,128)(2,1)S(1)} %copy-done.10, bf16[256,128]{1,0:T(8,128)(2,1)S(1)} %copy-done.12, f32[128,128]{1,0:T(8,128)S(1)} %get-tuple-element.9.trunk_dk_ref, ...), custom_call_target="tpu_custom_call" | custom-call | flops 209715200 | bytes 1000000 | tf_op jit(solution)/shard_map/pallas_call | solution.py:262
  52.9 0.7 copy-done.8
  53.7 0.0 all-gather.2.cloned.1.call-update
  53.7 1.0 fusion.1
  54.7 0.0 collective-permute-done.refs_1_
  54.8 12.0 %collective-permute-done.1.refs_2_ = bf16[2,2,640,128]{3,2,1,0:T(8,128)(2,1)S(1)} collective-permute-done((bf16[2,2,640,128]{3,2,1,0:T(8,128)(2,1)}, bf16[2,2,640,128]{3,2,1,0:T(8,128)(2,1)S(1)}, u32[]{:S(2)}, u32[]{:S(2)}) %collective-permute-start.1) | collective-permute-done | bytes 655392 | tf_op jit(solution)/shard_map/ppermute | solution.py:249
  66.8 3.4 %collective-permute-done.2.refs_3_ = bf16[2,2,640,128]{3,2,1,0:T(8,128)(2,1)S(1)} collective-permute-done((bf16[2,2,640,128]{3,2,1,0:T(8,128)(2,1)}, bf16[2,2,640,128]{3,2,1,0:T(8,128)(2,1)S(1)}, u32[]{:S(2)}, u32[]{:S(2)}) %collective-permute-start.2) | collective-permute-done | bytes 655392 | tf_op jit(solution)/shard_map/ppermute | solution.py:249
  70.3 1.3 pad_maximum_fusion
  71.6 2.9 %collective-permute-start.3 = (bf16[4,2,640,128]{3,2,1,0:T(8,128)(2,1)}, bf16[4,2,640,128]{3,2,1,0:T(8,128)(2,1)S(1)}, u32[]{:S(2)}, u32[]{:S(2)}) collective-permute-start(bf16[4,2,640,128]{3,2,1,0:T(8,128)(2,1)} %pad_maximum_fusion), channel_id=1, source_target_pairs={{0,1},{1,0},{2,3},{3,2},{4,5},{5,4},{6,7},{7,6},{8,9},{9,8},{10,11... | collective-permute-start | bytes 3932168 | tf_op jit(solution)/shard_map/ppermute | solution.py:251
  74.5 12.2 %all-to-all-start.1 = ((bf16[64,16,128]{2,1,0:T(8,128)(2,1)}), bf16[64,16,128]{2,1,0:T(8,128)(2,1)S(1)}, u32[]{:S(2)}, u32[]{:S(2)}) async-start(bf16[64,16,128]{2,1,0:T(8,128)(2,1)} %bitcast.22), calls=%async_computation.1 | async-start | bytes 524288 | tf_op jit(solution)/shard_map/all_to_all | solution.py:277
  86.7 1.1 pad_maximum_fusion.1.refs_0_
  87.8 12.4 %all-to-all-done.1 = bf16[64,16,128]{2,1,0:T(8,128)(2,1)S(1)} async-done(((bf16[64,16,128]{2,1,0:T(8,128)(2,1)}), bf16[64,16,128]{2,1,0:T(8,128)(2,1)S(1)}, u32[]{:S(2)}, u32[]{:S(2)}) %all-to-all-start.1) | async-done | bytes 262176 | tf_op jit(solution)/shard_map/all_to_all | solution.py:277
  100.2 0.9 copy-done.14
  101.1 0.8 copy-done.17
  101.9 1.1 shard_map.107
  103.0 16.4 %all_gather.6.kv_ref = bf16[1024,256]{1,0:T(8,128)(2,1)} all-gather(bf16[128,256]{1,0:T(8,128)(2,1)S(1)} %get-tuple-element.14), channel_id=1, replica_groups=mesh['seg'=64,'kvh'=8] {'kvh'}, dimensions={0}, use_global_device_ids=true | all-gather | bytes 589824 | tf_op jit(solution)/shard_map/all_gather | solution.py:288
  119.4 0.0 collective-permute-done.3.swapped_ref
  119.4 1.1 copy-done.1
  120.5 1.2 copy-done.7
  121.7 1.0 shard_map.108.trunk_ref
  122.8 0.0 copy-done.2
  122.8 1.8 %shard_map.109 = bf16[256,640]{1,0:T(8,128)(2,1)} custom-call(bf16[1024,256]{1,0:T(8,128)(2,1)S(1)} %copy-done.2, bf16[128,640]{1,0:T(8,128)(2,1)S(1)} %shard_map.108.trunk_ref, bf16[4,2,640,128]{3,2,1,0:T(8,128)(2,1)S(1)} %collective-permute-done.3.swapped_ref, bf16[2,2,640,128]{3,2,1,0:T(8,128)(2,1)S(1)} %pad_maximum_fusion.1.refs_0_, ...), custom_call_target="tpu_custom_call" | custom-call | flops 335544320 | bytes 4000000 | tf_op jit(solution)/shard_map/pallas_call | solution.py:294
  (26 shorter events, 0.1 us)
Async XLA Ops:
  7.2 1.0 copy-start.3
  8.1 1.0 copy-start.5
  9.1 0.8 copy-start.9
  10.0 0.8 copy-start.11
  10.8 0.8 copy-start.15
  11.6 18.5 %copy-start.20 = (bf16[5120,128]{1,0:T(8,128)(2,1)S(1)}, bf16[5120,128]{1,0:T(8,128)(2,1)}, u32[]{:S(2)}) copy-start(bf16[5120,128]{1,0:T(8,128)(2,1)} %param.14) | copy-start | bytes 3932164
  12.7 36.6 %all-to-all-start = ((bf16[64,24,128]{2,1,0:T(8,128)(2,1)}), bf16[64,24,128]{2,1,0:T(8,128)(2,1)S(1)}, u32[]{:S(2)}, u32[]{:S(2)}) async-start(bf16[64,24,128]{2,1,0:T(8,128)(2,1)} %bitcast), calls=%async_computation | async-start | bytes 786432 | tf_op jit(solution)/shard_map/all_to_all | solution.py:235
  29.9 89.5 %all-gather.2.cloned.1.call-start = ((), (), s32[]{:S(2)}) async-start(), calls=%async_computation.2 | async-start | bytes 1179648 | tf_op jit(solution)/shard_map/all_gather | solution.py:276
  33.2 21.5 %collective-permute-start = (bf16[2,2,640,128]{3,2,1,0:T(8,128)(2,1)}, bf16[2,2,640,128]{3,2,1,0:T(8,128)(2,1)S(1)}, u32[]{:S(2)}, u32[]{:S(2)}) collective-permute-start(bf16[2,2,640,128]{3,2,1,0:T(8,128)(2,1)} %pad_maximum_fusion.2), channel_id=1, source_target_pairs={{0,2},{1,3},{2,4},{3,5},{4,6},{5,7},{6,0},{7,1},{8,10},{9,11},{10,... | collective-permute-start | bytes 1966088 | tf_op jit(solution)/shard_map/ppermute | solution.py:249
  36.3 9.5 %copy-start.4 = (bf16[256,640]{1,0:T(8,128)(2,1)S(1)}, bf16[256,640]{1,0:T(8,128)(2,1)}, u32[]{:S(2)}) copy-start(bf16[256,640]{1,0:T(8,128)(2,1)} %q_ref.3) | copy-start | bytes 983044
  36.3 9.4 %copy-start.6 = (bf16[256,640]{1,0:T(8,128)(2,1)S(1)}, bf16[256,640]{1,0:T(8,128)(2,1)}, u32[]{:S(2)}) copy-start(bf16[256,640]{1,0:T(8,128)(2,1)} %g_ref.3) | copy-start | bytes 983044
  36.3 9.4 %copy-start.10 = (bf16[256,128]{1,0:T(8,128)(2,1)S(1)}, bf16[256,128]{1,0:T(8,128)(2,1)}, u32[]{:S(2)}) copy-start(bf16[256,128]{1,0:T(8,128)(2,1)} %k_ref.5) | copy-start | bytes 196612
  36.3 9.4 %copy-start.12 = (bf16[256,128]{1,0:T(8,128)(2,1)S(1)}, bf16[256,128]{1,0:T(8,128)(2,1)}, u32[]{:S(2)}) copy-start(bf16[256,128]{1,0:T(8,128)(2,1)} %v_ref.5) | copy-start | bytes 196612
  36.4 9.4 %copy-start.18 = (s32[64]{0:T(128)S(1)}, s32[64]{0:T(128)}, u32[]{:S(2)}) copy-start(s32[64]{0:T(128)} %trunk_len_ref.3) | copy-start | bytes 772
  37.3 12.0 %copy-start.16 = (s32[64,64]{1,0:T(8,128)S(1)}, s32[64,64]{1,0:T(8,128)}, u32[]{:S(2)}) copy-start(s32[64,64]{1,0:T(8,128)} %leaf_tree_ref.5) | copy-start | bytes 49156
  37.3 12.0 %copy-start.19 = (s32[64,64]{1,0:T(8,128)S(1)}, s32[64,64]{1,0:T(8,128)}, u32[]{:S(2)}) copy-start(s32[64,64]{1,0:T(8,128)} %leaf_len_ref.1) | copy-start | bytes 49156
  37.3 29.5 %collective-permute-start.1 = (bf16[2,2,640,128]{3,2,1,0:T(8,128)(2,1)}, bf16[2,2,640,128]{3,2,1,0:T(8,128)(2,1)S(1)}, u32[]{:S(2)}, u32[]{:S(2)}) collective-permute-start(bf16[2,2,640,128]{3,2,1,0:T(8,128)(2,1)} %pad_maximum_fusion.3), channel_id=1, source_target_pairs={{0,4},{1,5},{2,6},{3,7},{4,0},{5,1},{6,2},{7,3},{8,12},{9,13},{10,... | collective-permute-start | bytes 1966088 | tf_op jit(solution)/shard_map/ppermute | solution.py:249
  42.7 27.6 %collective-permute-start.2 = (bf16[2,2,640,128]{3,2,1,0:T(8,128)(2,1)}, bf16[2,2,640,128]{3,2,1,0:T(8,128)(2,1)S(1)}, u32[]{:S(2)}, u32[]{:S(2)}) collective-permute-start(bf16[2,2,640,128]{3,2,1,0:T(8,128)(2,1)} %pad_maximum_fusion.4), channel_id=1, source_target_pairs={{0,6},{1,7},{2,0},{3,1},{4,2},{5,3},{6,4},{7,5},{8,14},{9,15},{10,... | collective-permute-start | bytes 1966088 | tf_op jit(solution)/shard_map/ppermute | solution.py:249
  48.7 0.7 copy-start.13
  52.9 0.7 copy-start.8
  70.3 1.3 copy-start
  71.6 47.8 %collective-permute-start.3 = (bf16[4,2,640,128]{3,2,1,0:T(8,128)(2,1)}, bf16[4,2,640,128]{3,2,1,0:T(8,128)(2,1)S(1)}, u32[]{:S(2)}, u32[]{:S(2)}) collective-permute-start(bf16[4,2,640,128]{3,2,1,0:T(8,128)(2,1)} %pad_maximum_fusion), channel_id=1, source_target_pairs={{0,1},{1,0},{2,3},{3,2},{4,5},{5,4},{6,7},{7,6},{8,9},{9,8},{10,11... | collective-permute-start | bytes 3932168 | tf_op jit(solution)/shard_map/ppermute | solution.py:251
  74.5 25.6 %all-to-all-start.1 = ((bf16[64,16,128]{2,1,0:T(8,128)(2,1)}), bf16[64,16,128]{2,1,0:T(8,128)(2,1)S(1)}, u32[]{:S(2)}, u32[]{:S(2)}) async-start(bf16[64,16,128]{2,1,0:T(8,128)(2,1)} %bitcast.22), calls=%async_computation.1 | async-start | bytes 524288 | tf_op jit(solution)/shard_map/all_to_all | solution.py:277
  100.2 0.9 copy-start.14
  101.1 0.8 copy-start.17
  119.4 1.1 copy-start.1
  120.5 1.2 copy-start.7
  121.7 1.0 copy-start.2
Sparse Core Ops, SparseCore 0:
  53.8 28.5 all-gather.1

commit v2 on v1

v2 whole, which is shorter than its diff:
```python
import functools
import math

import jax
import jax.numpy as jnp
from jax import lax
from jax.experimental import pallas as pl
from jax.experimental.pallas import tpu as pltpu
from jax.sharding import PartitionSpec as P

GROUP = 5
TRUNK = 128
LEAF = 2
HEAD = 128
OUT_TILES = 2 * GROUP + 2
OUT_ROWS = OUT_TILES * LEAF
BACK_TILES = GROUP + 2
BACK_ROWS = 16
VERY_NEGATIVE = -1e30
SCALE = 1.0 / math.sqrt(HEAD)

f32 = jnp.float32
bf16 = jnp.bfloat16
vmem = pl.BlockSpec(memory_space=pltpu.VMEM)
smem = pl.BlockSpec(memory_space=pltpu.SMEM)
hbm = pl.BlockSpec(memory_space=pltpu.HBM)


def dot(a, b, contract):
    return lax.dot_general(a, b, ((contract[0:1], contract[1:2]), ((), ())), preferred_element_type=f32)


def leaf_selector(leaf_tree_ref, seg):
    count = leaf_tree_ref.shape[0]
    tree_row = leaf_tree_ref[pl.ds(seg, 1), :].astype(f32).astype(bf16)
    tree_rows = jnp.broadcast_to(tree_row, (16, count))
    leaf = lax.broadcasted_iota(jnp.int32, (count, LEAF * count), 0)
    col = lax.broadcasted_iota(jnp.int32, (count, LEAF * count), 1)
    repeat = (leaf == (col >> 1)).astype(f32).astype(bf16)
    tree_of_col = dot(tree_rows, repeat, (1, 0))[0:1, :].astype(jnp.int32)
    row = lax.broadcasted_iota(jnp.int32, (LEAF * count, LEAF * count), 0)
    col = lax.broadcasted_iota(jnp.int32, (LEAF * count, LEAF * count), 1)
    row_pos = (row >= count).astype(jnp.int32)
    hit = (tree_of_col == row - row_pos * count) & (row_pos == (col & 1))
    return hit.astype(f32).astype(bf16)


def copies(pairs, sems):
    started = [pltpu.make_async_copy(src, dst, sems.at[i]) for i, (src, dst) in enumerate(pairs)]
    for copy in started:
        copy.start()
    return started


def send_kernel(
    q_ref, g_ref, k_ref, v_ref, leaf_tree_ref,
    out_ref, tree_ref, q_buf, g_buf, k_buf, v_buf, rows_ref, out_buf, sems, out_sem,
):
    count = tree_ref.shape[0]
    leaves = pl.ds(TRUNK, LEAF * count)
    loads = [(leaf_tree_ref, tree_ref)]
    loads += [(src.at[leaves, :], dst) for src, dst in zip((q_ref, g_ref, k_ref, v_ref), (q_buf, g_buf, k_buf, v_buf))]
    loads = copies(loads, sems)
    seg = lax.axis_index("seg")
    loads[0].wait()
    selector = leaf_selector(tree_ref, seg)
    tile = 0
    for load, ref in zip(loads[1:], (q_buf, g_buf, k_buf, v_buf)):
        load.wait()
        moved = dot(selector, ref[...], (1, 0))
        for part in range(ref.shape[1] // HEAD):
            for a in range(LEAF):
                rows_ref[pl.ds(tile * LEAF + a, count, OUT_ROWS), :] = moved[
                    a * count : (a + 1) * count, part * HEAD : (part + 1) * HEAD
                ]
            tile += 1
    out_buf[...] = rows_ref[...].astype(bf16)
    store = pltpu.make_async_copy(out_buf, out_ref, out_sem)
    store.start()
    store.wait()


def softmax_grads(scores, prob_grad, visible):
    masked = jnp.where(visible, scores, VERY_NEGATIVE)
    row_max = jnp.max(masked, axis=-1, keepdims=True)
    weights = jnp.where(visible, jnp.exp(masked - row_max), 0.0)
    row_total = jnp.maximum(jnp.sum(weights, axis=-1, keepdims=True), 1.0)
    probability = weights * (1.0 / row_total)
    row_delta = jnp.sum(probability * prob_grad, axis=-1, keepdims=True)
    score_grad = (probability * (prob_grad - row_delta)).astype(bf16)
    return probability.astype(bf16), score_grad


def leaf_visible(leaf_tree_ref, leaf_len_ref, trunk_len, seg):
    count = leaf_tree_ref.shape[0]
    in_len = jnp.sum(jnp.where(leaf_tree_ref[...] == seg, leaf_len_ref[...], 0), axis=1, keepdims=True)
    row_len = jnp.concatenate([in_len] * LEAF, axis=0)
    leaf_rows = LEAF * count
    shape = (leaf_rows, TRUNK + leaf_rows)
    row = lax.broadcasted_iota(jnp.int32, shape, 0)
    col = lax.broadcasted_iota(jnp.int32, shape, 1)
    row_pos = (row >= count).astype(jnp.int32)
    leaf_col = col - TRUNK
    col_pos = (leaf_col >= count).astype(jnp.int32)
    own = (row - row_pos * count == leaf_col - col_pos * count) & (col_pos <= row_pos)
    visible = ((col < trunk_len) & (col < TRUNK)) | ((col >= TRUNK) & own)
    return (visible & (row_pos < row_len)).astype(f32)


def trunk_kernel(
    q_in, g_in, k_in, v_in, leaf_tree_in, leaf_len_in, trunk_len_in, w_key_ref, w_value_ref,
    dq_ref, dkv_ref, visible_ref, selector_ref, own_ref, give_ref,
    q_ref, g_ref, k_ref, v_ref, leaf_tree_ref, leaf_len_ref, trunk_len_ref,
    dq_buf, dkv_buf, visible_buf, selector_buf, give_buf, sems, out_sems, weight_sems,
):
    trunk = pl.ds(0, TRUNK)
    core = lax.axis_index("kvh") & 1
    chips, block = own_ref.shape[1:3]
    pairs = []
    for chip in range(chips):
        for ref, which in ((give_buf, 1 - core), (own_ref, core)):
            rows = pl.ds(pl.multiple_of((2 * chip + which) * block, block), block)
            pairs += [(w.at[rows, :], ref.at[part, chip]) for part, w in enumerate((w_key_ref, w_value_ref))]
    loads = copies(
        [
            (trunk_len_in, trunk_len_ref),
            (k_in.at[trunk, :], k_ref),
            (v_in.at[trunk, :], v_ref),
            (q_in.at[trunk, :], q_ref),
            (g_in.at[trunk, :], g_ref),
            (leaf_tree_in, leaf_tree_ref),
            (leaf_len_in, leaf_len_ref),
        ],
        sems,
    )
    weight_loads = copies(pairs, weight_sems)
    for load in loads:
        load.wait()
    seg = lax.axis_index("seg")
    trunk_len = trunk_len_ref[seg]
    keys = k_ref[...]
    values = v_ref[...]
    row = lax.broadcasted_iota(jnp.int32, (TRUNK, TRUNK), 0)
    col = lax.broadcasted_iota(jnp.int32, (TRUNK, TRUNK), 1)
    visible = (col <= row) & (row < trunk_len)
    for g in range(GROUP):
        head_q = q_ref[:, g * HEAD : (g + 1) * HEAD]
        head_g = g_ref[:, g * HEAD : (g + 1) * HEAD]
        scores = dot(head_q, keys, (1, 1)) * SCALE
        prob_grad = dot(head_g, values, (1, 1))
        probability, score_grad = softmax_grads(scores, prob_grad, visible)
        dq_buf[:, g * HEAD : (g + 1) * HEAD] = (dot(score_grad, keys, (1, 0)) * SCALE).astype(bf16)
        head_dk = dot(score_grad, head_q, (0, 0))
        head_dv = dot(probability, head_g, (0, 0))
        if g == 0:
            dkv_buf[:, 0:HEAD] = head_dk
            dkv_buf[:, HEAD:] = head_dv
        else:
            dkv_buf[:, 0:HEAD] += head_dk
            dkv_buf[:, HEAD:] += head_dv
    visible_buf[...] = leaf_visible(leaf_tree_ref, leaf_len_ref, trunk_len, seg)
    selector_buf[...] = leaf_selector(leaf_tree_ref, seg)
    for load in weight_loads:
        load.wait()
    stores = copies(
        [
            (dq_buf, dq_ref.at[trunk, :]),
            (dkv_buf, dkv_ref),
            (visible_buf, visible_ref),
            (selector_buf, selector_ref),
            (give_buf, give_ref),
        ],
        out_sems,
    )
    for store in stores:
        store.wait()


def leaf_kernel(
    in_ref, k_in, v_in, trunk_dkv_in, visible_in,
    out_ref, trunk_kv_ref, rows_ref, back_ref, dk_ref, dv_ref, out_buf, kv_buf,
    k_ref, v_ref, trunk_dkv_ref, visible_ref, sems, out_sems,
):
    trunk = pl.ds(0, TRUNK)
    loads = copies(
        [
            (k_in.at[trunk, :], k_ref),
            (v_in.at[trunk, :], v_ref),
            (visible_in, visible_ref),
            (trunk_dkv_in, trunk_dkv_ref),
        ],
        sems,
    )
    leaf_rows = visible_ref.shape[0]
    count = leaf_rows // LEAF
    rows_ref[...] = in_ref[...].astype(f32)

    def gather(tile):
        parts = [rows_ref[pl.ds(tile * LEAF + a, count, OUT_ROWS), :] for a in range(LEAF)]
        return jnp.concatenate(parts, axis=0).astype(bf16)

    for load in loads:
        load.wait()
    keys = jnp.concatenate([k_ref[...], gather(2 * GROUP)], axis=0)
    values = jnp.concatenate([v_ref[...], gather(2 * GROUP + 1)], axis=0)
    visible = visible_ref[...] > 0.5
    for g in range(GROUP):
        head_q = gather(g)
        head_g = gather(GROUP + g)
        scores = dot(head_q, keys, (1, 1)) * SCALE
        prob_grad = dot(head_g, values, (1, 1))
        probability, score_grad = softmax_grads(scores, prob_grad, visible)
        head_dq = dot(score_grad, keys, (1, 0)) * SCALE
        for a in range(LEAF):
            back_ref[pl.ds(g * LEAF + a, count, BACK_ROWS), :] = head_dq[a * count : (a + 1) * count, :]
        head_dk = dot(score_grad, head_q, (0, 0))
        head_dv = dot(probability, head_g, (0, 0))
        if g == 0:
            dk_ref[...] = head_dk
            dv_ref[...] = head_dv
        else:
            dk_ref[...] += head_dk
            dv_ref[...] += head_dv
    for a in range(LEAF):
        at = TRUNK + a * count
        back_ref[pl.ds(GROUP * LEAF + a, count, BACK_ROWS), :] = dk_ref[at : at + count, :] * SCALE
        back_ref[pl.ds((GROUP + 1) * LEAF + a, count, BACK_ROWS), :] = dv_ref[at : at + count, :]
    for spare in range(BACK_TILES * LEAF, BACK_ROWS):
        back_ref[pl.ds(spare, count, BACK_ROWS), :] = jnp.zeros((count, HEAD), f32)
    out_buf[...] = back_ref[...].astype(bf16)
    store = pltpu.make_async_copy(out_buf, out_ref, out_sems.at[0])
    store.start()
    kv_buf[:, 0:HEAD] = ((trunk_dkv_ref[:, 0:HEAD] + dk_ref[0:TRUNK, :]) * SCALE).astype(bf16)
    kv_buf[:, HEAD:] = (trunk_dkv_ref[:, HEAD:] + dv_ref[0:TRUNK, :]).astype(bf16)
    store_kv = pltpu.make_async_copy(kv_buf, trunk_kv_ref, out_sems.at[1])
    store_kv.start()
    store.wait()
    store_kv.wait()


def moved_tile(in_ref, rows_ref, selector, tile):
    count = in_ref.shape[0] // BACK_ROWS
    parts = [rows_ref[pl.ds(tile * LEAF + a, count, BACK_ROWS), :] for a in range(LEAF)]
    return dot(selector, jnp.concatenate(parts, axis=0).astype(bf16), (0, 0)).astype(bf16)


def leaf_kv_kernel(in_ref, selector_ref, after_ref, out_ref, rows_ref, selector_buf, kv_buf, sem, out_sem):
    load = pltpu.make_async_copy(selector_ref, selector_buf, sem)
    load.start()
    rows_ref[...] = in_ref[...].astype(f32)
    load.wait()
    for part in range(2):
        kv_buf[:, part * HEAD : (part + 1) * HEAD] = moved_tile(in_ref, rows_ref, selector_buf[...], GROUP + part)
    store = pltpu.make_async_copy(kv_buf, out_ref, out_sem)
    store.start()
    store.wait()


def leaf_query_kernel(in_ref, selector_ref, dq_in_ref, dq_ref, rows_ref, selector_buf, dq_buf, sem, out_sem):
    load = pltpu.make_async_copy(selector_ref, selector_buf, sem)
    load.start()
    rows_ref[...] = in_ref[...].astype(f32)
    load.wait()
    for tile in range(GROUP):
        dq_buf[:, tile * HEAD : (tile + 1) * HEAD] = moved_tile(in_ref, rows_ref, selector_buf[...], tile)
    store = pltpu.make_async_copy(dq_buf, dq_ref.at[pl.ds(TRUNK, dq_buf.shape[0]), :], out_sem)
    store.start()
    store.wait()


def chip_part(kv_ref, kv_other_ref, own_ref, other_ref, block):
    kv = jnp.concatenate([kv_ref[...], kv_other_ref[...]], axis=1)
    weight = jnp.concatenate([ref[part, block] for ref in (own_ref, other_ref) for part in range(2)], axis=1)
    return dot(weight, kv, (1, 1)).astype(bf16)


def send_parts(half, kv_ref, kv_other_ref, own_ref, other_ref, out_ref, buf, sems):
    stores = []
    for block in range(buf.shape[0]):
        buf[block] = chip_part(kv_ref, kv_other_ref, own_ref, other_ref, block)
        stores.append(pltpu.make_async_copy(buf.at[block], out_ref.at[block, half], sems.at[block]))
        stores[-1].start()
    for store in stores:
        store.wait()


def trunk_part_kernel(kv_ref, kv_other_ref, own_ref, other_ref, out_ref, token_ref, buf, sems):
    send_parts(0, kv_ref, kv_other_ref, own_ref, other_ref, out_ref, buf, sems)
    token_ref[...] = jnp.zeros(token_ref.shape, f32)


def leaf_part_kernel(kv_ref, kv_other_ref, own_ref, other_ref, parts_ref, out_ref, buf, sems):
    send_parts(1, kv_ref, kv_other_ref, own_ref, other_ref, out_ref, buf, sems)


def hidden_kernel(came_ref, out_ref):
    rows = came_ref.shape[3]
    for half in range(came_ref.shape[1]):
        total = came_ref[0, half].astype(f32)
        for chip in range(1, came_ref.shape[0]):
            total += came_ref[chip, half].astype(f32)
        out_ref[half * rows : (half + 1) * rows, :] = total.T.astype(bf16)


def call(kernel, outs, in_specs, out_specs, scratch=(), flops=0, moved=0, aliases={}, limit=24):
    return pl.pallas_call(
        kernel,
        out_shape=outs,
        in_specs=in_specs,
        out_specs=out_specs,
        scratch_shapes=list(scratch),
        input_output_aliases=aliases,
        compiler_params=pltpu.CompilerParams(vmem_limit_bytes=limit * 1024 * 1024),
        cost_estimate=pl.CostEstimate(flops=flops, bytes_accessed=moved, transcendentals=0),
    )


def shards(queries, key_rows, value_rows, grad_out, w_key, w_value, trunk_len, leaf_len, leaf_tree):
    count = lax.axis_size("seg")
    heads = lax.axis_size("kvh")
    chips = heads // 2
    leaf_rows = LEAF * count
    row_width = queries.shape[1]
    hidden = w_key.shape[0]
    columns = hidden // heads
    out = jax.ShapeDtypeStruct
    dma = pltpu.SemaphoreType.DMA

    vm = pltpu.VMEM

    send = call(
        send_kernel,
        out((count * OUT_ROWS, HEAD), bf16),
        [hbm] * 5,
        hbm,
        [
            vm((count, count), jnp.int32),
            vm((leaf_rows, row_width), bf16),
            vm((leaf_rows, row_width), bf16),
            vm((leaf_rows, HEAD), bf16),
            vm((leaf_rows, HEAD), bf16),
            vm((count * OUT_ROWS, HEAD), f32),
            vm((count * OUT_ROWS, HEAD), bf16),
            dma((5,)),
            dma,
        ],
        flops=10**8,
        moved=10**6,
        limit=60,
    )(queries, grad_out, key_rows, value_rows, leaf_tree)
    got = lax.all_to_all(
        send.reshape(count, OUT_ROWS, HEAD), "seg", split_axis=0, concat_axis=0, tiled=True
    ).reshape(count * OUT_ROWS, HEAD)

    keys_all = TRUNK + leaf_rows
    dq, trunk_dkv, visible, selector, own, give = call(
        trunk_kernel,
        [
            out(queries.shape, bf16),
            out((TRUNK, 2 * HEAD), f32),
            out((leaf_rows, keys_all), f32),
            out((leaf_rows, leaf_rows), bf16),
            out((2, chips, columns, HEAD), bf16),
            out((2, chips, columns, HEAD), bf16),
        ],
        [hbm] * 9,
        [hbm] * 4 + [vmem, hbm],
        [
            vm((TRUNK, row_width), bf16),
            vm((TRUNK, row_width), bf16),
            vm((TRUNK, HEAD), bf16),
            vm((TRUNK, HEAD), bf16),
            vm((count, count), jnp.int32),
            vm((count, count), jnp.int32),
            pltpu.SMEM((count,), jnp.int32),
            vm((TRUNK, row_width), bf16),
            vm((TRUNK, 2 * HEAD), f32),
            vm((leaf_rows, keys_all), f32),
            vm((leaf_rows, leaf_rows), bf16),
            vm((2, chips, columns, HEAD), bf16),
            dma((7,)),
            dma((5,)),
            dma((4 * chips,)),
        ],
        flops=4 * 10**10,
        moved=10**7,
        limit=60,
    )(queries, grad_out, key_rows, value_rows, leaf_tree, leaf_len, trunk_len, w_key, w_value)

    def swap(value):
        return lax.ppermute(value, "kvh", [(i, i ^ 1) for i in range(heads)])

    other = swap(give)

    back, trunk_kv = call(
        leaf_kernel,
        [out((count * BACK_ROWS, HEAD), bf16), out((TRUNK, 2 * HEAD), bf16)],
        [vmem] + [hbm] * 4,
        [hbm] * 2,
        [
            vm((count * OUT_ROWS, HEAD), f32),
            vm((count * BACK_ROWS, HEAD), f32),
            vm((keys_all, HEAD), f32),
            vm((keys_all, HEAD), f32),
            vm((count * BACK_ROWS, HEAD), bf16),
            vm((TRUNK, 2 * HEAD), bf16),
            vm((TRUNK, HEAD), bf16),
            vm((TRUNK, HEAD), bf16),
            vm((TRUNK, 2 * HEAD), f32),
            vm((leaf_rows, keys_all), f32),
            dma((4,)),
            dma((2,)),
        ],
        flops=4 * 10**10,
        moved=10**6,
    )(got, key_rows, value_rows, trunk_dkv, visible)

    part_flops = 2 * TRUNK * 4 * HEAD * chips * columns
    parts_shape = out((chips, 2, columns, TRUNK), bf16)
    parts_scratch = [vm((chips, columns, TRUNK), bf16), dma((chips,))]
    parts, token = call(
        trunk_part_kernel,
        [parts_shape, out((8, HEAD), f32)],
        [vmem] * 4,
        [hbm, vmem],
        parts_scratch,
        flops=part_flops,
        moved=4 * 10**6,
    )(trunk_kv, swap(trunk_kv), own, other)
    back = lax.all_to_all(
        back.reshape(count, BACK_ROWS, HEAD), "seg", split_axis=0, concat_axis=0, tiled=True
    ).reshape(count * BACK_ROWS, HEAD)
    leaf_kv = call(
        leaf_kv_kernel,
        out((leaf_rows, 2 * HEAD), bf16),
        [vmem, hbm, hbm],
        hbm,
        [
            vm((count * BACK_ROWS, HEAD), f32),
            vm((leaf_rows, leaf_rows), bf16),
            vm((leaf_rows, 2 * HEAD), bf16),
            dma,
            dma,
        ],
        flops=10**7,
        moved=10**6,
    )(back, selector, token)
    parts = call(
        leaf_part_kernel,
        parts_shape,
        [vmem] * 4 + [hbm],
        hbm,
        parts_scratch,
        flops=part_flops,
        moved=4 * 10**6,
        aliases={4: 0},
        limit=60,
    )(leaf_kv, swap(leaf_kv), own, other, parts)
    came = lax.all_to_all(
        parts,
        "kvh",
        split_axis=0,
        concat_axis=0,
        tiled=True,
        axis_index_groups=[[2 * x + c for x in range(chips)] for c in range(2)],
    )
    grad_query = call(
        leaf_query_kernel,
        out(queries.shape, bf16),
        [vmem, hbm, hbm],
        hbm,
        [
            vm((count * BACK_ROWS, HEAD), f32),
            vm((leaf_rows, leaf_rows), bf16),
            vm((leaf_rows, row_width), bf16),
            dma,
            dma,
        ],
        flops=10**8,
        moved=10**6,
        aliases={2: 0},
    )(back, selector, dq)
    grad_hidden = call(
        hidden_kernel,
        out((TRUNK + leaf_rows, columns), bf16),
        [vmem],
        vmem,
        flops=10**6,
        moved=10**6,
    )(came)
    return (grad_query, grad_hidden)


def solution(mesh):
    in_specs = (
        P("seg", "kvh"),
        P("seg", "kvh"),
        P("seg", "kvh"),
        P("seg", "kvh"),
        P(None, "kvh"),
        P(None, "kvh"),
        P(),
        P(),
        P(),
    )
    out_specs = (P("seg", "kvh"), P("seg", "kvh"))
    return jax.shard_map(shards, mesh=mesh, in_specs=in_specs, out_specs=out_specs, check_vma=False)
```

time: 132 us -> 93.7 us (0.71)
  blocking collectives: 16.4 us -> 0 us
  between operations: 14.3 us -> 0.78 us
  Pallas kernels: 11.5 us -> 21.2 us
  local copies, waits for them, and re-layouts: 12.1 us -> 3.5 us
  other arithmetic: 6.17 us -> 0 us
  starting transfers between devices: 42.9 us -> 38.9 us
    all_gather x1 -> x0, blocking collectives: 16.4 us -> none  [shards(): leaf_all = lax.all_gather(leaf_kv, 'kvh', axis=0, tiled=True)]
    all_to_all x0 -> x1, waiting for transfers between devices: none -> 16.4 us  [shards(): lax.all_to_all(parts, 'kvh', split_axis=0, concat_axis=0, tiled=True, axi...]
    ppermute x4 -> x3, waiting for transfers between devices: 15.5 us -> 1.76 us  [swap(): return lax.ppermute(value, 'kvh', [(i, i ^ 1) for i in range(heads)])]
    pallas_call x5 -> x7, Pallas kernels: 7.92 us -> 17.6 us  [the longest x1 6.67 us: shards(): call(trunk_kernel, [out(queries.shape, bf16), out((TRUNK, 2 * HEAD), f32)...]
    all_to_all x1, waiting for transfers between devices: 12.4 us -> 5.59 us  [shards(): lax.all_to_all(back.reshape(count, BACK_ROWS, HEAD), 'seg', split_axis=0,...]
    unnamed x42 -> x20, local copies, waits for them, and re-layouts: 9.78 us -> 3.5 us
    another operation x6 -> x0, other arithmetic: 6.17 us -> none  [the longest x4 3.85 us: piece(): return jnp.stack(parts).reshape(2, 2, per_chip // 2, HEAD)]
    all_to_all x1, waiting for transfers between devices: 0.01 us -> 5.09 us  [shards(): lax.all_to_all(send.reshape(count, OUT_ROWS, HEAD), 'seg', split_axis=0,...]
  transfers between devices with their start and end apart: 7 -> 6, of which waited for: 3 -> 5; matrix products, arithmetic and copies ran while one was open for 6% -> 0% of each run, Pallas kernels for 6% -> 15%
where the time goes in v2:
time: 93.7 us; the launch traced here: 93.2 us
  starting transfers between devices  38.9 us (42%)
  waiting for transfers between devices  28.8 us (31%)
  Pallas kernels  21.2 us (23%)
  local copies, waits for them, and re-layouts  3.5 us (4%)
    all_to_all x1, starting transfers between devices, shards(): lax.all_to_all(send.reshape(count, OUT_ROWS, HEAD), 'seg', split_axis=0,...  17.1 us
    all_to_all x1, waiting for transfers between devices, shards(): lax.all_to_all(parts, 'kvh', split_axis=0, concat_axis=0, tiled=True, axi...  16.4 us
    ppermute x3, starting transfers between devices, swap(): return lax.ppermute(value, 'kvh', [(i, i ^ 1) for i in range(heads)])  10.3 us
    all_to_all x1, starting transfers between devices, shards(): lax.all_to_all(back.reshape(count, BACK_ROWS, HEAD), 'seg', split_axis=0,...  7.37 us
    pallas_call x1, Pallas kernels, shards(): call(trunk_kernel, [out(queries.shape, bf16), out((TRUNK, 2 * HEAD), f32)...  6.67 us
    all_to_all x1, waiting for transfers between devices, shards(): lax.all_to_all(back.reshape(count, BACK_ROWS, HEAD), 'seg', split_axis=0,...  5.59 us
    all_to_all x1, waiting for transfers between devices, shards(): lax.all_to_all(send.reshape(count, OUT_ROWS, HEAD), 'seg', split_axis=0,...  5.09 us
    all_to_all x1, starting transfers between devices, shards(): lax.all_to_all(parts, 'kvh', split_axis=0, concat_axis=0, tiled=True, axi...  4.03 us
  transfers between devices with their start and end apart: 6, of which 5 were waited for; matrix products, arithmetic and copies ran while one was open for 0% of the time, Pallas kernels for 15%

profile of v2, /device:TPU:1, one launch (start us, length us, event | category | flops | bytes accessed | tf_op | source)
XLA Modules:
  0.0 93.2 jit_solution(14430019888153776617)
XLA Ops:
  0.6 2.5 %shard_map.104 = bf16[1536,128]{1,0:T(8,128)(2,1)} custom-call(bf16[256,640]{1,0:T(8,128)(2,1)} %q_in.1, bf16[256,640]{1,0:T(8,128)(2,1)} %g_in.1, bf16[256,128]{1,0:T(8,128)(2,1)} %k_in.3, bf16[256,128]{1,0:T(8,128)(2,1)} %v_in.3, s32[64,64]{1,0:T(8,128)} %leaf_tree_in.1), custom_call_target="tpu_custom_call" | custom-call | flops 100000000 | bytes 1000000 | tf_op jit(solution)/shard_map/pallas_call | solution.py:331
  3.1 17.1 %all-to-all-start = ((bf16[64,24,128]{2,1,0:T(8,128)(2,1)}), bf16[64,24,128]{2,1,0:T(8,128)(2,1)S(1)}, u32[]{:S(2)}, u32[]{:S(2)}) async-start(bf16[64,24,128]{2,1,0:T(8,128)(2,1)} %bitcast.7), calls=%async_computation | async-start | bytes 786432 | tf_op jit(solution)/shard_map/all_to_all | solution.py:351
  20.3 0.0 copy-start.5
  20.3 0.0 copy-start.6
  20.3 6.7 %shard_map.105 = (bf16[256,640]{1,0:T(8,128)(2,1)}, f32[128,256]{1,0:T(8,128)}, f32[128,256]{1,0:T(8,128)}, bf16[128,128]{1,0:T(8,128)(2,1)}, bf16[2,4,640,128]{...) custom-call(bf16[256,640]{1,0:T(8,128)(2,1)} %q_in.1, bf16[256,640]{1,0:T(8,128)(2,1)} %g_in.1, bf16[256,128]{1,0:T(8,128)(2,1)} %k_in.3, ...), custom_call_target="tpu_custom_call" | custom-call | flops 40000000000 | bytes 10000000 | tf_op jit(solution)/shard_map/pallas_call | solution.py:356
  27.0 2.9 %collective-permute-start.1 = (bf16[2,4,640,128]{3,2,1,0:T(8,128)(2,1)}, bf16[2,4,640,128]{3,2,1,0:T(8,128)(2,1)S(1)}, u32[]{:S(2)}, u32[]{:S(2)}) collective-permute-start(bf16[2,4,640,128]{3,2,1,0:T(8,128)(2,1)} %get-tuple-element.19), channel_id=1, source_target_pairs={{0,1},{1,0},{2,3},{3,2},{4,5},{5,4},{6,7},{7,6},{8,9},{9,8},{10,11... | collective-permute-start | bytes 3932168 | tf_op jit(solution)/shard_map/ppermute | solution.py:391
  29.8 5.1 %all-to-all-done = bf16[64,24,128]{2,1,0:T(8,128)(2,1)S(1)} async-done(((bf16[64,24,128]{2,1,0:T(8,128)(2,1)}), bf16[64,24,128]{2,1,0:T(8,128)(2,1)S(1)}, u32[]{:S(2)}, u32[]{:S(2)}) %all-to-all-start) | async-done | bytes 393248 | tf_op jit(solution)/shard_map/all_to_all | solution.py:351
  34.9 0.0 copy-done.5
  34.9 0.0 copy-done.6
  34.9 0.0 copy-start.7
  34.9 0.9 copy-done.7
  35.8 0.0 copy-start.8
  35.8 0.9 copy-done.8
  36.7 0.0 copy-start
  36.7 3.7 %shard_map.106 = (bf16[1024,128]{1,0:T(8,128)(2,1)}, bf16[128,256]{1,0:T(8,128)(2,1)S(1)}) custom-call(bf16[1536,128]{1,0:T(8,128)(2,1)S(1)} %bitcast.6, bf16[256,128]{1,0:T(8,128)(2,1)S(1)} %copy-done.5, bf16[256,128]{1,0:T(8,128)(2,1)S(1)} %copy-done.6, f32[128,256]{1,0:T(8,128)S(1)} %copy-done.7, f32[128,256]{1,0:T(8,128)S(1)} %copy-done.8), custom_call_target="tpu_custom_call" | custom-call | flops 40000000000 | bytes 1000000 | tf_op jit(solution)/shard_map/pallas_call | solution.py:395
  40.4 7.4 %all-to-all-start.1 = ((bf16[64,16,128]{2,1,0:T(8,128)(2,1)}), bf16[64,16,128]{2,1,0:T(8,128)(2,1)S(1)}, u32[]{:S(2)}, u32[]{:S(2)}) async-start(bf16[64,16,128]{2,1,0:T(8,128)(2,1)} %bitcast.2), calls=%async_computation.1 | async-start | bytes 524288 | tf_op jit(solution)/shard_map/all_to_all | solution.py:430
  47.8 2.6 %collective-permute-start = (bf16[128,256]{1,0:T(8,128)(2,1)S(1)}, bf16[128,256]{1,0:T(8,128)(2,1)S(1)}, u32[]{:S(2)}, u32[]{:S(2)}) collective-permute-start(bf16[128,256]{1,0:T(8,128)(2,1)S(1)} %get-tuple-element.17.kv_ref), channel_id=1, source_target_pairs={{0,1},{1,0},{2,3},{3,2},{4,5},{5,4},{6,7},{7,6},{8,9},{9,8},{10,11... | collective-permute-start | bytes 196616 | tf_op jit(solution)/shard_map/ppermute | solution.py:391
  50.4 0.9 collective-permute-done.kv_other_ref
  51.3 0.0 collective-permute-done.1.other_ref
  51.3 0.0 copy-start.1
  51.3 0.0 copy-done
  51.3 0.0 copy-start.4
  51.3 2.8 %shard_map.108 = (bf16[4,2,640,128]{3,2,1,0:T(8,128)(2,1)S(1)}, f32[8,128]{1,0:T(8,128)S(1)}) custom-call(bf16[128,256]{1,0:T(8,128)(2,1)S(1)} %get-tuple-element.17.kv_ref, bf16[128,256]{1,0:T(8,128)(2,1)S(1)} %collective-permute-done.kv_other_ref, bf16[2,4,640,128]{3,2,1,0:T(8,128)(2,1)S(1)} %copy-done, ...), custom_call_target="tpu_custom_call" | custom-call | flops 335544320 | bytes 4000000 | tf_op jit(solution)/shard_map/pallas_call | solution.py:421
  54.1 0.0 copy-done.1
  54.1 0.0 copy-start.2
  54.1 1.0 %copy-done.2 = bf16[4,2,640,128]{3,2,1,0:T(8,128)(2,1)} copy-done((bf16[4,2,640,128]{3,2,1,0:T(8,128)(2,1)}, bf16[4,2,640,128]{3,2,1,0:T(8,128)(2,1)S(1)}, u32[]{:S(2)}) %copy-start.2) | copy-done | bytes 1310744
  55.2 5.6 %all-to-all-done.1 = bf16[64,16,128]{2,1,0:T(8,128)(2,1)S(1)} async-done(((bf16[64,16,128]{2,1,0:T(8,128)(2,1)}), bf16[64,16,128]{2,1,0:T(8,128)(2,1)S(1)}, u32[]{:S(2)}, u32[]{:S(2)}) %all-to-all-start.1) | async-done | bytes 262176 | tf_op jit(solution)/shard_map/all_to_all | solution.py:430
  60.8 0.0 copy-done.4
  60.8 0.3 shard_map.109.kv_ref
  61.1 0.0 copy-start.3
  61.1 4.8 %collective-permute-start.2 = (bf16[128,256]{1,0:T(8,128)(2,1)S(1)}, bf16[128,256]{1,0:T(8,128)(2,1)S(1)}, u32[]{:S(2)}, u32[]{:S(2)}) collective-permute-start(bf16[128,256]{1,0:T(8,128)(2,1)S(1)} %shard_map.109.kv_ref), channel_id=1, source_target_pairs={{0,1},{1,0},{2,3},{3,2},{4,5},{5,4},{6,7},{7,6},{8,9},{9,8},{10,11... | collective-permute-start | bytes 196616 | tf_op jit(solution)/shard_map/ppermute | solution.py:391
  66.0 0.9 collective-permute-done.2.kv_other_ref
  66.8 0.0 copy-start.9
  66.8 0.0 copy-done.3
  66.9 0.6 copy-done.9
  67.5 3.4 %shard_map.110 = bf16[4,2,640,128]{3,2,1,0:T(8,128)(2,1)} custom-call(bf16[128,256]{1,0:T(8,128)(2,1)} %copy-done.3, bf16[128,256]{1,0:T(8,128)(2,1)} %copy-done.9, bf16[2,4,640,128]{3,2,1,0:T(8,128)(2,1)} %get-tuple-element.18.own_ref, bf16[2,4,640,128]{3,2,1,0:T(8,128)(2,1)} %copy-done.1, ...), custom_call_target="tpu_custom_call", output_to_operand_aliasing={{}: (4, {})} | custom-call | flops 335544320 | bytes 4000000 | tf_op jit(solution)/shard_map/pallas_call | solution.py:448
  70.9 4.0 %all-to-all-start.2 = ((bf16[4,2,640,128]{3,2,1,0:T(8,128)(2,1)}), bf16[4,2,640,128]{3,2,1,0:T(8,128)(2,1)S(1)}, u32[]{:S(2)}, u32[]{:S(2)}) async-start(bf16[4,2,640,128]{3,2,1,0:T(8,128)(2,1)} %shard_map.110), calls=%async_computation.2 | async-start | bytes 2621440 | tf_op jit(solution)/shard_map/all_to_all | solution.py:459
  74.9 1.0 %shard_map.107 = bf16[256,640]{1,0:T(8,128)(2,1)} custom-call(bf16[1024,128]{1,0:T(8,128)(2,1)S(1)} %bitcast.5, bf16[128,128]{1,0:T(8,128)(2,1)S(1)} %copy-done.4, bf16[256,640]{1,0:T(8,128)(2,1)} %get-tuple-element.16.dq_in_ref), custom_call_target="tpu_custom_call", output_to_operand_aliasing={{}: (2, {})} | custom-call | flops 100000000 | bytes 1000000 | tf_op jit(solution)/shard_map/pallas_call | solution.py:467
  75.9 16.4 %all-to-all-done.2.came_ref = bf16[4,2,640,128]{3,2,1,0:T(8,128)(2,1)S(1)} async-done(((bf16[4,2,640,128]{3,2,1,0:T(8,128)(2,1)}), bf16[4,2,640,128]{3,2,1,0:T(8,128)(2,1)S(1)}, u32[]{:S(2)}, u32[]{:S(2)}) %all-to-all-start.2) | async-done | bytes 1310752 | tf_op jit(solution)/shard_map/all_to_all | solution.py:459
  92.3 1.0 %shard_map.111 = bf16[256,640]{1,0:T(8,128)(2,1)} custom-call(bf16[4,2,640,128]{3,2,1,0:T(8,128)(2,1)S(1)} %all-to-all-done.2.came_ref), custom_call_target="tpu_custom_call" | custom-call | flops 1000000 | bytes 1000000 | tf_op jit(solution)/shard_map/pallas_call | solution.py:483
Async XLA Ops:
  3.1 31.8 %all-to-all-start = ((bf16[64,24,128]{2,1,0:T(8,128)(2,1)}), bf16[64,24,128]{2,1,0:T(8,128)(2,1)S(1)}, u32[]{:S(2)}, u32[]{:S(2)}) async-start(bf16[64,24,128]{2,1,0:T(8,128)(2,1)} %bitcast.7), calls=%async_computation | async-start | bytes 786432 | tf_op jit(solution)/shard_map/all_to_all | solution.py:351
  20.3 14.7 %copy-start.5 = (bf16[256,128]{1,0:T(8,128)(2,1)S(1)}, bf16[256,128]{1,0:T(8,128)(2,1)}, u32[]{:S(2)}) copy-start(bf16[256,128]{1,0:T(8,128)(2,1)} %k_in.3) | copy-start | bytes 196612
  20.3 14.7 %copy-start.6 = (bf16[256,128]{1,0:T(8,128)(2,1)S(1)}, bf16[256,128]{1,0:T(8,128)(2,1)}, u32[]{:S(2)}) copy-start(bf16[256,128]{1,0:T(8,128)(2,1)} %v_in.3) | copy-start | bytes 196612
  27.0 24.3 %collective-permute-start.1 = (bf16[2,4,640,128]{3,2,1,0:T(8,128)(2,1)}, bf16[2,4,640,128]{3,2,1,0:T(8,128)(2,1)S(1)}, u32[]{:S(2)}, u32[]{:S(2)}) collective-permute-start(bf16[2,4,640,128]{3,2,1,0:T(8,128)(2,1)} %get-tuple-element.19), channel_id=1, source_target_pairs={{0,1},{1,0},{2,3},{3,2},{4,5},{5,4},{6,7},{7,6},{8,9},{9,8},{10,11... | collective-permute-start | bytes 3932168 | tf_op jit(solution)/shard_map/ppermute | solution.py:391
  34.9 0.9 copy-start.7
  35.8 0.9 copy-start.8
  36.7 14.6 %copy-start = (bf16[2,4,640,128]{3,2,1,0:T(8,128)(2,1)S(1)}, bf16[2,4,640,128]{3,2,1,0:T(8,128)(2,1)}, u32[]{:S(2)}) copy-start(bf16[2,4,640,128]{3,2,1,0:T(8,128)(2,1)} %get-tuple-element.18.own_ref) | copy-start | bytes 3932164
  40.4 20.4 %all-to-all-start.1 = ((bf16[64,16,128]{2,1,0:T(8,128)(2,1)}), bf16[64,16,128]{2,1,0:T(8,128)(2,1)S(1)}, u32[]{:S(2)}, u32[]{:S(2)}) async-start(bf16[64,16,128]{2,1,0:T(8,128)(2,1)} %bitcast.2), calls=%async_computation.1 | async-start | bytes 524288 | tf_op jit(solution)/shard_map/all_to_all | solution.py:430
  47.8 3.5 %collective-permute-start = (bf16[128,256]{1,0:T(8,128)(2,1)S(1)}, bf16[128,256]{1,0:T(8,128)(2,1)S(1)}, u32[]{:S(2)}, u32[]{:S(2)}) collective-permute-start(bf16[128,256]{1,0:T(8,128)(2,1)S(1)} %get-tuple-element.17.kv_ref), channel_id=1, source_target_pairs={{0,1},{1,0},{2,3},{3,2},{4,5},{5,4},{6,7},{7,6},{8,9},{9,8},{10,11... | collective-permute-start | bytes 196616 | tf_op jit(solution)/shard_map/ppermute | solution.py:391
  51.3 2.8 %copy-start.1 = (bf16[2,4,640,128]{3,2,1,0:T(8,128)(2,1)}, bf16[2,4,640,128]{3,2,1,0:T(8,128)(2,1)S(1)}, u32[]{:S(2)}) copy-start(bf16[2,4,640,128]{3,2,1,0:T(8,128)(2,1)S(1)} %collective-permute-done.1.other_ref) | copy-start | bytes 3932164
  51.3 9.5 %copy-start.4 = (bf16[128,128]{1,0:T(8,128)(2,1)S(1)}, bf16[128,128]{1,0:T(8,128)(2,1)}, u32[]{:S(2)}) copy-start(bf16[128,128]{1,0:T(8,128)(2,1)} %get-tuple-element.15.selector_ref) | copy-start | bytes 98308
  54.1 1.1 %copy-start.2 = (bf16[4,2,640,128]{3,2,1,0:T(8,128)(2,1)}, bf16[4,2,640,128]{3,2,1,0:T(8,128)(2,1)S(1)}, u32[]{:S(2)}) copy-start(bf16[4,2,640,128]{3,2,1,0:T(8,128)(2,1)S(1)} %get-tuple-element.21.parts_ref) | copy-start | bytes 3932164
  61.1 5.7 %copy-start.3 = (bf16[128,256]{1,0:T(8,128)(2,1)}, bf16[128,256]{1,0:T(8,128)(2,1)S(1)}, u32[]{:S(2)}) copy-start(bf16[128,256]{1,0:T(8,128)(2,1)S(1)} %shard_map.109.kv_ref) | copy-start | bytes 196612
  61.1 5.7 %collective-permute-start.2 = (bf16[128,256]{1,0:T(8,128)(2,1)S(1)}, bf16[128,256]{1,0:T(8,128)(2,1)S(1)}, u32[]{:S(2)}, u32[]{:S(2)}) collective-permute-start(bf16[128,256]{1,0:T(8,128)(2,1)S(1)} %shard_map.109.kv_ref), channel_id=1, source_target_pairs={{0,1},{1,0},{2,3},{3,2},{4,5},{5,4},{6,7},{7,6},{8,9},{9,8},{10,11... | collective-permute-start | bytes 196616 | tf_op jit(solution)/shard_map/ppermute | solution.py:391
  66.8 0.6 copy-start.9
  70.9 21.4 %all-to-all-start.2 = ((bf16[4,2,640,128]{3,2,1,0:T(8,128)(2,1)}), bf16[4,2,640,128]{3,2,1,0:T(8,128)(2,1)S(1)}, u32[]{:S(2)}, u32[]{:S(2)}) async-start(bf16[4,2,640,128]{3,2,1,0:T(8,128)(2,1)} %shard_map.110), calls=%async_computation.2 | async-start | bytes 2621440 | tf_op jit(solution)/shard_map/all_to_all | solution.py:459

commit v3 on v2

v3 whole, which is shorter than its diff:
```python
import functools
import math

import jax
import jax.numpy as jnp
from jax import lax
from jax.experimental import pallas as pl
from jax.experimental.pallas import tpu as pltpu
from jax.sharding import PartitionSpec as P

GROUP = 5
TRUNK = 128
LEAF = 2
HEAD = 128
OUT_TILES = 2 * GROUP + 2
OUT_ROWS = OUT_TILES * LEAF
BACK_TILES = GROUP + 2
BACK_ROWS = 16
VERY_NEGATIVE = -1e30
SCALE = 1.0 / math.sqrt(HEAD)

f32 = jnp.float32
bf16 = jnp.bfloat16
vmem = pl.BlockSpec(memory_space=pltpu.VMEM)
smem = pl.BlockSpec(memory_space=pltpu.SMEM)
hbm = pl.BlockSpec(memory_space=pltpu.HBM)


def dot(a, b, contract):
    return lax.dot_general(a, b, ((contract[0:1], contract[1:2]), ((), ())), preferred_element_type=f32)


def leaf_selector(leaf_tree_ref, seg):
    count = leaf_tree_ref.shape[0]
    tree_row = leaf_tree_ref[pl.ds(seg, 1), :].astype(f32).astype(bf16)
    tree_rows = jnp.broadcast_to(tree_row, (16, count))
    leaf = lax.broadcasted_iota(jnp.int32, (count, LEAF * count), 0)
    col = lax.broadcasted_iota(jnp.int32, (count, LEAF * count), 1)
    repeat = (leaf == (col >> 1)).astype(f32).astype(bf16)
    tree_of_col = dot(tree_rows, repeat, (1, 0))[0:1, :].astype(jnp.int32)
    row = lax.broadcasted_iota(jnp.int32, (LEAF * count, LEAF * count), 0)
    col = lax.broadcasted_iota(jnp.int32, (LEAF * count, LEAF * count), 1)
    row_pos = (row >= count).astype(jnp.int32)
    hit = (tree_of_col == row - row_pos * count) & (row_pos == (col & 1))
    return hit.astype(f32).astype(bf16)


def copies(pairs, sems):
    started = [pltpu.make_async_copy(src, dst, sems.at[i]) for i, (src, dst) in enumerate(pairs)]
    for copy in started:
        copy.start()
    return started


def send_kernel(
    q_ref, g_ref, k_ref, v_ref, leaf_tree_ref,
    out_ref, tree_ref, q_buf, g_buf, k_buf, v_buf, rows_ref, out_buf, sems, out_sems,
):
    count = tree_ref.shape[0]
    leaves = pl.ds(TRUNK, LEAF * count)
    loads = [(leaf_tree_ref, tree_ref)]
    loads += [(src.at[leaves, :], dst) for src, dst in zip((q_ref, g_ref, k_ref, v_ref), (q_buf, g_buf, k_buf, v_buf))]
    loads = copies(loads, sems)
    seg = lax.axis_index("seg")
    loads[0].wait()
    selector = leaf_selector(tree_ref, seg)
    half = count // 2
    stores = []
    for part in range(2):
        at = part * half
        chosen = jnp.concatenate([selector[a * count + at : a * count + at + half, :] for a in range(LEAF)], axis=0)
        tile = 0
        for load, ref in zip(loads[1:], (q_buf, g_buf, k_buf, v_buf)):
            if part == 0:
                load.wait()
            moved = dot(chosen, ref[...], (1, 0))
            for column in range(0, ref.shape[1], HEAD):
                for a in range(LEAF):
                    rows_ref[pl.ds(at * OUT_ROWS + tile * LEAF + a, half, OUT_ROWS), :] = moved[
                        a * half : (a + 1) * half, column : column + HEAD
                    ]
                tile += 1
        rows = pl.ds(at * OUT_ROWS, half * OUT_ROWS)
        out_buf[rows, :] = rows_ref[rows, :].astype(bf16)
        stores.append(pltpu.make_async_copy(out_buf.at[rows, :], out_ref.at[rows, :], out_sems.at[part]))
        stores[-1].start()
    for store in stores:
        store.wait()


def softmax_grads(scores, prob_grad, visible):
    masked = jnp.where(visible, scores, VERY_NEGATIVE)
    row_max = jnp.max(masked, axis=-1, keepdims=True)
    weights = jnp.where(visible, jnp.exp(masked - row_max), 0.0)
    row_total = jnp.maximum(jnp.sum(weights, axis=-1, keepdims=True), 1.0)
    probability = weights * (1.0 / row_total)
    row_delta = jnp.sum(probability * prob_grad, axis=-1, keepdims=True)
    score_grad = (probability * (prob_grad - row_delta)).astype(bf16)
    return probability.astype(bf16), score_grad


def leaf_visible(leaf_tree_ref, leaf_len_ref, trunk_len, seg):
    count = leaf_tree_ref.shape[0]
    in_len = jnp.sum(jnp.where(leaf_tree_ref[...] == seg, leaf_len_ref[...], 0), axis=1, keepdims=True)
    row_len = jnp.concatenate([in_len] * LEAF, axis=0)
    leaf_rows = LEAF * count
    shape = (leaf_rows, TRUNK + leaf_rows)
    row = lax.broadcasted_iota(jnp.int32, shape, 0)
    col = lax.broadcasted_iota(jnp.int32, shape, 1)
    row_pos = (row >= count).astype(jnp.int32)
    leaf_col = col - TRUNK
    col_pos = (leaf_col >= count).astype(jnp.int32)
    own = (row - row_pos * count == leaf_col - col_pos * count) & (col_pos <= row_pos)
    visible = ((col < trunk_len) & (col < TRUNK)) | ((col >= TRUNK) & own)
    return visible & (row_pos < row_len)


def trunk_kernel(
    q_in, g_in, k_in, v_in, trunk_len_in, w_key_ref, w_value_ref,
    dq_ref, dkv_ref, own_ref, give_ref,
    q_ref, g_ref, k_ref, v_ref, trunk_len_ref, dq_buf, dkv_buf, give_buf, sems, out_sems, weight_sems,
):
    trunk = pl.ds(0, TRUNK)
    core = lax.axis_index("kvh") & 1
    chips, block = own_ref.shape[1:3]
    pairs = []
    for chip in range(chips):
        for ref, which in ((give_buf, 1 - core), (own_ref, core)):
            rows = pl.ds(pl.multiple_of((2 * chip + which) * block, block), block)
            pairs += [(w.at[rows, :], ref.at[part, chip]) for part, w in enumerate((w_key_ref, w_value_ref))]
    loads = copies(
        [
            (trunk_len_in, trunk_len_ref),
            (k_in.at[trunk, :], k_ref),
            (v_in.at[trunk, :], v_ref),
            (q_in.at[trunk, :], q_ref),
            (g_in.at[trunk, :], g_ref),
        ],
        sems,
    )
    weight_loads = copies(pairs, weight_sems)
    for load in loads:
        load.wait()
    seg = lax.axis_index("seg")
    trunk_len = trunk_len_ref[seg]
    keys = k_ref[...]
    values = v_ref[...]
    row = lax.broadcasted_iota(jnp.int32, (TRUNK, TRUNK), 0)
    col = lax.broadcasted_iota(jnp.int32, (TRUNK, TRUNK), 1)
    visible = (col <= row) & (row < trunk_len)
    for g in range(GROUP):
        head_q = q_ref[:, g * HEAD : (g + 1) * HEAD]
        head_g = g_ref[:, g * HEAD : (g + 1) * HEAD]
        scores = dot(head_q, keys, (1, 1)) * SCALE
        prob_grad = dot(head_g, values, (1, 1))
        probability, score_grad = softmax_grads(scores, prob_grad, visible)
        dq_buf[:, g * HEAD : (g + 1) * HEAD] = (dot(score_grad, keys, (1, 0)) * SCALE).astype(bf16)
        head_dk = dot(score_grad, head_q, (0, 0))
        head_dv = dot(probability, head_g, (0, 0))
        if g == 0:
            dkv_buf[:, 0:HEAD] = head_dk
            dkv_buf[:, HEAD:] = head_dv
        else:
            dkv_buf[:, 0:HEAD] += head_dk
            dkv_buf[:, HEAD:] += head_dv
    dkv_buf[:, 0:HEAD] *= SCALE
    for load in weight_loads:
        load.wait()
    stores = copies(
        [
            (dq_buf, dq_ref.at[trunk, :]),
            (dkv_buf, dkv_ref),
            (give_buf, give_ref),
        ],
        out_sems,
    )
    for store in stores:
        store.wait()


def leaf_kernel(
    in_ref, k_ref, v_ref, leaf_tree_ref, leaf_len_ref, trunk_len_in,
    out_ref, dkv_ref, rows_ref, back_ref, q_buf, g_buf, ds_buf, p_buf, out_buf, trunk_len_ref, sem, out_sem,
):
    load = pltpu.make_async_copy(trunk_len_in, trunk_len_ref, sem)
    load.start()
    count = leaf_tree_ref.shape[0]
    leaf_rows = LEAF * count
    rows_ref[...] = in_ref[...].astype(f32)

    def gather(tile):
        parts = [rows_ref[pl.ds(tile * LEAF + a, count, OUT_ROWS), :] for a in range(LEAF)]
        return jnp.concatenate(parts, axis=0).astype(bf16)

    keys = jnp.concatenate([k_ref[0:TRUNK, :], gather(2 * GROUP)], axis=0)
    values = jnp.concatenate([v_ref[0:TRUNK, :], gather(2 * GROUP + 1)], axis=0)
    seg = lax.axis_index("seg")
    load.wait()
    visible = leaf_visible(leaf_tree_ref, leaf_len_ref, trunk_len_ref[seg], seg)
    for g in range(GROUP):
        rows = slice(g * leaf_rows, (g + 1) * leaf_rows)
        head_q = gather(g)
        head_g = gather(GROUP + g)
        q_buf[rows, :] = head_q
        g_buf[rows, :] = head_g
        scores = dot(head_q, keys, (1, 1)) * SCALE
        prob_grad = dot(head_g, values, (1, 1))
        p_buf[rows, :], ds_buf[rows, :] = softmax_grads(scores, prob_grad, visible)
    query_grad = dot(ds_buf[...], keys, (1, 0)) * SCALE
    for g in range(GROUP):
        for a in range(LEAF):
            at = g * leaf_rows + a * count
            back_ref[pl.ds(g * LEAF + a, count, BACK_ROWS), :] = query_grad[at : at + count, :]
    key_grad = dot(ds_buf[...], q_buf[...], (0, 0)) * SCALE
    value_grad = dot(p_buf[...], g_buf[...], (0, 0))
    for a in range(LEAF):
        at = TRUNK + a * count
        back_ref[pl.ds(GROUP * LEAF + a, count, BACK_ROWS), :] = key_grad[at : at + count, :]
        back_ref[pl.ds((GROUP + 1) * LEAF + a, count, BACK_ROWS), :] = value_grad[at : at + count, :]
    leaf = lax.broadcasted_iota(jnp.int32, (count, count), 1)
    number = jnp.sum(jnp.where(leaf_tree_ref[...] == seg, leaf, 0), axis=1, keepdims=True).astype(f32)
    for spare in range(BACK_TILES * LEAF, BACK_ROWS):
        back_ref[pl.ds(spare, count, BACK_ROWS), :] = jnp.broadcast_to(number, (count, HEAD))
    out_buf[...] = back_ref[...].astype(bf16)
    store = pltpu.make_async_copy(out_buf, out_ref, out_sem)
    store.start()
    dkv_ref[:, 0:HEAD] = key_grad[0:TRUNK, :]
    dkv_ref[:, HEAD:] = value_grad[0:TRUNK, :]
    store.wait()


def back_selector(rows_ref):
    count = rows_ref.shape[0] // BACK_ROWS
    number = rows_ref[pl.ds(BACK_TILES * LEAF, count, BACK_ROWS), :].astype(jnp.int32)
    col = lax.broadcasted_iota(jnp.int32, number.shape, 1)
    hits = [((number == (col >> 1)) & ((col & 1) == a)).astype(f32) for a in range(LEAF)]
    return jnp.concatenate(hits, axis=0)[:, 0 : LEAF * count].astype(bf16)


def moved_tile(rows_ref, selector, tile):
    count = rows_ref.shape[0] // BACK_ROWS
    parts = [rows_ref[pl.ds(tile * LEAF + a, count, BACK_ROWS), :] for a in range(LEAF)]
    return dot(selector, jnp.concatenate(parts, axis=0).astype(bf16), (0, 0)).astype(bf16)


def leaf_kv_kernel(in_ref, after_ref, out_ref, rows_ref):
    rows_ref[...] = in_ref[...].astype(f32)
    selector = back_selector(rows_ref)
    for part in range(2):
        out_ref[:, part * HEAD : (part + 1) * HEAD] = moved_tile(rows_ref, selector, GROUP + part)


def leaf_query_kernel(in_ref, dq_in_ref, dq_ref, token_ref, rows_ref, dq_buf, sem):
    rows_ref[...] = in_ref[...].astype(f32)
    selector = back_selector(rows_ref)
    for tile in range(GROUP):
        dq_buf[:, tile * HEAD : (tile + 1) * HEAD] = moved_tile(rows_ref, selector, tile)
    store = pltpu.make_async_copy(dq_buf, dq_ref.at[pl.ds(TRUNK, dq_buf.shape[0]), :], sem)
    store.start()
    token_ref[...] = jnp.zeros(token_ref.shape, f32)
    store.wait()


def chip_part(kv_ref, kv_other_ref, own_ref, other_ref, block):
    kv = jnp.concatenate([kv_ref[...], kv_other_ref[...]], axis=1)
    weight = jnp.concatenate([ref[part, block] for ref in (own_ref, other_ref) for part in range(2)], axis=1)
    return dot(weight, kv, (1, 1)).astype(bf16)


def trunk_part_kernel(kv_ref, kv_other_ref, own_ref, other_ref, *refs):
    chips = own_ref.shape[1]
    outs, token_ref, buf, sems = refs[:chips], refs[chips], refs[-2], refs[-1]
    chip = lax.axis_index("kvh") >> 1
    stores = []
    for step in reversed(range(chips)):
        buf[step] = chip_part(kv_ref, kv_other_ref, own_ref, other_ref, lax.rem(chip + step, chips))
        stores.append(pltpu.make_async_copy(buf.at[step], outs[step], sems.at[step]))
        stores[-1].start()
    token_ref[...] = jnp.zeros(token_ref.shape, f32)
    for store in stores:
        store.wait()


def leaf_part_kernel(kv_ref, kv_other_ref, own_ref, other_ref, after_ref, *refs):
    out_ref = refs[-1]
    for block in range(out_ref.shape[0]):
        out_ref[block] = chip_part(kv_ref, kv_other_ref, own_ref, other_ref, block)


def hidden_kernel(leaf_ref, *refs):
    trunk_refs, (out_ref, buf, sems) = refs[:-3], refs[-3:]
    stores = []
    for i, parts in enumerate(([ref[...] for ref in trunk_refs], [leaf_ref[chip] for chip in range(leaf_ref.shape[0])])):
        total = parts[0].astype(f32)
        for part in parts[1:]:
            total += part.astype(f32)
        rows = pl.ds(i * TRUNK, TRUNK)
        buf[rows, :] = total.T.astype(bf16)
        stores.append(pltpu.make_async_copy(buf.at[rows, :], out_ref.at[rows, :], sems.at[i]))
        stores[-1].start()
    for store in stores:
        store.wait()


def call(kernel, outs, in_specs, out_specs, scratch=(), flops=0, moved=0, aliases={}, limit=24):
    return pl.pallas_call(
        kernel,
        out_shape=outs,
        in_specs=in_specs,
        out_specs=out_specs,
        scratch_shapes=list(scratch),
        input_output_aliases=aliases,
        compiler_params=pltpu.CompilerParams(vmem_limit_bytes=limit * 1024 * 1024),
        cost_estimate=pl.CostEstimate(flops=flops, bytes_accessed=moved, transcendentals=0),
    )


def shards(queries, key_rows, value_rows, grad_out, w_key, w_value, trunk_len, leaf_len, leaf_tree):
    count = lax.axis_size("seg")
    heads = lax.axis_size("kvh")
    chips = heads // 2
    leaf_rows = LEAF * count
    row_width = queries.shape[1]
    hidden = w_key.shape[0]
    columns = hidden // heads
    out = jax.ShapeDtypeStruct
    dma = pltpu.SemaphoreType.DMA

    vm = pltpu.VMEM

    send = call(
        send_kernel,
        out((count * OUT_ROWS, HEAD), bf16),
        [hbm] * 5,
        hbm,
        [
            vm((count, count), jnp.int32),
            vm((leaf_rows, row_width), bf16),
            vm((leaf_rows, row_width), bf16),
            vm((leaf_rows, HEAD), bf16),
            vm((leaf_rows, HEAD), bf16),
            vm((count * OUT_ROWS, HEAD), f32),
            vm((count * OUT_ROWS, HEAD), bf16),
            dma((5,)),
            dma((2,)),
        ],
        flops=10**8,
        moved=10**6,
        limit=60,
    )(queries, grad_out, key_rows, value_rows, leaf_tree)
    got = lax.all_to_all(
        send.reshape(count, OUT_ROWS, HEAD), "seg", split_axis=0, concat_axis=0, tiled=True
    ).reshape(count * OUT_ROWS, HEAD)

    keys_all = TRUNK + leaf_rows
    dq, trunk_dkv, own, give = call(
        trunk_kernel,
        [
            out(queries.shape, bf16),
            out((TRUNK, 2 * HEAD), f32),
            out((2, chips, columns, HEAD), bf16),
            out((2, chips, columns, HEAD), bf16),
        ],
        [hbm] * 7,
        [hbm] * 2 + [vmem, hbm],
        [
            vm((TRUNK, row_width), bf16),
            vm((TRUNK, row_width), bf16),
            vm((TRUNK, HEAD), bf16),
            vm((TRUNK, HEAD), bf16),
            pltpu.SMEM((count,), jnp.int32),
            vm((TRUNK, row_width), bf16),
            vm((TRUNK, 2 * HEAD), f32),
            vm((2, chips, columns, HEAD), bf16),
            dma((5,)),
            dma((3,)),
            dma((4 * chips,)),
        ],
        flops=4 * 10**10,
        moved=10**7,
        limit=60,
    )(queries, grad_out, key_rows, value_rows, trunk_len, w_key, w_value)

    def swap(value):
        return lax.ppermute(value, "kvh", [(i, i ^ 1) for i in range(heads)])

    other = swap(give)

    back, leaf_dkv = call(
        leaf_kernel,
        [out((count * BACK_ROWS, HEAD), bf16), out((TRUNK, 2 * HEAD), f32)],
        [vmem] * 5 + [hbm],
        [hbm, vmem],
        [
            vm((count * OUT_ROWS, HEAD), f32),
            vm((count * BACK_ROWS, HEAD), f32),
            vm((GROUP * leaf_rows, HEAD), bf16),
            vm((GROUP * leaf_rows, HEAD), bf16),
            vm((GROUP * leaf_rows, keys_all), bf16),
            vm((GROUP * leaf_rows, keys_all), bf16),
            vm((count * BACK_ROWS, HEAD), bf16),
            pltpu.SMEM((count,), jnp.int32),
            dma,
            dma,
        ],
        flops=4 * 10**10,
        moved=10**6,
    )(got, key_rows, value_rows, leaf_tree, leaf_len, trunk_len)
    trunk_kv = (trunk_dkv + leaf_dkv).astype(bf16)

    part_flops = 2 * TRUNK * 4 * HEAD * chips * columns
    part_shape = (columns, TRUNK)
    *trunk_parts, token = call(
        trunk_part_kernel,
        [out(part_shape, bf16)] * chips + [out((8, HEAD), f32)],
        [vmem] * 4,
        [hbm] * chips + [vmem],
        [vm((chips,) + part_shape, bf16), dma((chips,))],
        flops=part_flops,
        moved=4 * 10**6,
    )(trunk_kv, swap(trunk_kv), own, other)
    trunk_came = [trunk_parts[0]]
    for step in (2, 1, 3):
        route = [(2 * x + c, 2 * ((x + step) % chips) + c) for x in range(chips) for c in range(2)]
        trunk_came.append(lax.ppermute(trunk_parts[step], "kvh", route))
    back = lax.all_to_all(
        back.reshape(count, BACK_ROWS, HEAD), "seg", split_axis=0, concat_axis=0, tiled=True
    ).reshape(count * BACK_ROWS, HEAD)
    leaf_kv = call(
        leaf_kv_kernel,
        out((leaf_rows, 2 * HEAD), bf16),
        [vmem] * 2,
        vmem,
        [vm((count * BACK_ROWS, HEAD), f32)],
        flops=4 * 10**10,
        moved=10**6,
    )(back, token)
    grad_query, token = call(
        leaf_query_kernel,
        [out(queries.shape, bf16), out((8, HEAD), f32)],
        [vmem, hbm],
        [hbm, vmem],
        [vm((count * BACK_ROWS, HEAD), f32), vm((leaf_rows, row_width), bf16), dma],
        flops=10**8,
        moved=10**6,
        aliases={1: 0},
    )(back, dq)
    parts = call(
        leaf_part_kernel,
        out((chips, columns, leaf_rows), bf16),
        [vmem] * 5 + [hbm] * (chips - 1),
        vmem,
        flops=4 * 10**10,
        moved=4 * 10**6,
    )(leaf_kv, swap(leaf_kv), own, other, token, *trunk_came[1:])
    came = lax.all_to_all(
        parts,
        "kvh",
        split_axis=0,
        concat_axis=0,
        tiled=True,
        axis_index_groups=[[2 * x + c for x in range(chips)] for c in range(2)],
    )
    grad_hidden = call(
        hidden_kernel,
        out((TRUNK + leaf_rows, columns), bf16),
        [vmem] * (1 + chips),
        hbm,
        [vm((TRUNK + leaf_rows, columns), bf16), dma((2,))],
        flops=10**6,
        moved=10**6,
    )(came, *trunk_came)
    return (grad_query, grad_hidden)


def solution(mesh):
    in_specs = (
        P("seg", "kvh"),
        P("seg", "kvh"),
        P("seg", "kvh"),
        P("seg", "kvh"),
        P(None, "kvh"),
        P(None, "kvh"),
        P(),
        P(),
        P(),
    )
    out_specs = (P("seg", "kvh"), P("seg", "kvh"))
    return jax.shard_map(shards, mesh=mesh, in_specs=in_specs, out_specs=out_specs, check_vma=False)
```

time: 93.7 us -> 81 us (0.86)
  the two profiles are of different devices: /device:TPU:1 before, /device:TPU:8 now
where the time goes in v3:
time: 81 us; the launch traced here: 80.5 us
  starting transfers between devices  39.8 us (49%)
  Pallas kernels  16.1 us (20%)
  blocking collectives  14.4 us (18%)
  waiting for transfers between devices  9.24 us (11%)
  between operations  0.84 us (1%)
    all_to_all x1, starting transfers between devices, shards(): lax.all_to_all(send.reshape(count, OUT_ROWS, HEAD), 'seg', split_axis=0,...  16.6 us
    all_to_all x1, blocking collectives, shards(): lax.all_to_all(parts, 'kvh', split_axis=0, concat_axis=0, tiled=True, axi...  14.4 us
    ppermute x3, starting transfers between devices, shards(): trunk_came.append(lax.ppermute(trunk_parts[step], 'kvh', route))  12 us
    all_to_all x1, waiting for transfers between devices, shards(): lax.all_to_all(send.reshape(count, OUT_ROWS, HEAD), 'seg', split_axis=0,...  7.63 us
    pallas_call x1, Pallas kernels, shards(): call(trunk_kernel, [out(queries.shape, bf16), out((TRUNK, 2 * HEAD), f32)...  6.67 us
    ppermute x3, starting transfers between devices, swap(): return lax.ppermute(value, 'kvh', [(i, i ^ 1) for i in range(heads)])  5.76 us
    all_to_all x1, starting transfers between devices, shards(): lax.all_to_all(back.reshape(count, BACK_ROWS, HEAD), 'seg', split_axis=0,...  5.51 us
    pallas_call x1, Pallas kernels, shards(): call(leaf_kernel, [out((count * BACK_ROWS, HEAD), bf16), out((TRUNK, 2 *...  2.53 us
  transfers between devices with their start and end apart: 8, of which 4 were waited for; matrix products, arithmetic and copies ran while one was open for 0% of the time, Pallas kernels for 15%

profile of v3, /device:TPU:8, one launch (start us, length us, event | category | flops | bytes accessed | tf_op | source)
XLA Modules:
  0.0 80.5 jit_solution(1739588513804873159)
XLA Ops:
  0.6 2.4 %shard_map.104 = bf16[1536,128]{1,0:T(8,128)(2,1)} custom-call(bf16[256,640]{1,0:T(8,128)(2,1)} %q_in.1, bf16[256,640]{1,0:T(8,128)(2,1)} %g_in.1, bf16[256,128]{1,0:T(8,128)(2,1)} %k_in.1, bf16[256,128]{1,0:T(8,128)(2,1)} %v_in.1, s32[64,64]{1,0:T(8,128)} %leaf_tree_ref.3), custom_call_target="tpu_custom_call" | custom-call | flops 100000000 | bytes 1000000 | tf_op jit(solution)/shard_map/pallas_call | solution.py:331
  3.1 16.6 %all-to-all-start = ((bf16[64,24,128]{2,1,0:T(8,128)(2,1)}), bf16[64,24,128]{2,1,0:T(8,128)(2,1)S(1)}, u32[]{:S(2)}, u32[]{:S(2)}) async-start(bf16[64,24,128]{2,1,0:T(8,128)(2,1)} %bitcast.7), calls=%async_computation | async-start | bytes 786432 | tf_op jit(solution)/shard_map/all_to_all | solution.py:351
  19.7 0.0 copy-start.1
  19.7 0.0 copy-start.2
  19.7 0.0 copy-start.3
  19.7 0.0 copy-start.4
  19.7 0.0 copy-start.5
  19.7 6.7 %shard_map.106 = (bf16[256,640]{1,0:T(8,128)(2,1)}, f32[128,256]{1,0:T(8,128)}, bf16[2,4,640,128]{3,2,1,0:T(8,128)(2,1)}, bf16[2,4,640,128]{3,2,1,0:T(8,128)(2,1)}) custom-call(bf16[256,640]{1,0:T(8,128)(2,1)} %q_in.1, bf16[256,640]{1,0:T(8,128)(2,1)} %g_in.1, bf16[256,128]{1,0:T(8,128)(2,1)} %k_in.1, bf16[256,128]{1,0:T(8,128)(2,1)} %v_in.1, ...), custom_call_target="tpu_custom_call" | custom-call | flops 40000000000 | bytes 10000000 | tf_op jit(solution)/shard_map/pallas_call | solution.py:356
  26.4 1.9 %collective-permute-start.1 = (bf16[2,4,640,128]{3,2,1,0:T(8,128)(2,1)}, bf16[2,4,640,128]{3,2,1,0:T(8,128)(2,1)S(1)}, u32[]{:S(2)}, u32[]{:S(2)}) collective-permute-start(bf16[2,4,640,128]{3,2,1,0:T(8,128)(2,1)} %get-tuple-element.21), channel_id=1, source_target_pairs={{0,1},{1,0},{2,3},{3,2},{4,5},{5,4},{6,7},{7,6},{8,9},{9,8},{10,11... | collective-permute-start | bytes 3932168 | tf_op jit(solution)/shard_map/ppermute | solution.py:385
  28.3 7.6 %all-to-all-done = bf16[64,24,128]{2,1,0:T(8,128)(2,1)S(1)} async-done(((bf16[64,24,128]{2,1,0:T(8,128)(2,1)}), bf16[64,24,128]{2,1,0:T(8,128)(2,1)S(1)}, u32[]{:S(2)}, u32[]{:S(2)}) %all-to-all-start) | async-done | bytes 393248 | tf_op jit(solution)/shard_map/all_to_all | solution.py:351
  36.0 0.0 copy-done.1
  36.0 0.0 copy-done.2
  36.0 0.0 copy-done.3
  36.0 0.0 copy-done.4
  36.0 0.0 copy-done.5
  36.0 0.0 copy-start.6
  36.0 0.0 copy-start
  36.0 2.5 %shard_map.105 = (bf16[1024,128]{1,0:T(8,128)(2,1)}, f32[128,256]{1,0:T(8,128)S(1)}) custom-call(bf16[1536,128]{1,0:T(8,128)(2,1)S(1)} %bitcast.6, bf16[256,128]{1,0:T(8,128)(2,1)S(1)} %copy-done.1, bf16[256,128]{1,0:T(8,128)(2,1)S(1)} %copy-done.2, s32[64,64]{1,0:T(8,128)S(1)} %copy-done.3, s32[64,64]{1,0:T(8,128)S(1)} %copy-done.4, s32[64]{0:T(128)S(1)} %copy-done.5), custom_call_target="tpu_custom_call" | custom-call | flops 40000000000 | bytes 1000000 | tf_op jit(solution)/shard_map/pallas_call | solution.py:389
  38.5 5.5 %all-to-all-start.1 = ((bf16[64,16,128]{2,1,0:T(8,128)(2,1)}), bf16[64,16,128]{2,1,0:T(8,128)(2,1)S(1)}, u32[]{:S(2)}, u32[]{:S(2)}) async-start(bf16[64,16,128]{2,1,0:T(8,128)(2,1)} %bitcast.2), calls=%async_computation.1 | async-start | bytes 524288 | tf_op jit(solution)/shard_map/all_to_all | solution.py:426
  44.1 0.0 copy-done.6
  44.1 1.9 %collective-permute-start = (bf16[128,256]{1,0:T(8,128)(2,1)S(1)}, bf16[128,256]{1,0:T(8,128)(2,1)S(1)}, u32[]{:S(2)}, u32[]{:S(2)}) collective-permute-start(bf16[128,256]{1,0:T(8,128)(2,1)S(1)} %add_convert_fusion.kv_ref), channel_id=1, source_target_pairs={{0,1},{1,0},{2,3},{3,2},{4,5},{5,4},{6,7},{7,6},{8,9},{9,8},{10,11... | collective-permute-start | bytes 196616 | tf_op jit(solution)/shard_map/ppermute | solution.py:385
  46.0 1.2 %collective-permute-done.kv_other_ref = bf16[128,256]{1,0:T(8,128)(2,1)S(1)} collective-permute-done((bf16[128,256]{1,0:T(8,128)(2,1)S(1)}, bf16[128,256]{1,0:T(8,128)(2,1)S(1)}, u32[]{:S(2)}, u32[]{:S(2)}) %collective-permute-start) | collective-permute-done | bytes 65568 | tf_op jit(solution)/shard_map/ppermute | solution.py:385
  47.2 0.0 collective-permute-done.1.other_ref
  47.3 0.0 copy-done
  47.3 1.5 %shard_map.108 = (bf16[640,128]{1,0:T(8,128)(2,1)S(1)}, bf16[640,128]{1,0:T(8,128)(2,1)}, bf16[640,128]{1,0:T(8,128)(2,1)}, bf16[640,128]{1,0:T(8,128)(2,1)}, f32[8,128]{1,0:T(8,128)S(1)}) custom-call(bf16[128,256]{1,0:T(8,128)(2,1)S(1)} %add_convert_fusion.kv_ref, bf16[128,256]{1,0:T(8,128)(2,1)S(1)} %collective-permute-done.kv_other_ref, ...), custom_call_target="tpu_custom_call" | custom-call | flops 335544320 | bytes 4000000 | tf_op jit(solution)/shard_map/pallas_call | solution.py:413
  48.8 4.9 %collective-permute-start.3 = (bf16[640,128]{1,0:T(8,128)(2,1)}, bf16[640,128]{1,0:T(8,128)(2,1)S(1)}, u32[]{:S(2)}, u32[]{:S(2)}) collective-permute-start(bf16[640,128]{1,0:T(8,128)(2,1)} %get-tuple-element.24), channel_id=1, source_target_pairs={{0,4},{1,5},{2,6},{3,7},{4,0},{5,1},{6,2},{7,3},{8,12},{9,13},{10,... | collective-permute-start | bytes 491528 | tf_op jit(solution)/shard_map/ppermute | solution.py:425
  53.7 2.5 %collective-permute-start.4 = (bf16[640,128]{1,0:T(8,128)(2,1)}, bf16[640,128]{1,0:T(8,128)(2,1)S(1)}, u32[]{:S(2)}, u32[]{:S(2)}) collective-permute-start(bf16[640,128]{1,0:T(8,128)(2,1)} %get-tuple-element.25), channel_id=1, source_target_pairs={{0,2},{1,3},{2,4},{3,5},{4,6},{5,7},{6,0},{7,1},{8,10},{9,11},{10,... | collective-permute-start | bytes 491528 | tf_op jit(solution)/shard_map/ppermute | solution.py:425
  56.3 4.5 %collective-permute-start.5 = (bf16[640,128]{1,0:T(8,128)(2,1)}, bf16[640,128]{1,0:T(8,128)(2,1)S(1)}, u32[]{:S(2)}, u32[]{:S(2)}) collective-permute-start(bf16[640,128]{1,0:T(8,128)(2,1)} %get-tuple-element.26), channel_id=1, source_target_pairs={{0,6},{1,7},{2,0},{3,1},{4,2},{5,3},{6,4},{7,5},{8,14},{9,15},{10,... | collective-permute-start | bytes 491528 | tf_op jit(solution)/shard_map/ppermute | solution.py:425
  60.8 0.0 all-to-all-done.1
  60.8 0.2 shard_map.109.kv_ref
  61.0 1.9 %collective-permute-start.2 = (bf16[128,256]{1,0:T(8,128)(2,1)S(1)}, bf16[128,256]{1,0:T(8,128)(2,1)S(1)}, u32[]{:S(2)}, u32[]{:S(2)}) collective-permute-start(bf16[128,256]{1,0:T(8,128)(2,1)S(1)} %shard_map.109.kv_ref), channel_id=1, source_target_pairs={{0,1},{1,0},{2,3},{3,2},{4,5},{5,4},{6,7},{7,6},{8,9},{9,8},{10,11... | collective-permute-start | bytes 196616 | tf_op jit(solution)/shard_map/ppermute | solution.py:385
  63.0 1.0 %shard_map.107 = (bf16[256,640]{1,0:T(8,128)(2,1)}, f32[8,128]{1,0:T(8,128)S(1)}) custom-call(bf16[1024,128]{1,0:T(8,128)(2,1)S(1)} %bitcast.5, bf16[256,640]{1,0:T(8,128)(2,1)} %get-tuple-element.16.dq_in_ref), custom_call_target="tpu_custom_call", output_to_operand_aliasing={{0}: (1, {})} | custom-call | flops 100000000 | bytes 1000000 | tf_op jit(solution)/shard_map/pallas_call | solution.py:438
  63.9 0.3 collective-permute-done.2.kv_other_ref
  64.2 0.0 collective-permute-done.3.refs_0_.refs_1_
  64.2 0.0 collective-permute-done.4.refs_1_.refs_2_
  64.2 0.1 collective-permute-done.5.refs_2_.refs_3_
  64.3 0.8 %shard_map.110 = bf16[4,640,128]{2,1,0:T(8,128)(2,1)S(1)} custom-call(bf16[128,256]{1,0:T(8,128)(2,1)S(1)} %shard_map.109.kv_ref, bf16[128,256]{1,0:T(8,128)(2,1)S(1)} %collective-permute-done.2.kv_other_ref, bf16[2,4,640,128]{3,2,1,0:T(8,128)(2,1)S(1)} %copy-done, bf16[2,4,640,128]{3,2,1,0:T(8,128)(2,1)S(1)} %collective-permute-done.1.other_ref, ...), custom_call_target="tpu_custom_call" | custom-call | flops 40000000000 | bytes 4000000 | tf_op jit(solution)/shard_map/pallas_call | solution.py:448
  65.2 14.4 %all_to_all.15.leaf_ref = bf16[4,640,128]{2,1,0:T(8,128)(2,1)S(1)} all-to-all(bf16[4,640,128]{2,1,0:T(8,128)(2,1)S(1)} %shard_map.110), channel_id=1, replica_groups={{0,2,4,6},{1,3,5,7},{8,10,12,14},{9,11,13,15},{16,18,20,22},{17,19,21,2..., dimensions={0} | all-to-all | bytes 1310720 | tf_op jit(solution)/shard_map/all_to_all | solution.py:456
  79.6 0.9 %shard_map.111 = bf16[256,640]{1,0:T(8,128)(2,1)} custom-call(bf16[4,640,128]{2,1,0:T(8,128)(2,1)S(1)} %all_to_all.15.leaf_ref, bf16[640,128]{1,0:T(8,128)(2,1)S(1)} %get-tuple-element.27.refs_0_, bf16[640,128]{1,0:T(8,128)(2,1)S(1)} %collective-permute-done.3.refs_0_.refs_1_, bf16[640,128]{1,0:T(8,128)(2,1)S(1)} %collective-permute-done.4.refs_1_.refs_2_, ...), custom_call_target="tpu_custom_call" | custom-call | flops 1000000 | bytes 1000000 | tf_op jit(solution)/shard_map/pallas_call | solution.py:464
  (1 shorter events, 0.0 us)
Async XLA Ops:
  3.1 32.9 %all-to-all-start = ((bf16[64,24,128]{2,1,0:T(8,128)(2,1)}), bf16[64,24,128]{2,1,0:T(8,128)(2,1)S(1)}, u32[]{:S(2)}, u32[]{:S(2)}) async-start(bf16[64,24,128]{2,1,0:T(8,128)(2,1)} %bitcast.7), calls=%async_computation | async-start | bytes 786432 | tf_op jit(solution)/shard_map/all_to_all | solution.py:351
  19.7 16.3 %copy-start.1 = (bf16[256,128]{1,0:T(8,128)(2,1)S(1)}, bf16[256,128]{1,0:T(8,128)(2,1)}, u32[]{:S(2)}) copy-start(bf16[256,128]{1,0:T(8,128)(2,1)} %k_in.1) | copy-start | bytes 196612
  19.7 16.3 %copy-start.2 = (bf16[256,128]{1,0:T(8,128)(2,1)S(1)}, bf16[256,128]{1,0:T(8,128)(2,1)}, u32[]{:S(2)}) copy-start(bf16[256,128]{1,0:T(8,128)(2,1)} %v_in.1) | copy-start | bytes 196612
  19.7 16.3 %copy-start.3 = (s32[64,64]{1,0:T(8,128)S(1)}, s32[64,64]{1,0:T(8,128)}, u32[]{:S(2)}) copy-start(s32[64,64]{1,0:T(8,128)} %leaf_tree_ref.3) | copy-start | bytes 49156
  19.7 16.3 %copy-start.4 = (s32[64,64]{1,0:T(8,128)S(1)}, s32[64,64]{1,0:T(8,128)}, u32[]{:S(2)}) copy-start(s32[64,64]{1,0:T(8,128)} %leaf_len_ref.1) | copy-start | bytes 49156
  19.7 16.3 %copy-start.5 = (s32[64]{0:T(128)S(1)}, s32[64]{0:T(128)}, u32[]{:S(2)}) copy-start(s32[64]{0:T(128)} %trunk_len_in.3) | copy-start | bytes 772
  26.4 20.9 %collective-permute-start.1 = (bf16[2,4,640,128]{3,2,1,0:T(8,128)(2,1)}, bf16[2,4,640,128]{3,2,1,0:T(8,128)(2,1)S(1)}, u32[]{:S(2)}, u32[]{:S(2)}) collective-permute-start(bf16[2,4,640,128]{3,2,1,0:T(8,128)(2,1)} %get-tuple-element.21), channel_id=1, source_target_pairs={{0,1},{1,0},{2,3},{3,2},{4,5},{5,4},{6,7},{7,6},{8,9},{9,8},{10,11... | collective-permute-start | bytes 3932168 | tf_op jit(solution)/shard_map/ppermute | solution.py:385
  36.0 8.1 %copy-start.6 = (f32[128,256]{1,0:T(8,128)S(1)}, f32[128,256]{1,0:T(8,128)}, u32[]{:S(2)}) copy-start(f32[128,256]{1,0:T(8,128)} %get-tuple-element.18) | copy-start | bytes 393220
  36.0 11.3 %copy-start = (bf16[2,4,640,128]{3,2,1,0:T(8,128)(2,1)S(1)}, bf16[2,4,640,128]{3,2,1,0:T(8,128)(2,1)}, u32[]{:S(2)}) copy-start(bf16[2,4,640,128]{3,2,1,0:T(8,128)(2,1)} %get-tuple-element.20.own_ref) | copy-start | bytes 3932164
  38.5 22.3 %all-to-all-start.1 = ((bf16[64,16,128]{2,1,0:T(8,128)(2,1)}), bf16[64,16,128]{2,1,0:T(8,128)(2,1)S(1)}, u32[]{:S(2)}, u32[]{:S(2)}) async-start(bf16[64,16,128]{2,1,0:T(8,128)(2,1)} %bitcast.2), calls=%async_computation.1 | async-start | bytes 524288 | tf_op jit(solution)/shard_map/all_to_all | solution.py:426
  44.1 3.1 %collective-permute-start = (bf16[128,256]{1,0:T(8,128)(2,1)S(1)}, bf16[128,256]{1,0:T(8,128)(2,1)S(1)}, u32[]{:S(2)}, u32[]{:S(2)}) collective-permute-start(bf16[128,256]{1,0:T(8,128)(2,1)S(1)} %add_convert_fusion.kv_ref), channel_id=1, source_target_pairs={{0,1},{1,0},{2,3},{3,2},{4,5},{5,4},{6,7},{7,6},{8,9},{9,8},{10,11... | collective-permute-start | bytes 196616 | tf_op jit(solution)/shard_map/ppermute | solution.py:385
  48.8 15.4 %collective-permute-start.3 = (bf16[640,128]{1,0:T(8,128)(2,1)}, bf16[640,128]{1,0:T(8,128)(2,1)S(1)}, u32[]{:S(2)}, u32[]{:S(2)}) collective-permute-start(bf16[640,128]{1,0:T(8,128)(2,1)} %get-tuple-element.24), channel_id=1, source_target_pairs={{0,4},{1,5},{2,6},{3,7},{4,0},{5,1},{6,2},{7,3},{8,12},{9,13},{10,... | collective-permute-start | bytes 491528 | tf_op jit(solution)/shard_map/ppermute | solution.py:425
  53.7 10.5 %collective-permute-start.4 = (bf16[640,128]{1,0:T(8,128)(2,1)}, bf16[640,128]{1,0:T(8,128)(2,1)S(1)}, u32[]{:S(2)}, u32[]{:S(2)}) collective-permute-start(bf16[640,128]{1,0:T(8,128)(2,1)} %get-tuple-element.25), channel_id=1, source_target_pairs={{0,2},{1,3},{2,4},{3,5},{4,6},{5,7},{6,0},{7,1},{8,10},{9,11},{10,... | collective-permute-start | bytes 491528 | tf_op jit(solution)/shard_map/ppermute | solution.py:425
  56.3 8.1 %collective-permute-start.5 = (bf16[640,128]{1,0:T(8,128)(2,1)}, bf16[640,128]{1,0:T(8,128)(2,1)S(1)}, u32[]{:S(2)}, u32[]{:S(2)}) collective-permute-start(bf16[640,128]{1,0:T(8,128)(2,1)} %get-tuple-element.26), channel_id=1, source_target_pairs={{0,6},{1,7},{2,0},{3,1},{4,2},{5,3},{6,4},{7,5},{8,14},{9,15},{10,... | collective-permute-start | bytes 491528 | tf_op jit(solution)/shard_map/ppermute | solution.py:425
  61.0 3.1 %collective-permute-start.2 = (bf16[128,256]{1,0:T(8,128)(2,1)S(1)}, bf16[128,256]{1,0:T(8,128)(2,1)S(1)}, u32[]{:S(2)}, u32[]{:S(2)}) collective-permute-start(bf16[128,256]{1,0:T(8,128)(2,1)S(1)} %shard_map.109.kv_ref), channel_id=1, source_target_pairs={{0,1},{1,0},{2,3},{3,2},{4,5},{5,4},{6,7},{7,6},{8,9},{9,8},{10,11... | collective-permute-start | bytes 196616 | tf_op jit(solution)/shard_map/ppermute | solution.py:385

commit v4 on v3

--- a/solution.py
+++ b/solution.py
@@ -115,19 +115,24 @@
     return visible & (row_pos < row_len)
 
 
+def weight_pairs(w_key_ref, w_value_ref, to_ref, core):
+    chips, block = to_ref.shape[1:3]
+    pairs = []
+    for chip in range(chips):
+        rows = pl.ds(pl.multiple_of((2 * chip + core) * block, block), block)
+        pairs += [(w.at[rows, :], to_ref.at[part, chip]) for part, w in enumerate((w_key_ref, w_value_ref))]
+    return pairs
+
+
 def trunk_kernel(
     q_in, g_in, k_in, v_in, trunk_len_in, w_key_ref, w_value_ref,
     dq_ref, dkv_ref, own_ref, give_ref,
-    q_ref, g_ref, k_ref, v_ref, trunk_len_ref, dq_buf, dkv_buf, give_buf, sems, out_sems, weight_sems,
+    q_ref, g_ref, k_ref, v_ref, trunk_len_ref, ds_buf, p_buf, dq_buf, dkv_buf, give_buf,
+    sems, out_sems, own_sems, give_sems, gave_sems,
 ):
     trunk = pl.ds(0, TRUNK)
     core = lax.axis_index("kvh") & 1
-    chips, block = own_ref.shape[1:3]
-    pairs = []
-    for chip in range(chips):
-        for ref, which in ((give_buf, 1 - core), (own_ref, core)):
-            rows = pl.ds(pl.multiple_of((2 * chip + which) * block, block), block)
-            pairs += [(w.at[rows, :], ref.at[part, chip]) for part, w in enumerate((w_key_ref, w_value_ref))]
+    chips = own_ref.shape[1]
     loads = copies(
         [
             (trunk_len_in, trunk_len_ref),
@@ -138,44 +143,38 @@
         ],
         sems,
     )
-    weight_loads = copies(pairs, weight_sems)
+    give_loads = copies(weight_pairs(w_key_ref, w_value_ref, give_buf, 1 - core), give_sems)
+    own_loads = copies(weight_pairs(w_key_ref, w_value_ref, own_ref, core), own_sems)
     for load in loads:
         load.wait()
-    seg = lax.axis_index("seg")
-    trunk_len = trunk_len_ref[seg]
+    trunk_len = trunk_len_ref[lax.axis_index("seg")]
     keys = k_ref[...]
     values = v_ref[...]
     row = lax.broadcasted_iota(jnp.int32, (TRUNK, TRUNK), 0)
     col = lax.broadcasted_iota(jnp.int32, (TRUNK, TRUNK), 1)
     visible = (col <= row) & (row < trunk_len)
+    stores = []
     for g in range(GROUP):
-        head_q = q_ref[:, g * HEAD : (g + 1) * HEAD]
-        head_g = g_ref[:, g * HEAD : (g + 1) * HEAD]
-        scores = dot(head_q, keys, (1, 1)) * SCALE
-        prob_grad = dot(head_g, values, (1, 1))
-        probability, score_grad = softmax_grads(scores, prob_grad, visible)
-        dq_buf[:, g * HEAD : (g + 1) * HEAD] = (dot(score_grad, keys, (1, 0)) * SCALE).astype(bf16)
-        head_dk = dot(score_grad, head_q, (0, 0))
-        head_dv = dot(probability, head_g, (0, 0))
-        if g == 0:
-            dkv_buf[:, 0:HEAD] = head_dk
-            dkv_buf[:, HEAD:] = head_dv
-        else:
-            dkv_buf[:, 0:HEAD] += head_dk
-            dkv_buf[:, HEAD:] += head_dv
-    dkv_buf[:, 0:HEAD] *= SCALE
-    for load in weight_loads:
-        load.wait()
-    stores = copies(
-        [
-            (dq_buf, dq_ref.at[trunk, :]),
-            (dkv_buf, dkv_ref),
-            (give_buf, give_ref),
-        ],
-        out_sems,
-    )
-    for store in stores:
-        store.wait()
+        columns = slice(g * HEAD, (g + 1) * HEAD)
+        rows = slice(g * TRUNK, (g + 1) * TRUNK)
+        scores = dot(q_ref[:, columns], keys, (1, 1)) * SCALE
+        prob_grad = dot(g_ref[:, columns], values, (1, 1))
+        p_buf[rows, :], ds_buf[rows, :] = softmax_grads(scores, prob_grad, visible)
+        if g == 1:
+            for i, load in enumerate(give_loads):
+                load.wait()
+                part, chip = i % 2, i // 2
+                stores += copies([(give_buf.at[part, chip], give_ref.at[part, chip])], gave_sems.at[pl.ds(i, 1)])
+    query_grad = dot(ds_buf[...], keys, (1, 0)) * SCALE
+    for g in range(GROUP):
+        dq_buf[:, g * HEAD : (g + 1) * HEAD] = query_grad[g * TRUNK : (g + 1) * TRUNK, :].astype(bf16)
+    head_q = jnp.concatenate([q_ref[:, g * HEAD : (g + 1) * HEAD] for g in range(GROUP)], axis=0)
+    head_g = jnp.concatenate([g_ref[:, g * HEAD : (g + 1) * HEAD] for g in range(GROUP)], axis=0)
+    dkv_buf[:, 0:HEAD] = dot(ds_buf[...], head_q, (0, 0)) * SCALE
+    dkv_buf[:, HEAD:] = dot(p_buf[...], head_g, (0, 0))
+    stores += copies([(dq_buf, dq_ref.at[trunk, :]), (dkv_buf, dkv_ref)], out_sems)
+    for copy in stores + own_loads:
+        copy.wait()
 
 
 def leaf_kernel(
@@ -267,22 +266,24 @@
     return dot(weight, kv, (1, 1)).astype(bf16)
 
 
-def trunk_part_kernel(kv_ref, kv_other_ref, own_ref, other_ref, *refs):
+def trunk_part_kernel(steps, kv_ref, kv_other_ref, own_ref, other_ref, *refs):
+    count = len(steps[0]) + 1
     chips = own_ref.shape[1]
-    outs, token_ref, buf, sems = refs[:chips], refs[chips], refs[-2], refs[-1]
-    chip = lax.axis_index("kvh") >> 1
+    outs, token_ref, buf, sems = refs[:count], refs[count], refs[-2], refs[-1]
+    kvh = lax.axis_index("kvh")
+    chip, core = kvh >> 1, kvh & 1
     stores = []
-    for step in reversed(range(chips)):
-        buf[step] = chip_part(kv_ref, kv_other_ref, own_ref, other_ref, lax.rem(chip + step, chips))
-        stores.append(pltpu.make_async_copy(buf.at[step], outs[step], sems.at[step]))
+    for i, (even, odd) in enumerate(zip(steps[0] + (0,), steps[1] + (0,))):
+        block = lax.rem(chip + even + core * (odd - even), chips)
+        buf[i] = chip_part(kv_ref, kv_other_ref, own_ref, other_ref, block)
+        stores.append(pltpu.make_async_copy(buf.at[i], outs[i], sems.at[i]))
         stores[-1].start()
     token_ref[...] = jnp.zeros(token_ref.shape, f32)
     for store in stores:
         store.wait()
 
 
-def leaf_part_kernel(kv_ref, kv_other_ref, own_ref, other_ref, after_ref, *refs):
-    out_ref = refs[-1]
+def leaf_part_kernel(kv_ref, kv_other_ref, own_ref, other_ref, after_ref, out_ref):
     for block in range(out_ref.shape[0]):
         out_ref[block] = chip_part(kv_ref, kv_other_ref, own_ref, other_ref, block)
 
@@ -295,7 +296,7 @@
         for part in parts[1:]:
             total += part.astype(f32)
         rows = pl.ds(i * TRUNK, TRUNK)
-        buf[rows, :] = total.T.astype(bf16)
+        buf[rows, :] = total.astype(bf16).T
         stores.append(pltpu.make_async_copy(buf.at[rows, :], out_ref.at[rows, :], sems.at[i]))
         stores[-1].start()
     for store in stores:
@@ -369,12 +370,16 @@
             vm((TRUNK, HEAD), bf16),
             vm((TRUNK, HEAD), bf16),
             pltpu.SMEM((count,), jnp.int32),
+            vm((GROUP * TRUNK, TRUNK), bf16),
+            vm((GROUP * TRUNK, TRUNK), bf16),
             vm((TRUNK, row_width), bf16),
             vm((TRUNK, 2 * HEAD), f32),
             vm((2, chips, columns, HEAD), bf16),
             dma((5,)),
-            dma((3,)),
-            dma((4 * chips,)),
+            dma((2,)),
+            dma((2 * chips,)),
+            dma((2 * chips,)),
+            dma((2 * chips,)),
         ],
         flops=4 * 10**10,
         moved=10**7,
@@ -410,8 +415,9 @@
 
     part_flops = 2 * TRUNK * 4 * HEAD * chips * columns
     part_shape = (columns, TRUNK)
+    steps = ((2, 1, 3), (2, 3, 1))
     *trunk_parts, token = call(
-        trunk_part_kernel,
+        functools.partial(trunk_part_kernel, steps),
         [out(part_shape, bf16)] * chips + [out((8, HEAD), f32)],
         [vmem] * 4,
         [hbm] * chips + [vmem],
@@ -419,10 +425,10 @@
         flops=part_flops,
         moved=4 * 10**6,
     )(trunk_kv, swap(trunk_kv), own, other)
-    trunk_came = [trunk_parts[0]]
-    for step in (2, 1, 3):
-        route = [(2 * x + c, 2 * ((x + step) % chips) + c) for x in range(chips) for c in range(2)]
-        trunk_came.append(lax.ppermute(trunk_parts[step], "kvh", route))
+    trunk_came = [trunk_parts[-1]]
+    for i in range(chips - 1):
+        route = [(2 * x + c, 2 * ((x + steps[c][i]) % chips) + c) for x in range(chips) for c in range(2)]
+        trunk_came.append(lax.ppermute(trunk_parts[i], "kvh", route))
     back = lax.all_to_all(
         back.reshape(count, BACK_ROWS, HEAD), "seg", split_axis=0, concat_axis=0, tiled=True
     ).reshape(count * BACK_ROWS, HEAD)
@@ -432,7 +438,7 @@
         [vmem] * 2,
         vmem,
         [vm((count * BACK_ROWS, HEAD), f32)],
-        flops=4 * 10**10,
+        flops=10**7,
         moved=10**6,
     )(back, token)
     grad_query, token = call(
@@ -448,11 +454,12 @@
     parts = call(
         leaf_part_kernel,
         out((chips, columns, leaf_rows), bf16),
-        [vmem] * 5 + [hbm] * (chips - 1),
+        [vmem] * 5,
         vmem,
-        flops=4 * 10**10,
+        flops=10**7,
         moved=4 * 10**6,
-    )(leaf_kv, swap(leaf_kv), own, other, token, *trunk_came[1:])
+    )(leaf_kv, swap(leaf_kv), own, other, token)
+    parts, *trunk_came = lax.optimization_barrier((parts, *trunk_came))
     came = lax.all_to_all(
         parts,
         "kvh",

time: 81 us -> 80.4 us (level)
  the two profiles are of different devices: /device:TPU:8 before, /device:TPU:1 now
where the time goes in v4:
time: 80.4 us; the launch traced here: 78.9 us
  starting transfers between devices  44.2 us (55%)
  Pallas kernels  14.5 us (18%)
  blocking collectives  11.7 us (15%)
  waiting for transfers between devices  7.54 us (9%)
  between operations  0.87 us (1%)
    all_to_all x1, starting transfers between devices, shards(): lax.all_to_all(send.reshape(count, OUT_ROWS, HEAD), 'seg', split_axis=0,...  17.1 us
    all_to_all x1, blocking collectives, shards(): lax.all_to_all(parts, 'kvh', split_axis=0, concat_axis=0, tiled=True, axi...  11.7 us
    ppermute x3, starting transfers between devices, swap(): return lax.ppermute(value, 'kvh', [(i, i ^ 1) for i in range(heads)])  10.6 us
    ppermute x3, starting transfers between devices, shards(): trunk_came.append(lax.ppermute(trunk_parts[i], 'kvh', route))  9.93 us
    all_to_all x1, waiting for transfers between devices, shards(): lax.all_to_all(send.reshape(count, OUT_ROWS, HEAD), 'seg', split_axis=0,...  6.65 us
    all_to_all x1, starting transfers between devices, shards(): lax.all_to_all(back.reshape(count, BACK_ROWS, HEAD), 'seg', split_axis=0,...  6.55 us
    pallas_call x1, Pallas kernels, shards(): call(trunk_kernel, [out(queries.shape, bf16), out((TRUNK, 2 * HEAD), f32)...  5.08 us
    pallas_call x1, Pallas kernels, shards(): call(leaf_kernel, [out((count * BACK_ROWS, HEAD), bf16), out((TRUNK, 2 *...  2.55 us
  transfers between devices with their start and end apart: 8, of which 2 were waited for; matrix products, arithmetic and copies ran while one was open for 0% of the time, Pallas kernels for 14%

profile of v4, /device:TPU:1, one launch (start us, length us, event | category | flops | bytes accessed | tf_op | source)
XLA Modules:
  0.0 78.9 jit_solution(7630558330697280515)
XLA Ops:
  0.6 2.4 %shard_map.104 = bf16[1536,128]{1,0:T(8,128)(2,1)} custom-call(bf16[256,640]{1,0:T(8,128)(2,1)} %q_in.1, bf16[256,640]{1,0:T(8,128)(2,1)} %g_in.1, bf16[256,128]{1,0:T(8,128)(2,1)} %k_in.1, bf16[256,128]{1,0:T(8,128)(2,1)} %v_in.1, s32[64,64]{1,0:T(8,128)} %leaf_tree_ref.3), custom_call_target="tpu_custom_call" | custom-call | flops 100000000 | bytes 1000000 | tf_op jit(solution)/shard_map/pallas_call | solution.py:332
  3.1 17.1 %all-to-all-start = ((bf16[64,24,128]{2,1,0:T(8,128)(2,1)}), bf16[64,24,128]{2,1,0:T(8,128)(2,1)S(1)}, u32[]{:S(2)}, u32[]{:S(2)}) async-start(bf16[64,24,128]{2,1,0:T(8,128)(2,1)} %bitcast.7), calls=%async_computation | async-start | bytes 786432 | tf_op jit(solution)/shard_map/all_to_all | solution.py:352
  20.2 0.0 copy-start.1
  20.2 0.0 copy-start.2
  20.2 0.0 copy-start.3
  20.3 0.0 copy-start.4
  20.3 0.0 copy-start.5
  20.3 5.1 %shard_map.106 = (bf16[256,640]{1,0:T(8,128)(2,1)}, f32[128,256]{1,0:T(8,128)}, bf16[2,4,640,128]{3,2,1,0:T(8,128)(2,1)}, bf16[2,4,640,128]{3,2,1,0:T(8,128)(2,1)}) custom-call(bf16[256,640]{1,0:T(8,128)(2,1)} %q_in.1, bf16[256,640]{1,0:T(8,128)(2,1)} %g_in.1, bf16[256,128]{1,0:T(8,128)(2,1)} %k_in.1, bf16[256,128]{1,0:T(8,128)(2,1)} %v_in.1, ...), custom_call_target="tpu_custom_call" | custom-call | flops 40000000000 | bytes 10000000 | tf_op jit(solution)/shard_map/pallas_call | solution.py:357
  25.4 2.9 %collective-permute-start.1 = (bf16[2,4,640,128]{3,2,1,0:T(8,128)(2,1)}, bf16[2,4,640,128]{3,2,1,0:T(8,128)(2,1)S(1)}, u32[]{:S(2)}, u32[]{:S(2)}) collective-permute-start(bf16[2,4,640,128]{3,2,1,0:T(8,128)(2,1)} %get-tuple-element.26), channel_id=1, source_target_pairs={{0,1},{1,0},{2,3},{3,2},{4,5},{5,4},{6,7},{7,6},{8,9},{9,8},{10,11... | collective-permute-start | bytes 3932168 | tf_op jit(solution)/shard_map/ppermute | solution.py:390
  28.2 6.6 %all-to-all-done = bf16[64,24,128]{2,1,0:T(8,128)(2,1)S(1)} async-done(((bf16[64,24,128]{2,1,0:T(8,128)(2,1)}), bf16[64,24,128]{2,1,0:T(8,128)(2,1)S(1)}, u32[]{:S(2)}, u32[]{:S(2)}) %all-to-all-start) | async-done | bytes 393248 | tf_op jit(solution)/shard_map/all_to_all | solution.py:352
  34.9 0.0 copy-done.1
  34.9 0.0 copy-done.2
  34.9 0.0 copy-done.3
  34.9 0.0 copy-done.4
  34.9 0.0 copy-done.5
  34.9 0.0 copy-start.6
  34.9 0.0 copy-start
  34.9 2.5 %shard_map.105 = (bf16[1024,128]{1,0:T(8,128)(2,1)}, f32[128,256]{1,0:T(8,128)S(1)}) custom-call(bf16[1536,128]{1,0:T(8,128)(2,1)S(1)} %bitcast.6, bf16[256,128]{1,0:T(8,128)(2,1)S(1)} %copy-done.1, bf16[256,128]{1,0:T(8,128)(2,1)S(1)} %copy-done.2, s32[64,64]{1,0:T(8,128)S(1)} %copy-done.3, s32[64,64]{1,0:T(8,128)S(1)} %copy-done.4, s32[64]{0:T(128)S(1)} %copy-done.5), custom_call_target="tpu_custom_call" | custom-call | flops 40000000000 | bytes 1000000 | tf_op jit(solution)/shard_map/pallas_call | solution.py:394
  37.5 6.6 %all-to-all-start.1 = ((bf16[64,16,128]{2,1,0:T(8,128)(2,1)}), bf16[64,16,128]{2,1,0:T(8,128)(2,1)S(1)}, u32[]{:S(2)}, u32[]{:S(2)}) async-start(bf16[64,16,128]{2,1,0:T(8,128)(2,1)} %bitcast.2), calls=%async_computation.1 | async-start | bytes 524288 | tf_op jit(solution)/shard_map/all_to_all | solution.py:432
  44.0 0.0 copy-done.6
  44.1 3.4 %collective-permute-start = (bf16[128,256]{1,0:T(8,128)(2,1)S(1)}, bf16[128,256]{1,0:T(8,128)(2,1)S(1)}, u32[]{:S(2)}, u32[]{:S(2)}) collective-permute-start(bf16[128,256]{1,0:T(8,128)(2,1)S(1)} %add_convert_fusion.kv_ref), channel_id=1, source_target_pairs={{0,1},{1,0},{2,3},{3,2},{4,5},{5,4},{6,7},{7,6},{8,9},{9,8},{10,11... | collective-permute-start | bytes 196616 | tf_op jit(solution)/shard_map/ppermute | solution.py:390
  47.5 0.9 %collective-permute-done.kv_other_ref = bf16[128,256]{1,0:T(8,128)(2,1)S(1)} collective-permute-done((bf16[128,256]{1,0:T(8,128)(2,1)S(1)}, bf16[128,256]{1,0:T(8,128)(2,1)S(1)}, u32[]{:S(2)}, u32[]{:S(2)}) %collective-permute-start) | collective-permute-done | bytes 65568 | tf_op jit(solution)/shard_map/ppermute | solution.py:390
  48.4 0.0 collective-permute-done.1.other_ref
  48.4 0.0 copy-done
  48.4 1.5 %shard_map.108 = (bf16[640,128]{1,0:T(8,128)(2,1)}, bf16[640,128]{1,0:T(8,128)(2,1)}, bf16[640,128]{1,0:T(8,128)(2,1)}, bf16[640,128]{1,0:T(8,128)(2,1)S(1)}, f32[8,128]{1,0:T(8,128)S(1)}) custom-call(bf16[128,256]{1,0:T(8,128)(2,1)S(1)} %add_convert_fusion.kv_ref, bf16[128,256]{1,0:T(8,128)(2,1)S(1)} %collective-permute-done.kv_other_ref, ...), custom_call_target="tpu_custom_call" | custom-call | flops 335544320 | bytes 4000000 | tf_op jit(solution)/shard_map/pallas_call | solution.py:419
  50.0 4.6 %collective-permute-start.3 = (bf16[640,128]{1,0:T(8,128)(2,1)}, bf16[640,128]{1,0:T(8,128)(2,1)S(1)}, u32[]{:S(2)}, u32[]{:S(2)}) collective-permute-start(bf16[640,128]{1,0:T(8,128)(2,1)} %get-tuple-element.30), channel_id=1, source_target_pairs={{0,4},{1,5},{2,6},{3,7},{4,0},{5,1},{6,2},{7,3},{8,12},{9,13},{10,... | collective-permute-start | bytes 491528 | tf_op jit(solution)/shard_map/ppermute | solution.py:431
  54.6 2.8 %collective-permute-start.4 = (bf16[640,128]{1,0:T(8,128)(2,1)}, bf16[640,128]{1,0:T(8,128)(2,1)S(1)}, u32[]{:S(2)}, u32[]{:S(2)}) collective-permute-start(bf16[640,128]{1,0:T(8,128)(2,1)} %get-tuple-element.31), channel_id=1, source_target_pairs={{0,2},{1,7},{2,4},{3,1},{4,6},{5,3},{6,0},{7,5},{8,10},{9,15},{10,... | collective-permute-start | bytes 491528 | tf_op jit(solution)/shard_map/ppermute | solution.py:431
  57.4 2.5 %collective-permute-start.5 = (bf16[640,128]{1,0:T(8,128)(2,1)}, bf16[640,128]{1,0:T(8,128)(2,1)S(1)}, u32[]{:S(2)}, u32[]{:S(2)}) collective-permute-start(bf16[640,128]{1,0:T(8,128)(2,1)} %get-tuple-element.32), channel_id=1, source_target_pairs={{0,6},{1,3},{2,0},{3,5},{4,2},{5,7},{6,4},{7,1},{8,14},{9,11},{10,... | collective-permute-start | bytes 491528 | tf_op jit(solution)/shard_map/ppermute | solution.py:431
  59.9 0.0 all-to-all-done.1
  59.9 0.2 shard_map.109.kv_ref
  60.1 4.3 %collective-permute-start.2 = (bf16[128,256]{1,0:T(8,128)(2,1)S(1)}, bf16[128,256]{1,0:T(8,128)(2,1)S(1)}, u32[]{:S(2)}, u32[]{:S(2)}) collective-permute-start(bf16[128,256]{1,0:T(8,128)(2,1)S(1)} %shard_map.109.kv_ref), channel_id=1, source_target_pairs={{0,1},{1,0},{2,3},{3,2},{4,5},{5,4},{6,7},{7,6},{8,9},{9,8},{10,11... | collective-permute-start | bytes 196616 | tf_op jit(solution)/shard_map/ppermute | solution.py:390
  64.5 1.0 %shard_map.107 = (bf16[256,640]{1,0:T(8,128)(2,1)}, f32[8,128]{1,0:T(8,128)S(1)}) custom-call(bf16[1024,128]{1,0:T(8,128)(2,1)S(1)} %bitcast.5, bf16[256,640]{1,0:T(8,128)(2,1)} %get-tuple-element.21.dq_in_ref), custom_call_target="tpu_custom_call", output_to_operand_aliasing={{0}: (1, {})} | custom-call | flops 100000000 | bytes 1000000 | tf_op jit(solution)/shard_map/pallas_call | solution.py:444
  65.4 0.0 collective-permute-done.2.kv_other_ref
  65.4 0.8 %shard_map.110 = bf16[4,640,128]{2,1,0:T(8,128)(2,1)S(1)} custom-call(bf16[128,256]{1,0:T(8,128)(2,1)S(1)} %shard_map.109.kv_ref, bf16[128,256]{1,0:T(8,128)(2,1)S(1)} %collective-permute-done.2.kv_other_ref, bf16[2,4,640,128]{3,2,1,0:T(8,128)(2,1)S(1)} %copy-done, bf16[2,4,640,128]{3,2,1,0:T(8,128)(2,1)S(1)} %collective-permute-done.1.other_ref, ...), custom_call_target="tpu_custom_call" | custom-call | flops 10000000 | bytes 4000000 | tf_op jit(solution)/shard_map/pallas_call | solution.py:454
  66.3 0.0 collective-permute-done.3.refs_1_
  66.3 0.0 collective-permute-done.4.refs_2_
  66.3 0.0 collective-permute-done.5.refs_3_
  66.3 11.7 %all_to_all.15.leaf_ref = bf16[4,640,128]{2,1,0:T(8,128)(2,1)S(1)} all-to-all(bf16[4,640,128]{2,1,0:T(8,128)(2,1)S(1)} %shard_map.110), channel_id=1, replica_groups={{0,2,4,6},{1,3,5,7},{8,10,12,14},{9,11,13,15},{16,18,20,22},{17,19,21,2..., dimensions={0} | all-to-all | bytes 1310720 | tf_op jit(solution)/shard_map/all_to_all | solution.py:463
  78.0 0.9 %shard_map.111 = bf16[256,640]{1,0:T(8,128)(2,1)} custom-call(bf16[4,640,128]{2,1,0:T(8,128)(2,1)S(1)} %all_to_all.15.leaf_ref, bf16[640,128]{1,0:T(8,128)(2,1)S(1)} %get-tuple-element.34.refs_0_, bf16[640,128]{1,0:T(8,128)(2,1)S(1)} %collective-permute-done.3.refs_1_, bf16[640,128]{1,0:T(8,128)(2,1)S(1)} %collective-permute-done.4.refs_2_, ...), custom_call_target="tpu_custom_call" | custom-call | flops 1000000 | bytes 1000000 | tf_op jit(solution)/shard_map/pallas_call | solution.py:471
  (1 shorter events, 0.0 us)
Async XLA Ops:
  3.1 31.8 %all-to-all-start = ((bf16[64,24,128]{2,1,0:T(8,128)(2,1)}), bf16[64,24,128]{2,1,0:T(8,128)(2,1)S(1)}, u32[]{:S(2)}, u32[]{:S(2)}) async-start(bf16[64,24,128]{2,1,0:T(8,128)(2,1)} %bitcast.7), calls=%async_computation | async-start | bytes 786432 | tf_op jit(solution)/shard_map/all_to_all | solution.py:352
  20.2 14.7 %copy-start.1 = (bf16[256,128]{1,0:T(8,128)(2,1)S(1)}, bf16[256,128]{1,0:T(8,128)(2,1)}, u32[]{:S(2)}) copy-start(bf16[256,128]{1,0:T(8,128)(2,1)} %k_in.1) | copy-start | bytes 196612
  20.2 14.7 %copy-start.2 = (bf16[256,128]{1,0:T(8,128)(2,1)S(1)}, bf16[256,128]{1,0:T(8,128)(2,1)}, u32[]{:S(2)}) copy-start(bf16[256,128]{1,0:T(8,128)(2,1)} %v_in.1) | copy-start | bytes 196612
  20.2 14.6 %copy-start.3 = (s32[64,64]{1,0:T(8,128)S(1)}, s32[64,64]{1,0:T(8,128)}, u32[]{:S(2)}) copy-start(s32[64,64]{1,0:T(8,128)} %leaf_tree_ref.3) | copy-start | bytes 49156
  20.3 14.6 %copy-start.4 = (s32[64,64]{1,0:T(8,128)S(1)}, s32[64,64]{1,0:T(8,128)}, u32[]{:S(2)}) copy-start(s32[64,64]{1,0:T(8,128)} %leaf_len_ref.1) | copy-start | bytes 49156
  20.3 14.6 %copy-start.5 = (s32[64]{0:T(128)S(1)}, s32[64]{0:T(128)}, u32[]{:S(2)}) copy-start(s32[64]{0:T(128)} %trunk_len_in.3) | copy-start | bytes 772
  25.4 23.0 %collective-permute-start.1 = (bf16[2,4,640,128]{3,2,1,0:T(8,128)(2,1)}, bf16[2,4,640,128]{3,2,1,0:T(8,128)(2,1)S(1)}, u32[]{:S(2)}, u32[]{:S(2)}) collective-permute-start(bf16[2,4,640,128]{3,2,1,0:T(8,128)(2,1)} %get-tuple-element.26), channel_id=1, source_target_pairs={{0,1},{1,0},{2,3},{3,2},{4,5},{5,4},{6,7},{7,6},{8,9},{9,8},{10,11... | collective-permute-start | bytes 3932168 | tf_op jit(solution)/shard_map/ppermute | solution.py:390
  34.9 9.1 %copy-start.6 = (f32[128,256]{1,0:T(8,128)S(1)}, f32[128,256]{1,0:T(8,128)}, u32[]{:S(2)}) copy-start(f32[128,256]{1,0:T(8,128)} %get-tuple-element.23) | copy-start | bytes 393220
  34.9 13.5 %copy-start = (bf16[2,4,640,128]{3,2,1,0:T(8,128)(2,1)S(1)}, bf16[2,4,640,128]{3,2,1,0:T(8,128)(2,1)}, u32[]{:S(2)}) copy-start(bf16[2,4,640,128]{3,2,1,0:T(8,128)(2,1)} %get-tuple-element.25.own_ref) | copy-start | bytes 3932164
  37.5 22.4 %all-to-all-start.1 = ((bf16[64,16,128]{2,1,0:T(8,128)(2,1)}), bf16[64,16,128]{2,1,0:T(8,128)(2,1)S(1)}, u32[]{:S(2)}, u32[]{:S(2)}) async-start(bf16[64,16,128]{2,1,0:T(8,128)(2,1)} %bitcast.2), calls=%async_computation.1 | async-start | bytes 524288 | tf_op jit(solution)/shard_map/all_to_all | solution.py:432
  44.1 4.3 %collective-permute-start = (bf16[128,256]{1,0:T(8,128)(2,1)S(1)}, bf16[128,256]{1,0:T(8,128)(2,1)S(1)}, u32[]{:S(2)}, u32[]{:S(2)}) collective-permute-start(bf16[128,256]{1,0:T(8,128)(2,1)S(1)} %add_convert_fusion.kv_ref), channel_id=1, source_target_pairs={{0,1},{1,0},{2,3},{3,2},{4,5},{5,4},{6,7},{7,6},{8,9},{9,8},{10,11... | collective-permute-start | bytes 196616 | tf_op jit(solution)/shard_map/ppermute | solution.py:390
  50.0 16.3 %collective-permute-start.3 = (bf16[640,128]{1,0:T(8,128)(2,1)}, bf16[640,128]{1,0:T(8,128)(2,1)S(1)}, u32[]{:S(2)}, u32[]{:S(2)}) collective-permute-start(bf16[640,128]{1,0:T(8,128)(2,1)} %get-tuple-element.30), channel_id=1, source_target_pairs={{0,4},{1,5},{2,6},{3,7},{4,0},{5,1},{6,2},{7,3},{8,12},{9,13},{10,... | collective-permute-start | bytes 491528 | tf_op jit(solution)/shard_map/ppermute | solution.py:431
  54.6 11.7 %collective-permute-start.4 = (bf16[640,128]{1,0:T(8,128)(2,1)}, bf16[640,128]{1,0:T(8,128)(2,1)S(1)}, u32[]{:S(2)}, u32[]{:S(2)}) collective-permute-start(bf16[640,128]{1,0:T(8,128)(2,1)} %get-tuple-element.31), channel_id=1, source_target_pairs={{0,2},{1,7},{2,4},{3,1},{4,6},{5,3},{6,0},{7,5},{8,10},{9,15},{10,... | collective-permute-start | bytes 491528 | tf_op jit(solution)/shard_map/ppermute | solution.py:431
  57.4 8.9 %collective-permute-start.5 = (bf16[640,128]{1,0:T(8,128)(2,1)}, bf16[640,128]{1,0:T(8,128)(2,1)S(1)}, u32[]{:S(2)}, u32[]{:S(2)}) collective-permute-start(bf16[640,128]{1,0:T(8,128)(2,1)} %get-tuple-element.32), channel_id=1, source_target_pairs={{0,6},{1,3},{2,0},{3,5},{4,2},{5,7},{6,4},{7,1},{8,14},{9,11},{10,... | collective-permute-start | bytes 491528 | tf_op jit(solution)/shard_map/ppermute | solution.py:431
  60.1 5.3 %collective-permute-start.2 = (bf16[128,256]{1,0:T(8,128)(2,1)S(1)}, bf16[128,256]{1,0:T(8,128)(2,1)S(1)}, u32[]{:S(2)}, u32[]{:S(2)}) collective-permute-start(bf16[128,256]{1,0:T(8,128)(2,1)S(1)} %shard_map.109.kv_ref), channel_id=1, source_target_pairs={{0,1},{1,0},{2,3},{3,2},{4,5},{5,4},{6,7},{7,6},{8,9},{9,8},{10,11... | collective-permute-start | bytes 196616 | tf_op jit(solution)/shard_map/ppermute | solution.py:390

commit v5 on v4

--- a/solution.py
+++ b/solution.py
@@ -415,7 +415,7 @@
 
     part_flops = 2 * TRUNK * 4 * HEAD * chips * columns
     part_shape = (columns, TRUNK)
-    steps = ((2, 1, 3), (2, 3, 1))
+    steps = ((1, 3, 2), (1, 3, 2))
     *trunk_parts, token = call(
         functools.partial(trunk_part_kernel, steps),
         [out(part_shape, bf16)] * chips + [out((8, HEAD), f32)],

time: 80.4 us -> 79.3 us (0.986)
  starting transfers between devices: 44.2 us -> 43 us
    ppermute x3, starting transfers between devices: 10.6 us -> 9.4 us  [swap(): return lax.ppermute(value, 'kvh', [(i, i ^ 1) for i in range(heads)])]
where the time goes in v5:
time: 79.3 us; the launch traced here: 77.8 us
  starting transfers between devices  43 us (54%)
  Pallas kernels  14.5 us (18%)
  blocking collectives  11.8 us (15%)
  waiting for transfers between devices  7.54 us (10%)
  between operations  0.87 us (1%)
    all_to_all x1, starting transfers between devices, shards(): lax.all_to_all(send.reshape(count, OUT_ROWS, HEAD), 'seg', split_axis=0,...  17.1 us
    all_to_all x1, blocking collectives, shards(): lax.all_to_all(parts, 'kvh', split_axis=0, concat_axis=0, tiled=True, axi...  11.8 us
    ppermute x3, starting transfers between devices, shards(): trunk_came.append(lax.ppermute(trunk_parts[i], 'kvh', route))  9.93 us
    ppermute x3, starting transfers between devices, swap(): return lax.ppermute(value, 'kvh', [(i, i ^ 1) for i in range(heads)])  9.4 us
    all_to_all x1, waiting for transfers between devices, shards(): lax.all_to_all(send.reshape(count, OUT_ROWS, HEAD), 'seg', split_axis=0,...  6.65 us
    all_to_all x1, starting transfers between devices, shards(): lax.all_to_all(back.reshape(count, BACK_ROWS, HEAD), 'seg', split_axis=0,...  6.55 us
    pallas_call x1, Pallas kernels, shards(): call(trunk_kernel, [out(queries.shape, bf16), out((TRUNK, 2 * HEAD), f32)...  5.08 us
    pallas_call x1, Pallas kernels, shards(): call(leaf_kernel, [out((count * BACK_ROWS, HEAD), bf16), out((TRUNK, 2 *...  2.55 us
  transfers between devices with their start and end apart: 8, of which 2 were waited for; matrix products, arithmetic and copies ran while one was open for 0% of the time, Pallas kernels for 14%

profile of v5, /device:TPU:1, one launch (start us, length us, event | category | flops | bytes accessed | tf_op | source)
XLA Modules:
  0.0 77.8 jit_solution(9585627419258375720)
XLA Ops:
  0.6 2.4 %shard_map.104 = bf16[1536,128]{1,0:T(8,128)(2,1)} custom-call(bf16[256,640]{1,0:T(8,128)(2,1)} %q_in.1, bf16[256,640]{1,0:T(8,128)(2,1)} %g_in.1, bf16[256,128]{1,0:T(8,128)(2,1)} %k_in.1, bf16[256,128]{1,0:T(8,128)(2,1)} %v_in.1, s32[64,64]{1,0:T(8,128)} %leaf_tree_ref.3), custom_call_target="tpu_custom_call" | custom-call | flops 100000000 | bytes 1000000 | tf_op jit(solution)/shard_map/pallas_call | solution.py:332
  3.1 17.1 %all-to-all-start = ((bf16[64,24,128]{2,1,0:T(8,128)(2,1)}), bf16[64,24,128]{2,1,0:T(8,128)(2,1)S(1)}, u32[]{:S(2)}, u32[]{:S(2)}) async-start(bf16[64,24,128]{2,1,0:T(8,128)(2,1)} %bitcast.7), calls=%async_computation | async-start | bytes 786432 | tf_op jit(solution)/shard_map/all_to_all | solution.py:352
  20.2 0.0 copy-start.1
  20.2 0.0 copy-start.2
  20.2 0.0 copy-start.3
  20.3 0.0 copy-start.4
  20.3 0.0 copy-start.5
  20.3 5.1 %shard_map.106 = (bf16[256,640]{1,0:T(8,128)(2,1)}, f32[128,256]{1,0:T(8,128)}, bf16[2,4,640,128]{3,2,1,0:T(8,128)(2,1)}, bf16[2,4,640,128]{3,2,1,0:T(8,128)(2,1)}) custom-call(bf16[256,640]{1,0:T(8,128)(2,1)} %q_in.1, bf16[256,640]{1,0:T(8,128)(2,1)} %g_in.1, bf16[256,128]{1,0:T(8,128)(2,1)} %k_in.1, bf16[256,128]{1,0:T(8,128)(2,1)} %v_in.1, ...), custom_call_target="tpu_custom_call" | custom-call | flops 40000000000 | bytes 10000000 | tf_op jit(solution)/shard_map/pallas_call | solution.py:357
  25.4 2.9 %collective-permute-start.1 = (bf16[2,4,640,128]{3,2,1,0:T(8,128)(2,1)}, bf16[2,4,640,128]{3,2,1,0:T(8,128)(2,1)S(1)}, u32[]{:S(2)}, u32[]{:S(2)}) collective-permute-start(bf16[2,4,640,128]{3,2,1,0:T(8,128)(2,1)} %get-tuple-element.26), channel_id=1, source_target_pairs={{0,1},{1,0},{2,3},{3,2},{4,5},{5,4},{6,7},{7,6},{8,9},{9,8},{10,11... | collective-permute-start | bytes 3932168 | tf_op jit(solution)/shard_map/ppermute | solution.py:390
  28.2 6.6 %all-to-all-done = bf16[64,24,128]{2,1,0:T(8,128)(2,1)S(1)} async-done(((bf16[64,24,128]{2,1,0:T(8,128)(2,1)}), bf16[64,24,128]{2,1,0:T(8,128)(2,1)S(1)}, u32[]{:S(2)}, u32[]{:S(2)}) %all-to-all-start) | async-done | bytes 393248 | tf_op jit(solution)/shard_map/all_to_all | solution.py:352
  34.9 0.0 copy-done.1
  34.9 0.0 copy-done.2
  34.9 0.0 copy-done.3
  34.9 0.0 copy-done.4
  34.9 0.0 copy-done.5
  34.9 0.0 copy-start.6
  34.9 0.0 copy-start
  34.9 2.5 %shard_map.105 = (bf16[1024,128]{1,0:T(8,128)(2,1)}, f32[128,256]{1,0:T(8,128)S(1)}) custom-call(bf16[1536,128]{1,0:T(8,128)(2,1)S(1)} %bitcast.6, bf16[256,128]{1,0:T(8,128)(2,1)S(1)} %copy-done.1, bf16[256,128]{1,0:T(8,128)(2,1)S(1)} %copy-done.2, s32[64,64]{1,0:T(8,128)S(1)} %copy-done.3, s32[64,64]{1,0:T(8,128)S(1)} %copy-done.4, s32[64]{0:T(128)S(1)} %copy-done.5), custom_call_target="tpu_custom_call" | custom-call | flops 40000000000 | bytes 1000000 | tf_op jit(solution)/shard_map/pallas_call | solution.py:394
  37.5 6.6 %all-to-all-start.1 = ((bf16[64,16,128]{2,1,0:T(8,128)(2,1)}), bf16[64,16,128]{2,1,0:T(8,128)(2,1)S(1)}, u32[]{:S(2)}, u32[]{:S(2)}) async-start(bf16[64,16,128]{2,1,0:T(8,128)(2,1)} %bitcast.2), calls=%async_computation.1 | async-start | bytes 524288 | tf_op jit(solution)/shard_map/all_to_all | solution.py:432
  44.0 0.0 copy-done.6
  44.1 3.4 %collective-permute-start = (bf16[128,256]{1,0:T(8,128)(2,1)S(1)}, bf16[128,256]{1,0:T(8,128)(2,1)S(1)}, u32[]{:S(2)}, u32[]{:S(2)}) collective-permute-start(bf16[128,256]{1,0:T(8,128)(2,1)S(1)} %add_convert_fusion.kv_ref), channel_id=1, source_target_pairs={{0,1},{1,0},{2,3},{3,2},{4,5},{5,4},{6,7},{7,6},{8,9},{9,8},{10,11... | collective-permute-start | bytes 196616 | tf_op jit(solution)/shard_map/ppermute | solution.py:390
  47.5 0.9 %collective-permute-done.kv_other_ref = bf16[128,256]{1,0:T(8,128)(2,1)S(1)} collective-permute-done((bf16[128,256]{1,0:T(8,128)(2,1)S(1)}, bf16[128,256]{1,0:T(8,128)(2,1)S(1)}, u32[]{:S(2)}, u32[]{:S(2)}) %collective-permute-start) | collective-permute-done | bytes 65568 | tf_op jit(solution)/shard_map/ppermute | solution.py:390
  48.4 0.0 collective-permute-done.1.other_ref
  48.4 0.0 copy-done
  48.4 1.5 %shard_map.108 = (bf16[640,128]{1,0:T(8,128)(2,1)}, bf16[640,128]{1,0:T(8,128)(2,1)}, bf16[640,128]{1,0:T(8,128)(2,1)}, bf16[640,128]{1,0:T(8,128)(2,1)S(1)}, f32[8,128]{1,0:T(8,128)S(1)}) custom-call(bf16[128,256]{1,0:T(8,128)(2,1)S(1)} %add_convert_fusion.kv_ref, bf16[128,256]{1,0:T(8,128)(2,1)S(1)} %collective-permute-done.kv_other_ref, ...), custom_call_target="tpu_custom_call" | custom-call | flops 335544320 | bytes 4000000 | tf_op jit(solution)/shard_map/pallas_call | solution.py:419
  50.0 3.1 %collective-permute-start.3 = (bf16[640,128]{1,0:T(8,128)(2,1)}, bf16[640,128]{1,0:T(8,128)(2,1)S(1)}, u32[]{:S(2)}, u32[]{:S(2)}) collective-permute-start(bf16[640,128]{1,0:T(8,128)(2,1)} %get-tuple-element.30), channel_id=1, source_target_pairs={{0,2},{1,3},{2,4},{3,5},{4,6},{5,7},{6,0},{7,1},{8,10},{9,11},{10,... | collective-permute-start | bytes 491528 | tf_op jit(solution)/shard_map/ppermute | solution.py:431
  53.1 3.4 %collective-permute-start.4 = (bf16[640,128]{1,0:T(8,128)(2,1)}, bf16[640,128]{1,0:T(8,128)(2,1)S(1)}, u32[]{:S(2)}, u32[]{:S(2)}) collective-permute-start(bf16[640,128]{1,0:T(8,128)(2,1)} %get-tuple-element.31), channel_id=1, source_target_pairs={{0,6},{1,7},{2,0},{3,1},{4,2},{5,3},{6,4},{7,5},{8,14},{9,15},{10,... | collective-permute-start | bytes 491528 | tf_op jit(solution)/shard_map/ppermute | solution.py:431
  56.5 3.4 %collective-permute-start.5 = (bf16[640,128]{1,0:T(8,128)(2,1)}, bf16[640,128]{1,0:T(8,128)(2,1)S(1)}, u32[]{:S(2)}, u32[]{:S(2)}) collective-permute-start(bf16[640,128]{1,0:T(8,128)(2,1)} %get-tuple-element.32), channel_id=1, source_target_pairs={{0,4},{1,5},{2,6},{3,7},{4,0},{5,1},{6,2},{7,3},{8,12},{9,13},{10,... | collective-permute-start | bytes 491528 | tf_op jit(solution)/shard_map/ppermute | solution.py:431
  59.9 0.0 all-to-all-done.1
  59.9 0.2 shard_map.109.kv_ref
  60.1 3.1 %collective-permute-start.2 = (bf16[128,256]{1,0:T(8,128)(2,1)S(1)}, bf16[128,256]{1,0:T(8,128)(2,1)S(1)}, u32[]{:S(2)}, u32[]{:S(2)}) collective-permute-start(bf16[128,256]{1,0:T(8,128)(2,1)S(1)} %shard_map.109.kv_ref), channel_id=1, source_target_pairs={{0,1},{1,0},{2,3},{3,2},{4,5},{5,4},{6,7},{7,6},{8,9},{9,8},{10,11... | collective-permute-start | bytes 196616 | tf_op jit(solution)/shard_map/ppermute | solution.py:390
  63.3 1.0 %shard_map.107 = (bf16[256,640]{1,0:T(8,128)(2,1)}, f32[8,128]{1,0:T(8,128)S(1)}) custom-call(bf16[1024,128]{1,0:T(8,128)(2,1)S(1)} %bitcast.5, bf16[256,640]{1,0:T(8,128)(2,1)} %get-tuple-element.21.dq_in_ref), custom_call_target="tpu_custom_call", output_to_operand_aliasing={{0}: (1, {})} | custom-call | flops 100000000 | bytes 1000000 | tf_op jit(solution)/shard_map/pallas_call | solution.py:444
  64.2 0.0 collective-permute-done.2.kv_other_ref
  64.2 0.8 %shard_map.110 = bf16[4,640,128]{2,1,0:T(8,128)(2,1)S(1)} custom-call(bf16[128,256]{1,0:T(8,128)(2,1)S(1)} %shard_map.109.kv_ref, bf16[128,256]{1,0:T(8,128)(2,1)S(1)} %collective-permute-done.2.kv_other_ref, bf16[2,4,640,128]{3,2,1,0:T(8,128)(2,1)S(1)} %copy-done, bf16[2,4,640,128]{3,2,1,0:T(8,128)(2,1)S(1)} %collective-permute-done.1.other_ref, ...), custom_call_target="tpu_custom_call" | custom-call | flops 10000000 | bytes 4000000 | tf_op jit(solution)/shard_map/pallas_call | solution.py:454
  65.1 0.0 collective-permute-done.3.refs_1_
  65.1 0.0 collective-permute-done.4.refs_2_
  65.1 0.0 collective-permute-done.5.refs_3_
  65.1 11.8 %all_to_all.15.leaf_ref = bf16[4,640,128]{2,1,0:T(8,128)(2,1)S(1)} all-to-all(bf16[4,640,128]{2,1,0:T(8,128)(2,1)S(1)} %shard_map.110), channel_id=1, replica_groups={{0,2,4,6},{1,3,5,7},{8,10,12,14},{9,11,13,15},{16,18,20,22},{17,19,21,2..., dimensions={0} | all-to-all | bytes 1310720 | tf_op jit(solution)/shard_map/all_to_all | solution.py:463
  76.9 0.9 %shard_map.111 = bf16[256,640]{1,0:T(8,128)(2,1)} custom-call(bf16[4,640,128]{2,1,0:T(8,128)(2,1)S(1)} %all_to_all.15.leaf_ref, bf16[640,128]{1,0:T(8,128)(2,1)S(1)} %get-tuple-element.34.refs_0_, bf16[640,128]{1,0:T(8,128)(2,1)S(1)} %collective-permute-done.3.refs_1_, bf16[640,128]{1,0:T(8,128)(2,1)S(1)} %collective-permute-done.4.refs_2_, ...), custom_call_target="tpu_custom_call" | custom-call | flops 1000000 | bytes 1000000 | tf_op jit(solution)/shard_map/pallas_call | solution.py:471
  (1 shorter events, 0.0 us)
Async XLA Ops:
  3.1 31.8 %all-to-all-start = ((bf16[64,24,128]{2,1,0:T(8,128)(2,1)}), bf16[64,24,128]{2,1,0:T(8,128)(2,1)S(1)}, u32[]{:S(2)}, u32[]{:S(2)}) async-start(bf16[64,24,128]{2,1,0:T(8,128)(2,1)} %bitcast.7), calls=%async_computation | async-start | bytes 786432 | tf_op jit(solution)/shard_map/all_to_all | solution.py:352
  20.2 14.7 %copy-start.1 = (bf16[256,128]{1,0:T(8,128)(2,1)S(1)}, bf16[256,128]{1,0:T(8,128)(2,1)}, u32[]{:S(2)}) copy-start(bf16[256,128]{1,0:T(8,128)(2,1)} %k_in.1) | copy-start | bytes 196612
  20.2 14.7 %copy-start.2 = (bf16[256,128]{1,0:T(8,128)(2,1)S(1)}, bf16[256,128]{1,0:T(8,128)(2,1)}, u32[]{:S(2)}) copy-start(bf16[256,128]{1,0:T(8,128)(2,1)} %v_in.1) | copy-start | bytes 196612
  20.2 14.6 %copy-start.3 = (s32[64,64]{1,0:T(8,128)S(1)}, s32[64,64]{1,0:T(8,128)}, u32[]{:S(2)}) copy-start(s32[64,64]{1,0:T(8,128)} %leaf_tree_ref.3) | copy-start | bytes 49156
  20.3 14.6 %copy-start.4 = (s32[64,64]{1,0:T(8,128)S(1)}, s32[64,64]{1,0:T(8,128)}, u32[]{:S(2)}) copy-start(s32[64,64]{1,0:T(8,128)} %leaf_len_ref.1) | copy-start | bytes 49156
  20.3 14.6 %copy-start.5 = (s32[64]{0:T(128)S(1)}, s32[64]{0:T(128)}, u32[]{:S(2)}) copy-start(s32[64]{0:T(128)} %trunk_len_in.3) | copy-start | bytes 772
  25.4 23.0 %collective-permute-start.1 = (bf16[2,4,640,128]{3,2,1,0:T(8,128)(2,1)}, bf16[2,4,640,128]{3,2,1,0:T(8,128)(2,1)S(1)}, u32[]{:S(2)}, u32[]{:S(2)}) collective-permute-start(bf16[2,4,640,128]{3,2,1,0:T(8,128)(2,1)} %get-tuple-element.26), channel_id=1, source_target_pairs={{0,1},{1,0},{2,3},{3,2},{4,5},{5,4},{6,7},{7,6},{8,9},{9,8},{10,11... | collective-permute-start | bytes 3932168 | tf_op jit(solution)/shard_map/ppermute | solution.py:390
  34.9 9.1 %copy-start.6 = (f32[128,256]{1,0:T(8,128)S(1)}, f32[128,256]{1,0:T(8,128)}, u32[]{:S(2)}) copy-start(f32[128,256]{1,0:T(8,128)} %get-tuple-element.23) | copy-start | bytes 393220
  34.9 13.5 %copy-start = (bf16[2,4,640,128]{3,2,1,0:T(8,128)(2,1)S(1)}, bf16[2,4,640,128]{3,2,1,0:T(8,128)(2,1)}, u32[]{:S(2)}) copy-start(bf16[2,4,640,128]{3,2,1,0:T(8,128)(2,1)} %get-tuple-element.25.own_ref) | copy-start | bytes 3932164
  37.5 22.4 %all-to-all-start.1 = ((bf16[64,16,128]{2,1,0:T(8,128)(2,1)}), bf16[64,16,128]{2,1,0:T(8,128)(2,1)S(1)}, u32[]{:S(2)}, u32[]{:S(2)}) async-start(bf16[64,16,128]{2,1,0:T(8,128)(2,1)} %bitcast.2), calls=%async_computation.1 | async-start | bytes 524288 | tf_op jit(solution)/shard_map/all_to_all | solution.py:432
  44.1 4.3 %collective-permute-start = (bf16[128,256]{1,0:T(8,128)(2,1)S(1)}, bf16[128,256]{1,0:T(8,128)(2,1)S(1)}, u32[]{:S(2)}, u32[]{:S(2)}) collective-permute-start(bf16[128,256]{1,0:T(8,128)(2,1)S(1)} %add_convert_fusion.kv_ref), channel_id=1, source_target_pairs={{0,1},{1,0},{2,3},{3,2},{4,5},{5,4},{6,7},{7,6},{8,9},{9,8},{10,11... | collective-permute-start | bytes 196616 | tf_op jit(solution)/shard_map/ppermute | solution.py:390
  50.0 15.1 %collective-permute-start.3 = (bf16[640,128]{1,0:T(8,128)(2,1)}, bf16[640,128]{1,0:T(8,128)(2,1)S(1)}, u32[]{:S(2)}, u32[]{:S(2)}) collective-permute-start(bf16[640,128]{1,0:T(8,128)(2,1)} %get-tuple-element.30), channel_id=1, source_target_pairs={{0,2},{1,3},{2,4},{3,5},{4,6},{5,7},{6,0},{7,1},{8,10},{9,11},{10,... | collective-permute-start | bytes 491528 | tf_op jit(solution)/shard_map/ppermute | solution.py:431
  53.1 12.0 %collective-permute-start.4 = (bf16[640,128]{1,0:T(8,128)(2,1)}, bf16[640,128]{1,0:T(8,128)(2,1)S(1)}, u32[]{:S(2)}, u32[]{:S(2)}) collective-permute-start(bf16[640,128]{1,0:T(8,128)(2,1)} %get-tuple-element.31), channel_id=1, source_target_pairs={{0,6},{1,7},{2,0},{3,1},{4,2},{5,3},{6,4},{7,5},{8,14},{9,15},{10,... | collective-permute-start | bytes 491528 | tf_op jit(solution)/shard_map/ppermute | solution.py:431
  56.5 8.6 %collective-permute-start.5 = (bf16[640,128]{1,0:T(8,128)(2,1)}, bf16[640,128]{1,0:T(8,128)(2,1)S(1)}, u32[]{:S(2)}, u32[]{:S(2)}) collective-permute-start(bf16[640,128]{1,0:T(8,128)(2,1)} %get-tuple-element.32), channel_id=1, source_target_pairs={{0,4},{1,5},{2,6},{3,7},{4,0},{5,1},{6,2},{7,3},{8,12},{9,13},{10,... | collective-permute-start | bytes 491528 | tf_op jit(solution)/shard_map/ppermute | solution.py:431
  60.1 4.1 %collective-permute-start.2 = (bf16[128,256]{1,0:T(8,128)(2,1)S(1)}, bf16[128,256]{1,0:T(8,128)(2,1)S(1)}, u32[]{:S(2)}, u32[]{:S(2)}) collective-permute-start(bf16[128,256]{1,0:T(8,128)(2,1)S(1)} %shard_map.109.kv_ref), channel_id=1, source_target_pairs={{0,1},{1,0},{2,3},{3,2},{4,5},{5,4},{6,7},{7,6},{8,9},{9,8},{10,11... | collective-permute-start | bytes 196616 | tf_op jit(solution)/shard_map/ppermute | solution.py:390

commit v6 on v5

--- a/solution.py
+++ b/solution.py
@@ -64,9 +64,9 @@
     seg = lax.axis_index("seg")
     loads[0].wait()
     selector = leaf_selector(tree_ref, seg)
-    half = count // 2
+    half = count // 4
     stores = []
-    for part in range(2):
+    for part in range(4):
         at = part * half
         chosen = jnp.concatenate([selector[a * count + at : a * count + at + half, :] for a in range(LEAF)], axis=0)
         tile = 0
@@ -179,7 +179,7 @@
 
 def leaf_kernel(
     in_ref, k_ref, v_ref, leaf_tree_ref, leaf_len_ref, trunk_len_in,
-    out_ref, dkv_ref, rows_ref, back_ref, q_buf, g_buf, ds_buf, p_buf, out_buf, trunk_len_ref, sem, out_sem,
+    out_ref, dkv_ref, rows_ref, back_ref, q_buf, g_buf, ds_buf, p_buf, out_buf, trunk_len_ref, sem, out_sems,
 ):
     load = pltpu.make_async_copy(trunk_len_in, trunk_len_ref, sem)
     load.start()
@@ -220,12 +220,15 @@
     number = jnp.sum(jnp.where(leaf_tree_ref[...] == seg, leaf, 0), axis=1, keepdims=True).astype(f32)
     for spare in range(BACK_TILES * LEAF, BACK_ROWS):
         back_ref[pl.ds(spare, count, BACK_ROWS), :] = jnp.broadcast_to(number, (count, HEAD))
-    out_buf[...] = back_ref[...].astype(bf16)
-    store = pltpu.make_async_copy(out_buf, out_ref, out_sem)
-    store.start()
+    stores = []
+    for part in range(4):
+        rows = pl.ds(part * (count // 4) * BACK_ROWS, count // 4 * BACK_ROWS)
+        out_buf[rows, :] = back_ref[rows, :].astype(bf16)
+        stores += copies([(out_buf.at[rows, :], out_ref.at[rows, :])], out_sems.at[pl.ds(part, 1)])
     dkv_ref[:, 0:HEAD] = key_grad[0:TRUNK, :]
     dkv_ref[:, HEAD:] = value_grad[0:TRUNK, :]
-    store.wait()
+    for store in stores:
+        store.wait()
 
 
 def back_selector(rows_ref):
@@ -275,9 +278,13 @@
     stores = []
     for i, (even, odd) in enumerate(zip(steps[0] + (0,), steps[1] + (0,))):
         block = lax.rem(chip + even + core * (odd - even), chips)
-        buf[i] = chip_part(kv_ref, kv_other_ref, own_ref, other_ref, block)
-        stores.append(pltpu.make_async_copy(buf.at[i], outs[i], sems.at[i]))
-        stores[-1].start()
+        part = chip_part(kv_ref, kv_other_ref, own_ref, other_ref, block)
+        if i == count - 1:
+            outs[i][...] = part
+        else:
+            buf[i] = part
+            stores.append(pltpu.make_async_copy(buf.at[i], outs[i], sems.at[i]))
+            stores[-1].start()
     token_ref[...] = jnp.zeros(token_ref.shape, f32)
     for store in stores:
         store.wait()
@@ -343,7 +350,7 @@
             vm((count * OUT_ROWS, HEAD), f32),
             vm((count * OUT_ROWS, HEAD), bf16),
             dma((5,)),
-            dma((2,)),
+            dma((4,)),
         ],
         flops=10**8,
         moved=10**6,
@@ -406,7 +413,7 @@
             vm((count * BACK_ROWS, HEAD), bf16),
             pltpu.SMEM((count,), jnp.int32),
             dma,
-            dma,
+            dma((4,)),
         ],
         flops=4 * 10**10,
         moved=10**6,
@@ -420,8 +427,8 @@
         functools.partial(trunk_part_kernel, steps),
         [out(part_shape, bf16)] * chips + [out((8, HEAD), f32)],
         [vmem] * 4,
-        [hbm] * chips + [vmem],
-        [vm((chips,) + part_shape, bf16), dma((chips,))],
+        [hbm] * (chips - 1) + [vmem] * 2,
+        [vm((chips - 1,) + part_shape, bf16), dma((chips - 1,))],
         flops=part_flops,
         moved=4 * 10**6,
     )(trunk_kv, swap(trunk_kv), own, other)

time: 79.3 us -> 79.4 us (level)
  no operation moved by 1% of the time
where the time goes in v6:
time: 79.4 us; the launch traced here: 77.9 us
  starting transfers between devices  43 us (54%)
  Pallas kernels  14.5 us (18%)
  blocking collectives  11.8 us (15%)
  waiting for transfers between devices  7.54 us (9%)
  between operations  0.87 us (1%)
    all_to_all x1, starting transfers between devices, shards(): lax.all_to_all(send.reshape(count, OUT_ROWS, HEAD), 'seg', split_axis=0,...  17.1 us
    all_to_all x1, blocking collectives, shards(): lax.all_to_all(parts, 'kvh', split_axis=0, concat_axis=0, tiled=True, axi...  11.8 us
    ppermute x3, starting transfers between devices, shards(): trunk_came.append(lax.ppermute(trunk_parts[i], 'kvh', route))  9.93 us
    ppermute x3, starting transfers between devices, swap(): return lax.ppermute(value, 'kvh', [(i, i ^ 1) for i in range(heads)])  9.43 us
    all_to_all x1, waiting for transfers between devices, shards(): lax.all_to_all(send.reshape(count, OUT_ROWS, HEAD), 'seg', split_axis=0,...  6.64 us
    all_to_all x1, starting transfers between devices, shards(): lax.all_to_all(back.reshape(count, BACK_ROWS, HEAD), 'seg', split_axis=0,...  6.54 us
    pallas_call x1, Pallas kernels, shards(): call(trunk_kernel, [out(queries.shape, bf16), out((TRUNK, 2 * HEAD), f32)...  5.08 us
    pallas_call x1, Pallas kernels, shards(): call(leaf_kernel, [out((count * BACK_ROWS, HEAD), bf16), out((TRUNK, 2 *...  2.54 us
  transfers between devices with their start and end apart: 8, of which 2 were waited for; matrix products, arithmetic and copies ran while one was open for 0% of the time, Pallas kernels for 14%

profile of v6, /device:TPU:1, one launch (start us, length us, event | category | flops | bytes accessed | tf_op | source)
XLA Modules:
  0.0 77.9 jit_solution(14581449047850023519)
XLA Ops:
  0.6 2.5 %shard_map.104 = bf16[1536,128]{1,0:T(8,128)(2,1)} custom-call(bf16[256,640]{1,0:T(8,128)(2,1)} %q_in.1, bf16[256,640]{1,0:T(8,128)(2,1)} %g_in.1, bf16[256,128]{1,0:T(8,128)(2,1)} %k_in.1, bf16[256,128]{1,0:T(8,128)(2,1)} %v_in.1, s32[64,64]{1,0:T(8,128)} %leaf_tree_ref.3), custom_call_target="tpu_custom_call" | custom-call | flops 100000000 | bytes 1000000 | tf_op jit(solution)/shard_map/pallas_call | solution.py:339
  3.1 17.1 %all-to-all-start = ((bf16[64,24,128]{2,1,0:T(8,128)(2,1)}), bf16[64,24,128]{2,1,0:T(8,128)(2,1)S(1)}, u32[]{:S(2)}, u32[]{:S(2)}) async-start(bf16[64,24,128]{2,1,0:T(8,128)(2,1)} %bitcast.7), calls=%async_computation | async-start | bytes 786432 | tf_op jit(solution)/shard_map/all_to_all | solution.py:359
  20.3 0.0 copy-start.1
  20.3 0.0 copy-start.2
  20.3 0.0 copy-start.3
  20.3 0.0 copy-start.4
  20.3 0.0 copy-start.5
  20.3 5.1 %shard_map.106 = (bf16[256,640]{1,0:T(8,128)(2,1)}, f32[128,256]{1,0:T(8,128)}, bf16[2,4,640,128]{3,2,1,0:T(8,128)(2,1)}, bf16[2,4,640,128]{3,2,1,0:T(8,128)(2,1)}) custom-call(bf16[256,640]{1,0:T(8,128)(2,1)} %q_in.1, bf16[256,640]{1,0:T(8,128)(2,1)} %g_in.1, bf16[256,128]{1,0:T(8,128)(2,1)} %k_in.1, bf16[256,128]{1,0:T(8,128)(2,1)} %v_in.1, ...), custom_call_target="tpu_custom_call" | custom-call | flops 40000000000 | bytes 10000000 | tf_op jit(solution)/shard_map/pallas_call | solution.py:364
  25.4 2.9 %collective-permute-start.1 = (bf16[2,4,640,128]{3,2,1,0:T(8,128)(2,1)}, bf16[2,4,640,128]{3,2,1,0:T(8,128)(2,1)S(1)}, u32[]{:S(2)}, u32[]{:S(2)}) collective-permute-start(bf16[2,4,640,128]{3,2,1,0:T(8,128)(2,1)} %get-tuple-element.26), channel_id=1, source_target_pairs={{0,1},{1,0},{2,3},{3,2},{4,5},{5,4},{6,7},{7,6},{8,9},{9,8},{10,11... | collective-permute-start | bytes 3932168 | tf_op jit(solution)/shard_map/ppermute | solution.py:397
  28.3 6.6 %all-to-all-done = bf16[64,24,128]{2,1,0:T(8,128)(2,1)S(1)} async-done(((bf16[64,24,128]{2,1,0:T(8,128)(2,1)}), bf16[64,24,128]{2,1,0:T(8,128)(2,1)S(1)}, u32[]{:S(2)}, u32[]{:S(2)}) %all-to-all-start) | async-done | bytes 393248 | tf_op jit(solution)/shard_map/all_to_all | solution.py:359
  34.9 0.0 copy-done.1
  34.9 0.0 copy-done.2
  34.9 0.0 copy-done.3
  34.9 0.0 copy-done.4
  34.9 0.0 copy-done.5
  35.0 0.0 copy-start.6
  35.0 0.0 copy-start
  35.0 2.5 %shard_map.105 = (bf16[1024,128]{1,0:T(8,128)(2,1)}, f32[128,256]{1,0:T(8,128)S(1)}) custom-call(bf16[1536,128]{1,0:T(8,128)(2,1)S(1)} %bitcast.6, bf16[256,128]{1,0:T(8,128)(2,1)S(1)} %copy-done.1, bf16[256,128]{1,0:T(8,128)(2,1)S(1)} %copy-done.2, s32[64,64]{1,0:T(8,128)S(1)} %copy-done.3, s32[64,64]{1,0:T(8,128)S(1)} %copy-done.4, s32[64]{0:T(128)S(1)} %copy-done.5), custom_call_target="tpu_custom_call" | custom-call | flops 40000000000 | bytes 1000000 | tf_op jit(solution)/shard_map/pallas_call | solution.py:401
  37.5 6.5 %all-to-all-start.1 = ((bf16[64,16,128]{2,1,0:T(8,128)(2,1)}), bf16[64,16,128]{2,1,0:T(8,128)(2,1)S(1)}, u32[]{:S(2)}, u32[]{:S(2)}) async-start(bf16[64,16,128]{2,1,0:T(8,128)(2,1)} %bitcast.2), calls=%async_computation.1 | async-start | bytes 524288 | tf_op jit(solution)/shard_map/all_to_all | solution.py:439
  44.1 0.0 copy-done.6
  44.1 3.5 %collective-permute-start = (bf16[128,256]{1,0:T(8,128)(2,1)S(1)}, bf16[128,256]{1,0:T(8,128)(2,1)S(1)}, u32[]{:S(2)}, u32[]{:S(2)}) collective-permute-start(bf16[128,256]{1,0:T(8,128)(2,1)S(1)} %add_convert_fusion.kv_ref), channel_id=1, source_target_pairs={{0,1},{1,0},{2,3},{3,2},{4,5},{5,4},{6,7},{7,6},{8,9},{9,8},{10,11... | collective-permute-start | bytes 196616 | tf_op jit(solution)/shard_map/ppermute | solution.py:397
  47.6 0.9 %collective-permute-done.kv_other_ref = bf16[128,256]{1,0:T(8,128)(2,1)S(1)} collective-permute-done((bf16[128,256]{1,0:T(8,128)(2,1)S(1)}, bf16[128,256]{1,0:T(8,128)(2,1)S(1)}, u32[]{:S(2)}, u32[]{:S(2)}) %collective-permute-start) | collective-permute-done | bytes 65568 | tf_op jit(solution)/shard_map/ppermute | solution.py:397
  48.5 0.0 collective-permute-done.1.other_ref
  48.5 0.0 copy-done
  48.5 1.5 %shard_map.108 = (bf16[640,128]{1,0:T(8,128)(2,1)}, bf16[640,128]{1,0:T(8,128)(2,1)}, bf16[640,128]{1,0:T(8,128)(2,1)}, bf16[640,128]{1,0:T(8,128)(2,1)S(1)}, f32[8,128]{1,0:T(8,128)S(1)}) custom-call(bf16[128,256]{1,0:T(8,128)(2,1)S(1)} %add_convert_fusion.kv_ref, bf16[128,256]{1,0:T(8,128)(2,1)S(1)} %collective-permute-done.kv_other_ref, ...), custom_call_target="tpu_custom_call" | custom-call | flops 335544320 | bytes 4000000 | tf_op jit(solution)/shard_map/pallas_call | solution.py:426
  50.0 3.1 %collective-permute-start.3 = (bf16[640,128]{1,0:T(8,128)(2,1)}, bf16[640,128]{1,0:T(8,128)(2,1)S(1)}, u32[]{:S(2)}, u32[]{:S(2)}) collective-permute-start(bf16[640,128]{1,0:T(8,128)(2,1)} %get-tuple-element.30), channel_id=1, source_target_pairs={{0,2},{1,3},{2,4},{3,5},{4,6},{5,7},{6,0},{7,1},{8,10},{9,11},{10,... | collective-permute-start | bytes 491528 | tf_op jit(solution)/shard_map/ppermute | solution.py:438
  53.1 3.4 %collective-permute-start.4 = (bf16[640,128]{1,0:T(8,128)(2,1)}, bf16[640,128]{1,0:T(8,128)(2,1)S(1)}, u32[]{:S(2)}, u32[]{:S(2)}) collective-permute-start(bf16[640,128]{1,0:T(8,128)(2,1)} %get-tuple-element.31), channel_id=1, source_target_pairs={{0,6},{1,7},{2,0},{3,1},{4,2},{5,3},{6,4},{7,5},{8,14},{9,15},{10,... | collective-permute-start | bytes 491528 | tf_op jit(solution)/shard_map/ppermute | solution.py:438
  56.5 3.4 %collective-permute-start.5 = (bf16[640,128]{1,0:T(8,128)(2,1)}, bf16[640,128]{1,0:T(8,128)(2,1)S(1)}, u32[]{:S(2)}, u32[]{:S(2)}) collective-permute-start(bf16[640,128]{1,0:T(8,128)(2,1)} %get-tuple-element.32), channel_id=1, source_target_pairs={{0,4},{1,5},{2,6},{3,7},{4,0},{5,1},{6,2},{7,3},{8,12},{9,13},{10,... | collective-permute-start | bytes 491528 | tf_op jit(solution)/shard_map/ppermute | solution.py:438
  60.0 0.0 all-to-all-done.1
  60.0 0.2 shard_map.109.kv_ref
  60.2 3.1 %collective-permute-start.2 = (bf16[128,256]{1,0:T(8,128)(2,1)S(1)}, bf16[128,256]{1,0:T(8,128)(2,1)S(1)}, u32[]{:S(2)}, u32[]{:S(2)}) collective-permute-start(bf16[128,256]{1,0:T(8,128)(2,1)S(1)} %shard_map.109.kv_ref), channel_id=1, source_target_pairs={{0,1},{1,0},{2,3},{3,2},{4,5},{5,4},{6,7},{7,6},{8,9},{9,8},{10,11... | collective-permute-start | bytes 196616 | tf_op jit(solution)/shard_map/ppermute | solution.py:397
  63.3 1.0 %shard_map.107 = (bf16[256,640]{1,0:T(8,128)(2,1)}, f32[8,128]{1,0:T(8,128)S(1)}) custom-call(bf16[1024,128]{1,0:T(8,128)(2,1)S(1)} %bitcast.5, bf16[256,640]{1,0:T(8,128)(2,1)} %get-tuple-element.21.dq_in_ref), custom_call_target="tpu_custom_call", output_to_operand_aliasing={{0}: (1, {})} | custom-call | flops 100000000 | bytes 1000000 | tf_op jit(solution)/shard_map/pallas_call | solution.py:451
  64.3 0.0 collective-permute-done.2.kv_other_ref
  64.3 0.8 %shard_map.110 = bf16[4,640,128]{2,1,0:T(8,128)(2,1)S(1)} custom-call(bf16[128,256]{1,0:T(8,128)(2,1)S(1)} %shard_map.109.kv_ref, bf16[128,256]{1,0:T(8,128)(2,1)S(1)} %collective-permute-done.2.kv_other_ref, bf16[2,4,640,128]{3,2,1,0:T(8,128)(2,1)S(1)} %copy-done, bf16[2,4,640,128]{3,2,1,0:T(8,128)(2,1)S(1)} %collective-permute-done.1.other_ref, ...), custom_call_target="tpu_custom_call" | custom-call | flops 10000000 | bytes 4000000 | tf_op jit(solution)/shard_map/pallas_call | solution.py:461
  65.1 0.0 collective-permute-done.3.refs_1_
  65.1 0.0 collective-permute-done.4.refs_2_
  65.1 0.0 collective-permute-done.5.refs_3_
  65.2 11.8 %all_to_all.15.leaf_ref = bf16[4,640,128]{2,1,0:T(8,128)(2,1)S(1)} all-to-all(bf16[4,640,128]{2,1,0:T(8,128)(2,1)S(1)} %shard_map.110), channel_id=1, replica_groups={{0,2,4,6},{1,3,5,7},{8,10,12,14},{9,11,13,15},{16,18,20,22},{17,19,21,2..., dimensions={0} | all-to-all | bytes 1310720 | tf_op jit(solution)/shard_map/all_to_all | solution.py:470
  77.0 0.9 %shard_map.111 = bf16[256,640]{1,0:T(8,128)(2,1)} custom-call(bf16[4,640,128]{2,1,0:T(8,128)(2,1)S(1)} %all_to_all.15.leaf_ref, bf16[640,128]{1,0:T(8,128)(2,1)S(1)} %get-tuple-element.34.refs_0_, bf16[640,128]{1,0:T(8,128)(2,1)S(1)} %collective-permute-done.3.refs_1_, bf16[640,128]{1,0:T(8,128)(2,1)S(1)} %collective-permute-done.4.refs_2_, ...), custom_call_target="tpu_custom_call" | custom-call | flops 1000000 | bytes 1000000 | tf_op jit(solution)/shard_map/pallas_call | solution.py:478
  (1 shorter events, 0.0 us)
Async XLA Ops:
  3.1 31.8 %all-to-all-start = ((bf16[64,24,128]{2,1,0:T(8,128)(2,1)}), bf16[64,24,128]{2,1,0:T(8,128)(2,1)S(1)}, u32[]{:S(2)}, u32[]{:S(2)}) async-start(bf16[64,24,128]{2,1,0:T(8,128)(2,1)} %bitcast.7), calls=%async_computation | async-start | bytes 786432 | tf_op jit(solution)/shard_map/all_to_all | solution.py:359
  20.3 14.7 %copy-start.1 = (bf16[256,128]{1,0:T(8,128)(2,1)S(1)}, bf16[256,128]{1,0:T(8,128)(2,1)}, u32[]{:S(2)}) copy-start(bf16[256,128]{1,0:T(8,128)(2,1)} %k_in.1) | copy-start | bytes 196612
  20.3 14.7 %copy-start.2 = (bf16[256,128]{1,0:T(8,128)(2,1)S(1)}, bf16[256,128]{1,0:T(8,128)(2,1)}, u32[]{:S(2)}) copy-start(bf16[256,128]{1,0:T(8,128)(2,1)} %v_in.1) | copy-start | bytes 196612
  20.3 14.6 %copy-start.3 = (s32[64,64]{1,0:T(8,128)S(1)}, s32[64,64]{1,0:T(8,128)}, u32[]{:S(2)}) copy-start(s32[64,64]{1,0:T(8,128)} %leaf_tree_ref.3) | copy-start | bytes 49156
  20.3 14.6 %copy-start.4 = (s32[64,64]{1,0:T(8,128)S(1)}, s32[64,64]{1,0:T(8,128)}, u32[]{:S(2)}) copy-start(s32[64,64]{1,0:T(8,128)} %leaf_len_ref.1) | copy-start | bytes 49156
  20.3 14.6 %copy-start.5 = (s32[64]{0:T(128)S(1)}, s32[64]{0:T(128)}, u32[]{:S(2)}) copy-start(s32[64]{0:T(128)} %trunk_len_in.3) | copy-start | bytes 772
  25.4 23.1 %collective-permute-start.1 = (bf16[2,4,640,128]{3,2,1,0:T(8,128)(2,1)}, bf16[2,4,640,128]{3,2,1,0:T(8,128)(2,1)S(1)}, u32[]{:S(2)}, u32[]{:S(2)}) collective-permute-start(bf16[2,4,640,128]{3,2,1,0:T(8,128)(2,1)} %get-tuple-element.26), channel_id=1, source_target_pairs={{0,1},{1,0},{2,3},{3,2},{4,5},{5,4},{6,7},{7,6},{8,9},{9,8},{10,11... | collective-permute-start | bytes 3932168 | tf_op jit(solution)/shard_map/ppermute | solution.py:397
  35.0 9.1 %copy-start.6 = (f32[128,256]{1,0:T(8,128)S(1)}, f32[128,256]{1,0:T(8,128)}, u32[]{:S(2)}) copy-start(f32[128,256]{1,0:T(8,128)} %get-tuple-element.23) | copy-start | bytes 393220
  35.0 13.5 %copy-start = (bf16[2,4,640,128]{3,2,1,0:T(8,128)(2,1)S(1)}, bf16[2,4,640,128]{3,2,1,0:T(8,128)(2,1)}, u32[]{:S(2)}) copy-start(bf16[2,4,640,128]{3,2,1,0:T(8,128)(2,1)} %get-tuple-element.25.own_ref) | copy-start | bytes 3932164
  37.5 22.4 %all-to-all-start.1 = ((bf16[64,16,128]{2,1,0:T(8,128)(2,1)}), bf16[64,16,128]{2,1,0:T(8,128)(2,1)S(1)}, u32[]{:S(2)}, u32[]{:S(2)}) async-start(bf16[64,16,128]{2,1,0:T(8,128)(2,1)} %bitcast.2), calls=%async_computation.1 | async-start | bytes 524288 | tf_op jit(solution)/shard_map/all_to_all | solution.py:439
  44.1 4.4 %collective-permute-start = (bf16[128,256]{1,0:T(8,128)(2,1)S(1)}, bf16[128,256]{1,0:T(8,128)(2,1)S(1)}, u32[]{:S(2)}, u32[]{:S(2)}) collective-permute-start(bf16[128,256]{1,0:T(8,128)(2,1)S(1)} %add_convert_fusion.kv_ref), channel_id=1, source_target_pairs={{0,1},{1,0},{2,3},{3,2},{4,5},{5,4},{6,7},{7,6},{8,9},{9,8},{10,11... | collective-permute-start | bytes 196616 | tf_op jit(solution)/shard_map/ppermute | solution.py:397
  50.0 15.1 %collective-permute-start.3 = (bf16[640,128]{1,0:T(8,128)(2,1)}, bf16[640,128]{1,0:T(8,128)(2,1)S(1)}, u32[]{:S(2)}, u32[]{:S(2)}) collective-permute-start(bf16[640,128]{1,0:T(8,128)(2,1)} %get-tuple-element.30), channel_id=1, source_target_pairs={{0,2},{1,3},{2,4},{3,5},{4,6},{5,7},{6,0},{7,1},{8,10},{9,11},{10,... | collective-permute-start | bytes 491528 | tf_op jit(solution)/shard_map/ppermute | solution.py:438
  53.1 12.0 %collective-permute-start.4 = (bf16[640,128]{1,0:T(8,128)(2,1)}, bf16[640,128]{1,0:T(8,128)(2,1)S(1)}, u32[]{:S(2)}, u32[]{:S(2)}) collective-permute-start(bf16[640,128]{1,0:T(8,128)(2,1)} %get-tuple-element.31), channel_id=1, source_target_pairs={{0,6},{1,7},{2,0},{3,1},{4,2},{5,3},{6,4},{7,5},{8,14},{9,15},{10,... | collective-permute-start | bytes 491528 | tf_op jit(solution)/shard_map/ppermute | solution.py:438
  56.5 8.6 %collective-permute-start.5 = (bf16[640,128]{1,0:T(8,128)(2,1)}, bf16[640,128]{1,0:T(8,128)(2,1)S(1)}, u32[]{:S(2)}, u32[]{:S(2)}) collective-permute-start(bf16[640,128]{1,0:T(8,128)(2,1)} %get-tuple-element.32), channel_id=1, source_target_pairs={{0,4},{1,5},{2,6},{3,7},{4,0},{5,1},{6,2},{7,3},{8,12},{9,13},{10,... | collective-permute-start | bytes 491528 | tf_op jit(solution)/shard_map/ppermute | solution.py:438
  60.2 4.1 %collective-permute-start.2 = (bf16[128,256]{1,0:T(8,128)(2,1)S(1)}, bf16[128,256]{1,0:T(8,128)(2,1)S(1)}, u32[]{:S(2)}, u32[]{:S(2)}) collective-permute-start(bf16[128,256]{1,0:T(8,128)(2,1)S(1)} %shard_map.109.kv_ref), channel_id=1, source_target_pairs={{0,1},{1,0},{2,3},{3,2},{4,5},{5,4},{6,7},{7,6},{8,9},{9,8},{10,11... | collective-permute-start | bytes 196616 | tf_op jit(solution)/shard_map/ppermute | solution.py:397

commit v7 on v6

--- a/solution.py
+++ b/solution.py
@@ -297,15 +297,19 @@
 
 def hidden_kernel(leaf_ref, *refs):
     trunk_refs, (out_ref, buf, sems) = refs[:-3], refs[-3:]
+    columns = buf.shape[1]
+    middle = columns // 256 * HEAD
     stores = []
-    for i, parts in enumerate(([ref[...] for ref in trunk_refs], [leaf_ref[chip] for chip in range(leaf_ref.shape[0])])):
-        total = parts[0].astype(f32)
-        for part in parts[1:]:
-            total += part.astype(f32)
+    for i, parts in enumerate((trunk_refs, [leaf_ref.at[chip] for chip in range(leaf_ref.shape[0])])):
         rows = pl.ds(i * TRUNK, TRUNK)
-        buf[rows, :] = total.astype(bf16).T
-        stores.append(pltpu.make_async_copy(buf.at[rows, :], out_ref.at[rows, :], sems.at[i]))
-        stores[-1].start()
+        for at, width in ((0, middle), (middle, columns - middle)):
+            features = pl.ds(at, width)
+            total = parts[0][features, :].astype(f32)
+            for part in parts[1:]:
+                total += part[features, :].astype(f32)
+            buf[rows, features] = total.astype(bf16).T
+            pair = (buf.at[rows, features], out_ref.at[rows, features])
+            stores += copies([pair], sems.at[pl.ds(len(stores), 1)])
     for store in stores:
         store.wait()
 
@@ -480,7 +484,7 @@
         out((TRUNK + leaf_rows, columns), bf16),
         [vmem] * (1 + chips),
         hbm,
-        [vm((TRUNK + leaf_rows, columns), bf16), dma((2,))],
+        [vm((TRUNK + leaf_rows, columns), bf16), dma((4,))],
         flops=10**6,
         moved=10**6,
     )(came, *trunk_came)

time: 79.4 us -> 79.4 us (level)
  no operation moved by 1% of the time
where the time goes in v7:
time: 79.4 us; the launch traced here: 77.9 us
  starting transfers between devices  43 us (54%)
  Pallas kernels  14.5 us (18%)
  blocking collectives  11.8 us (15%)
  waiting for transfers between devices  7.54 us (9%)
  between operations  0.87 us (1%)
    all_to_all x1, starting transfers between devices, shards(): lax.all_to_all(send.reshape(count, OUT_ROWS, HEAD), 'seg', split_axis=0,...  17.1 us
    all_to_all x1, blocking collectives, shards(): lax.all_to_all(parts, 'kvh', split_axis=0, concat_axis=0, tiled=True, axi...  11.8 us
    ppermute x3, starting transfers between devices, shards(): trunk_came.append(lax.ppermute(trunk_parts[i], 'kvh', route))  9.93 us
    ppermute x3, starting transfers between devices, swap(): return lax.ppermute(value, 'kvh', [(i, i ^ 1) for i in range(heads)])  9.43 us
    all_to_all x1, waiting for transfers between devices, shards(): lax.all_to_all(send.reshape(count, OUT_ROWS, HEAD), 'seg', split_axis=0,...  6.64 us
    all_to_all x1, starting transfers between devices, shards(): lax.all_to_all(back.reshape(count, BACK_ROWS, HEAD), 'seg', split_axis=0,...  6.54 us
    pallas_call x1, Pallas kernels, shards(): call(trunk_kernel, [out(queries.shape, bf16), out((TRUNK, 2 * HEAD), f32)...  5.08 us
    pallas_call x1, Pallas kernels, shards(): call(leaf_kernel, [out((count * BACK_ROWS, HEAD), bf16), out((TRUNK, 2 *...  2.54 us
  transfers between devices with their start and end apart: 8, of which 2 were waited for; matrix products, arithmetic and copies ran while one was open for 0% of the time, Pallas kernels for 14%

profile of v7, /device:TPU:1, one launch (start us, length us, event | category | flops | bytes accessed | tf_op | source)
XLA Modules:
  0.0 77.9 jit_solution(1035265187118713966)
XLA Ops:
  0.6 2.5 %shard_map.104 = bf16[1536,128]{1,0:T(8,128)(2,1)} custom-call(bf16[256,640]{1,0:T(8,128)(2,1)} %q_in.1, bf16[256,640]{1,0:T(8,128)(2,1)} %g_in.1, bf16[256,128]{1,0:T(8,128)(2,1)} %k_in.1, bf16[256,128]{1,0:T(8,128)(2,1)} %v_in.1, s32[64,64]{1,0:T(8,128)} %leaf_tree_ref.3), custom_call_target="tpu_custom_call" | custom-call | flops 100000000 | bytes 1000000 | tf_op jit(solution)/shard_map/pallas_call | solution.py:343
  3.1 17.1 %all-to-all-start = ((bf16[64,24,128]{2,1,0:T(8,128)(2,1)}), bf16[64,24,128]{2,1,0:T(8,128)(2,1)S(1)}, u32[]{:S(2)}, u32[]{:S(2)}) async-start(bf16[64,24,128]{2,1,0:T(8,128)(2,1)} %bitcast.7), calls=%async_computation | async-start | bytes 786432 | tf_op jit(solution)/shard_map/all_to_all | solution.py:363
  20.3 0.0 copy-start.1
  20.3 0.0 copy-start.2
  20.3 0.0 copy-start.3
  20.3 0.0 copy-start.4
  20.3 0.0 copy-start.5
  20.3 5.1 %shard_map.106 = (bf16[256,640]{1,0:T(8,128)(2,1)}, f32[128,256]{1,0:T(8,128)}, bf16[2,4,640,128]{3,2,1,0:T(8,128)(2,1)}, bf16[2,4,640,128]{3,2,1,0:T(8,128)(2,1)}) custom-call(bf16[256,640]{1,0:T(8,128)(2,1)} %q_in.1, bf16[256,640]{1,0:T(8,128)(2,1)} %g_in.1, bf16[256,128]{1,0:T(8,128)(2,1)} %k_in.1, bf16[256,128]{1,0:T(8,128)(2,1)} %v_in.1, ...), custom_call_target="tpu_custom_call" | custom-call | flops 40000000000 | bytes 10000000 | tf_op jit(solution)/shard_map/pallas_call | solution.py:368
  25.4 2.9 %collective-permute-start.1 = (bf16[2,4,640,128]{3,2,1,0:T(8,128)(2,1)}, bf16[2,4,640,128]{3,2,1,0:T(8,128)(2,1)S(1)}, u32[]{:S(2)}, u32[]{:S(2)}) collective-permute-start(bf16[2,4,640,128]{3,2,1,0:T(8,128)(2,1)} %get-tuple-element.26), channel_id=1, source_target_pairs={{0,1},{1,0},{2,3},{3,2},{4,5},{5,4},{6,7},{7,6},{8,9},{9,8},{10,11... | collective-permute-start | bytes 3932168 | tf_op jit(solution)/shard_map/ppermute | solution.py:401
  28.3 6.6 %all-to-all-done = bf16[64,24,128]{2,1,0:T(8,128)(2,1)S(1)} async-done(((bf16[64,24,128]{2,1,0:T(8,128)(2,1)}), bf16[64,24,128]{2,1,0:T(8,128)(2,1)S(1)}, u32[]{:S(2)}, u32[]{:S(2)}) %all-to-all-start) | async-done | bytes 393248 | tf_op jit(solution)/shard_map/all_to_all | solution.py:363
  34.9 0.0 copy-done.1
  34.9 0.0 copy-done.2
  34.9 0.0 copy-done.3
  34.9 0.0 copy-done.4
  34.9 0.0 copy-done.5
  35.0 0.0 copy-start.6
  35.0 0.0 copy-start
  35.0 2.5 %shard_map.105 = (bf16[1024,128]{1,0:T(8,128)(2,1)}, f32[128,256]{1,0:T(8,128)S(1)}) custom-call(bf16[1536,128]{1,0:T(8,128)(2,1)S(1)} %bitcast.6, bf16[256,128]{1,0:T(8,128)(2,1)S(1)} %copy-done.1, bf16[256,128]{1,0:T(8,128)(2,1)S(1)} %copy-done.2, s32[64,64]{1,0:T(8,128)S(1)} %copy-done.3, s32[64,64]{1,0:T(8,128)S(1)} %copy-done.4, s32[64]{0:T(128)S(1)} %copy-done.5), custom_call_target="tpu_custom_call" | custom-call | flops 40000000000 | bytes 1000000 | tf_op jit(solution)/shard_map/pallas_call | solution.py:405
  37.5 6.5 %all-to-all-start.1 = ((bf16[64,16,128]{2,1,0:T(8,128)(2,1)}), bf16[64,16,128]{2,1,0:T(8,128)(2,1)S(1)}, u32[]{:S(2)}, u32[]{:S(2)}) async-start(bf16[64,16,128]{2,1,0:T(8,128)(2,1)} %bitcast.2), calls=%async_computation.1 | async-start | bytes 524288 | tf_op jit(solution)/shard_map/all_to_all | solution.py:443
  44.1 0.0 copy-done.6
  44.1 3.5 %collective-permute-start = (bf16[128,256]{1,0:T(8,128)(2,1)S(1)}, bf16[128,256]{1,0:T(8,128)(2,1)S(1)}, u32[]{:S(2)}, u32[]{:S(2)}) collective-permute-start(bf16[128,256]{1,0:T(8,128)(2,1)S(1)} %add_convert_fusion.kv_ref), channel_id=1, source_target_pairs={{0,1},{1,0},{2,3},{3,2},{4,5},{5,4},{6,7},{7,6},{8,9},{9,8},{10,11... | collective-permute-start | bytes 196616 | tf_op jit(solution)/shard_map/ppermute | solution.py:401
  47.6 0.9 %collective-permute-done.kv_other_ref = bf16[128,256]{1,0:T(8,128)(2,1)S(1)} collective-permute-done((bf16[128,256]{1,0:T(8,128)(2,1)S(1)}, bf16[128,256]{1,0:T(8,128)(2,1)S(1)}, u32[]{:S(2)}, u32[]{:S(2)}) %collective-permute-start) | collective-permute-done | bytes 65568 | tf_op jit(solution)/shard_map/ppermute | solution.py:401
  48.5 0.0 collective-permute-done.1.other_ref
  48.5 0.0 copy-done
  48.5 1.5 %shard_map.108 = (bf16[640,128]{1,0:T(8,128)(2,1)}, bf16[640,128]{1,0:T(8,128)(2,1)}, bf16[640,128]{1,0:T(8,128)(2,1)}, bf16[640,128]{1,0:T(8,128)(2,1)S(1)}, f32[8,128]{1,0:T(8,128)S(1)}) custom-call(bf16[128,256]{1,0:T(8,128)(2,1)S(1)} %add_convert_fusion.kv_ref, bf16[128,256]{1,0:T(8,128)(2,1)S(1)} %collective-permute-done.kv_other_ref, ...), custom_call_target="tpu_custom_call" | custom-call | flops 335544320 | bytes 4000000 | tf_op jit(solution)/shard_map/pallas_call | solution.py:430
  50.0 3.1 %collective-permute-start.3 = (bf16[640,128]{1,0:T(8,128)(2,1)}, bf16[640,128]{1,0:T(8,128)(2,1)S(1)}, u32[]{:S(2)}, u32[]{:S(2)}) collective-permute-start(bf16[640,128]{1,0:T(8,128)(2,1)} %get-tuple-element.30), channel_id=1, source_target_pairs={{0,2},{1,3},{2,4},{3,5},{4,6},{5,7},{6,0},{7,1},{8,10},{9,11},{10,... | collective-permute-start | bytes 491528 | tf_op jit(solution)/shard_map/ppermute | solution.py:442
  53.1 3.4 %collective-permute-start.4 = (bf16[640,128]{1,0:T(8,128)(2,1)}, bf16[640,128]{1,0:T(8,128)(2,1)S(1)}, u32[]{:S(2)}, u32[]{:S(2)}) collective-permute-start(bf16[640,128]{1,0:T(8,128)(2,1)} %get-tuple-element.31), channel_id=1, source_target_pairs={{0,6},{1,7},{2,0},{3,1},{4,2},{5,3},{6,4},{7,5},{8,14},{9,15},{10,... | collective-permute-start | bytes 491528 | tf_op jit(solution)/shard_map/ppermute | solution.py:442
  56.5 3.4 %collective-permute-start.5 = (bf16[640,128]{1,0:T(8,128)(2,1)}, bf16[640,128]{1,0:T(8,128)(2,1)S(1)}, u32[]{:S(2)}, u32[]{:S(2)}) collective-permute-start(bf16[640,128]{1,0:T(8,128)(2,1)} %get-tuple-element.32), channel_id=1, source_target_pairs={{0,4},{1,5},{2,6},{3,7},{4,0},{5,1},{6,2},{7,3},{8,12},{9,13},{10,... | collective-permute-start | bytes 491528 | tf_op jit(solution)/shard_map/ppermute | solution.py:442
  60.0 0.0 all-to-all-done.1
  60.0 0.2 shard_map.109.kv_ref
  60.2 3.1 %collective-permute-start.2 = (bf16[128,256]{1,0:T(8,128)(2,1)S(1)}, bf16[128,256]{1,0:T(8,128)(2,1)S(1)}, u32[]{:S(2)}, u32[]{:S(2)}) collective-permute-start(bf16[128,256]{1,0:T(8,128)(2,1)S(1)} %shard_map.109.kv_ref), channel_id=1, source_target_pairs={{0,1},{1,0},{2,3},{3,2},{4,5},{5,4},{6,7},{7,6},{8,9},{9,8},{10,11... | collective-permute-start | bytes 196616 | tf_op jit(solution)/shard_map/ppermute | solution.py:401
  63.3 1.0 %shard_map.107 = (bf16[256,640]{1,0:T(8,128)(2,1)}, f32[8,128]{1,0:T(8,128)S(1)}) custom-call(bf16[1024,128]{1,0:T(8,128)(2,1)S(1)} %bitcast.5, bf16[256,640]{1,0:T(8,128)(2,1)} %get-tuple-element.21.dq_in_ref), custom_call_target="tpu_custom_call", output_to_operand_aliasing={{0}: (1, {})} | custom-call | flops 100000000 | bytes 1000000 | tf_op jit(solution)/shard_map/pallas_call | solution.py:455
  64.3 0.0 collective-permute-done.2.kv_other_ref
  64.3 0.8 %shard_map.110 = bf16[4,640,128]{2,1,0:T(8,128)(2,1)S(1)} custom-call(bf16[128,256]{1,0:T(8,128)(2,1)S(1)} %shard_map.109.kv_ref, bf16[128,256]{1,0:T(8,128)(2,1)S(1)} %collective-permute-done.2.kv_other_ref, bf16[2,4,640,128]{3,2,1,0:T(8,128)(2,1)S(1)} %copy-done, bf16[2,4,640,128]{3,2,1,0:T(8,128)(2,1)S(1)} %collective-permute-done.1.other_ref, ...), custom_call_target="tpu_custom_call" | custom-call | flops 10000000 | bytes 4000000 | tf_op jit(solution)/shard_map/pallas_call | solution.py:465
  65.1 0.0 collective-permute-done.3.refs_1_
  65.1 0.0 collective-permute-done.4.refs_2_
  65.1 0.0 collective-permute-done.5.refs_3_
  65.2 11.8 %all_to_all.15.leaf_ref = bf16[4,640,128]{2,1,0:T(8,128)(2,1)S(1)} all-to-all(bf16[4,640,128]{2,1,0:T(8,128)(2,1)S(1)} %shard_map.110), channel_id=1, replica_groups={{0,2,4,6},{1,3,5,7},{8,10,12,14},{9,11,13,15},{16,18,20,22},{17,19,21,2..., dimensions={0} | all-to-all | bytes 1310720 | tf_op jit(solution)/shard_map/all_to_all | solution.py:474
  77.0 0.9 %shard_map.111 = bf16[256,640]{1,0:T(8,128)(2,1)} custom-call(bf16[4,640,128]{2,1,0:T(8,128)(2,1)S(1)} %all_to_all.15.leaf_ref, bf16[640,128]{1,0:T(8,128)(2,1)S(1)} %get-tuple-element.34.refs_0_, bf16[640,128]{1,0:T(8,128)(2,1)S(1)} %collective-permute-done.3.refs_1_, bf16[640,128]{1,0:T(8,128)(2,1)S(1)} %collective-permute-done.4.refs_2_, ...), custom_call_target="tpu_custom_call" | custom-call | flops 1000000 | bytes 1000000 | tf_op jit(solution)/shard_map/pallas_call | solution.py:482
  (1 shorter events, 0.0 us)
Async XLA Ops:
  3.1 31.8 %all-to-all-start = ((bf16[64,24,128]{2,1,0:T(8,128)(2,1)}), bf16[64,24,128]{2,1,0:T(8,128)(2,1)S(1)}, u32[]{:S(2)}, u32[]{:S(2)}) async-start(bf16[64,24,128]{2,1,0:T(8,128)(2,1)} %bitcast.7), calls=%async_computation | async-start | bytes 786432 | tf_op jit(solution)/shard_map/all_to_all | solution.py:363
  20.3 14.7 %copy-start.1 = (bf16[256,128]{1,0:T(8,128)(2,1)S(1)}, bf16[256,128]{1,0:T(8,128)(2,1)}, u32[]{:S(2)}) copy-start(bf16[256,128]{1,0:T(8,128)(2,1)} %k_in.1) | copy-start | bytes 196612
  20.3 14.7 %copy-start.2 = (bf16[256,128]{1,0:T(8,128)(2,1)S(1)}, bf16[256,128]{1,0:T(8,128)(2,1)}, u32[]{:S(2)}) copy-start(bf16[256,128]{1,0:T(8,128)(2,1)} %v_in.1) | copy-start | bytes 196612
  20.3 14.6 %copy-start.3 = (s32[64,64]{1,0:T(8,128)S(1)}, s32[64,64]{1,0:T(8,128)}, u32[]{:S(2)}) copy-start(s32[64,64]{1,0:T(8,128)} %leaf_tree_ref.3) | copy-start | bytes 49156
  20.3 14.6 %copy-start.4 = (s32[64,64]{1,0:T(8,128)S(1)}, s32[64,64]{1,0:T(8,128)}, u32[]{:S(2)}) copy-start(s32[64,64]{1,0:T(8,128)} %leaf_len_ref.1) | copy-start | bytes 49156
  20.3 14.6 %copy-start.5 = (s32[64]{0:T(128)S(1)}, s32[64]{0:T(128)}, u32[]{:S(2)}) copy-start(s32[64]{0:T(128)} %trunk_len_in.3) | copy-start | bytes 772
  25.4 23.1 %collective-permute-start.1 = (bf16[2,4,640,128]{3,2,1,0:T(8,128)(2,1)}, bf16[2,4,640,128]{3,2,1,0:T(8,128)(2,1)S(1)}, u32[]{:S(2)}, u32[]{:S(2)}) collective-permute-start(bf16[2,4,640,128]{3,2,1,0:T(8,128)(2,1)} %get-tuple-element.26), channel_id=1, source_target_pairs={{0,1},{1,0},{2,3},{3,2},{4,5},{5,4},{6,7},{7,6},{8,9},{9,8},{10,11... | collective-permute-start | bytes 3932168 | tf_op jit(solution)/shard_map/ppermute | solution.py:401
  35.0 9.1 %copy-start.6 = (f32[128,256]{1,0:T(8,128)S(1)}, f32[128,256]{1,0:T(8,128)}, u32[]{:S(2)}) copy-start(f32[128,256]{1,0:T(8,128)} %get-tuple-element.23) | copy-start | bytes 393220
  35.0 13.5 %copy-start = (bf16[2,4,640,128]{3,2,1,0:T(8,128)(2,1)S(1)}, bf16[2,4,640,128]{3,2,1,0:T(8,128)(2,1)}, u32[]{:S(2)}) copy-start(bf16[2,4,640,128]{3,2,1,0:T(8,128)(2,1)} %get-tuple-element.25.own_ref) | copy-start | bytes 3932164
  37.5 22.4 %all-to-all-start.1 = ((bf16[64,16,128]{2,1,0:T(8,128)(2,1)}), bf16[64,16,128]{2,1,0:T(8,128)(2,1)S(1)}, u32[]{:S(2)}, u32[]{:S(2)}) async-start(bf16[64,16,128]{2,1,0:T(8,128)(2,1)} %bitcast.2), calls=%async_computation.1 | async-start | bytes 524288 | tf_op jit(solution)/shard_map/all_to_all | solution.py:443
  44.1 4.4 %collective-permute-start = (bf16[128,256]{1,0:T(8,128)(2,1)S(1)}, bf16[128,256]{1,0:T(8,128)(2,1)S(1)}, u32[]{:S(2)}, u32[]{:S(2)}) collective-permute-start(bf16[128,256]{1,0:T(8,128)(2,1)S(1)} %add_convert_fusion.kv_ref), channel_id=1, source_target_pairs={{0,1},{1,0},{2,3},{3,2},{4,5},{5,4},{6,7},{7,6},{8,9},{9,8},{10,11... | collective-permute-start | bytes 196616 | tf_op jit(solution)/shard_map/ppermute | solution.py:401
  50.0 15.1 %collective-permute-start.3 = (bf16[640,128]{1,0:T(8,128)(2,1)}, bf16[640,128]{1,0:T(8,128)(2,1)S(1)}, u32[]{:S(2)}, u32[]{:S(2)}) collective-permute-start(bf16[640,128]{1,0:T(8,128)(2,1)} %get-tuple-element.30), channel_id=1, source_target_pairs={{0,2},{1,3},{2,4},{3,5},{4,6},{5,7},{6,0},{7,1},{8,10},{9,11},{10,... | collective-permute-start | bytes 491528 | tf_op jit(solution)/shard_map/ppermute | solution.py:442
  53.1 12.0 %collective-permute-start.4 = (bf16[640,128]{1,0:T(8,128)(2,1)}, bf16[640,128]{1,0:T(8,128)(2,1)S(1)}, u32[]{:S(2)}, u32[]{:S(2)}) collective-permute-start(bf16[640,128]{1,0:T(8,128)(2,1)} %get-tuple-element.31), channel_id=1, source_target_pairs={{0,6},{1,7},{2,0},{3,1},{4,2},{5,3},{6,4},{7,5},{8,14},{9,15},{10,... | collective-permute-start | bytes 491528 | tf_op jit(solution)/shard_map/ppermute | solution.py:442
  56.5 8.6 %collective-permute-start.5 = (bf16[640,128]{1,0:T(8,128)(2,1)}, bf16[640,128]{1,0:T(8,128)(2,1)S(1)}, u32[]{:S(2)}, u32[]{:S(2)}) collective-permute-start(bf16[640,128]{1,0:T(8,128)(2,1)} %get-tuple-element.32), channel_id=1, source_target_pairs={{0,4},{1,5},{2,6},{3,7},{4,0},{5,1},{6,2},{7,3},{8,12},{9,13},{10,... | collective-permute-start | bytes 491528 | tf_op jit(solution)/shard_map/ppermute | solution.py:442
  60.2 4.1 %collective-permute-start.2 = (bf16[128,256]{1,0:T(8,128)(2,1)S(1)}, bf16[128,256]{1,0:T(8,128)(2,1)S(1)}, u32[]{:S(2)}, u32[]{:S(2)}) collective-permute-start(bf16[128,256]{1,0:T(8,128)(2,1)S(1)} %shard_map.109.kv_ref), channel_id=1, source_target_pairs={{0,1},{1,0},{2,3},{3,2},{4,5},{5,4},{6,7},{7,6},{8,9},{9,8},{10,11... | collective-permute-start | bytes 196616 | tf_op jit(solution)/shard_map/ppermute | solution.py:401
